TPU v7x, 128 devices: a whole 4x4x4 slice. The times are simulated.
128 devices in a mesh: band: 32 (over z_hi, x, y), bus: 4 (over z_lo, core).
Axes of the slice: x: 4, y: 4, z: 4 (z_hi: 2, z_lo: 2; z = z_hi * 2 + z_lo), core: 2. Of those that a mesh axis runs over, the one named last changes fastest.
Arguments:
- dispatch0: float32 [64, 20480], P(None, ('band', 'bus')), may hold values from 0 to 1
- cost_lin: float32 [20480], P(('band', 'bus')), may hold values from -1 to 1
- cost_quad: float32 [20480], P(('band', 'bus')), may hold values from 0.5 to 4
- gen_max: float32 [20480], P(('band', 'bus')), may hold values from 0.5 to 2
- bus_map: int32 [20480], P(('band', 'bus')), may hold values from 0 to 98303, as said below
- demand: float32 [64, 4, 24576], P(None, 'bus', 'band'), may hold values from -6 to 6
- ptdf: float32 [8192, 98304], P('band', 'bus'), may hold values from -0.01953125 to 0.01953125
- line_price0: float32 [64, 8192], P(None, 'band'), may hold values from -3 to 3
- flow_max: float32 [8192], P('band'), may hold values from 0.3 to 3
Outputs:
- dispatch: float32 [64, 20480], P(None, ('band', 'bus'))
- line_price: float32 [64, 8192], P(None, 'band')
Inputs may be any that keep to these rules, and one draw needn't show every extreme that they name: `bus_map`: call bus 24576 * j + 768 * i + k with 0 <= k < 768 a bus of sub-block (i, j). Among the 160 generators of one aligned block (generators 160 * d to 160 * d + 159), at most 3 are sited in one sub-block, and one sub-block holds exactly 3 generators of every block.
All inputs are finite; a program needn't handle non-finite values.
Results may differ from a plain program's by a relative error of at most 0.0003.
Values sent between devices are 32-bit elements; how exact they have to be, the bound alone decides.
No kernel may reach another device: no remote copies, remote signals or barrier semaphores. Data moves between devices by JAX's collectives and lax.ppermute only.
A program may use at most 128 MiB of HBM per device.

v0:
```python
import jax
import jax.numpy as jnp
from jax import lax
from jax.sharding import PartitionSpec as P

ITERS = 2


primal_step = 0.5
dual_step = 1.0


def cut_along(shard, dim, peers):
    dims = shard.shape
    blocks = shard.reshape(*dims[:dim], peers, dims[dim] // peers, *dims[dim + 1 :])
    return jnp.moveaxis(blocks, dim, 0)


def sent_and_summed(shard, axis, dim):
    blocks = cut_along(shard, dim, lax.axis_size(axis))
    arrived = lax.all_to_all(blocks, axis, split_axis=0, concat_axis=0, tiled=True)
    return arrived.sum(axis=0)


def in_one_piece(arrays, axis, split_dim, concat_dim, along):
    widths = [a.shape[along] for a in arrays]
    both = jnp.concatenate(arrays, axis=along)
    filled = lax.all_to_all(both, axis, split_axis=split_dim, concat_axis=concat_dim, tiled=True)
    return tuple(jnp.split(filled, [sum(widths[:k]) for k in range(1, len(widths))], axis=along))


def owner_slots(bus_map, bus_width, sub_width, bus_count, slot_cap):
    block = bus_map // bus_width
    within = bus_map % bus_width
    owner = within // sub_width * bus_count + block
    local = within % sub_width
    same = owner[:, None] == owner[None, :]
    earlier = lax.broadcasted_iota(jnp.int32, same.shape, 0) > lax.broadcasted_iota(
        jnp.int32, same.shape, 1
    )
    rank = jnp.sum((same & earlier).astype(jnp.int32), axis=1)
    return (owner * slot_cap + rank, local)


def pack_rows(values, target, total):
    return jnp.zeros((total, values.shape[1]), values.dtype).at[target].set(values)


def on_device(
    dispatch0, cost_lin, cost_quad, gen_max, bus_map, demand, ptdf, line_price0, flow_max
):
    band_count = lax.axis_size("band")
    bus_count = lax.axis_size("bus")
    owner_count = band_count * bus_count
    gen_count = bus_map.shape[0]
    slot_cap = (gen_count + owner_count - 1) // owner_count + 1
    total = owner_count * slot_cap
    scenarios = dispatch0.shape[0]
    sub_width = demand.shape[2]
    bus_width = ptdf.shape[1]
    target, local = owner_slots(bus_map, bus_width, sub_width, bus_count, slot_cap)
    site_code = (local + 1).astype(jnp.float32)
    load = demand[:, 0, :]
    line_price = line_price0
    params = jnp.stack([site_code, cost_lin, cost_quad, gen_max], axis=1)
    sent = pack_rows(dispatch0.T, target, total).reshape(owner_count, slot_cap * scenarios)
    sent_params = pack_rows(params, target, total).reshape(owner_count, slot_cap * 4)
    slot_values, slot_params = in_one_piece((sent, sent_params), ("band", "bus"), 0, 0, 1)
    slot_values = slot_values.reshape(total, scenarios)
    slot_params = slot_params.reshape(total, 4)
    slot_local = jnp.maximum(slot_params[:, 0] - 1.0, 0.0).astype(jnp.int32)
    for iteration in range(ITERS):
        spread = jnp.zeros((sub_width, scenarios), jnp.float32).at[slot_local].add(slot_values)
        injection = spread.T - load
        share = sent_and_summed(
            lax.dot_general(
                lax.all_gather(injection, "band", axis=1, tiled=True),
                ptdf,
                (((1,), (1,)), ((), ())),
                precision=lax.Precision.HIGHEST,
                preferred_element_type=jnp.float32,
            ),
            "bus",
            1,
        )
        width = share.shape[1]
        offset = lax.axis_index("bus") * width
        mine = lax.dynamic_slice_in_dim(line_price, offset, width, 1)
        bound = dual_step * lax.dynamic_slice_in_dim(flow_max, offset, width, 0)
        trial = mine + dual_step * share
        price_next = trial - jnp.clip(trial, -bound, bound)
        line_price = lax.all_gather(price_next, "bus", axis=1, tiled=True)
        reflected = lax.all_gather(2.0 * price_next - mine, "bus", axis=1, tiled=True)
        slot_price = sent_and_summed(
            lax.dot_general(
                ptdf,
                reflected,
                (((0,), (1,)), ((), ())),
                precision=lax.Precision.HIGHEST,
                preferred_element_type=jnp.float32,
            ),
            "band",
            0,
        )[slot_local]
        slot_values = jnp.clip(
            (slot_values - primal_step * (slot_params[:, 1:2] + slot_price))
            / (1.0 + primal_step * slot_params[:, 2:3]),
            0.0,
            slot_params[:, 3:4],
        )
    home = lax.all_to_all(
        slot_values.reshape(owner_count, slot_cap * scenarios),
        ("band", "bus"),
        split_axis=0,
        concat_axis=0,
        tiled=True,
    )
    dispatch = home.reshape(total, scenarios)[target].T
    return (dispatch, line_price)


def solution(mesh):
    in_specs = (
        P(None, ("band", "bus")),
        P(("band", "bus")),
        P(("band", "bus")),
        P(("band", "bus")),
        P(("band", "bus")),
        P(None, "bus", "band"),
        P("band", "bus"),
        P(None, "band"),
        P("band"),
    )
    out_specs = (P(None, ("band", "bus")), P(None, "band"))
    return jax.shard_map(
        on_device, mesh=mesh, in_specs=in_specs, out_specs=out_specs, check_vma=False
    )
```

profile of v0, /device:TPU:1, one launch (start us, length us, event | category | flops | bytes accessed | tf_op | source)
XLA Modules:
  0.0 660.9 jit_solution(11311450892417828647)
XLA Ops:
  9.9 1.0 scatter_custom_fusion
  12.9 11.5 %all-to-all-start = ((f32[128,1,204]{2,1,0:T(1,128)}), f32[128,1,204]{2,1,0:T(1,128)S(1)}, u32[]{:S(2)}, u32[]{:S(2)}) async-start(f32[128,1,204]{2,1,0:T(1,128)} %copy.92), calls=%async_computation | async-start | bytes 262144 | tf_op jit(solution)/shard_map/all_to_all | solution.py:28
  24.5 1.1 copy.98
  25.6 8.8 %all-to-all-done = f32[128,1,204]{2,1,0:T(1,128)S(1)} async-done(((f32[128,1,204]{2,1,0:T(1,128)}), f32[128,1,204]{2,1,0:T(1,128)S(1)}, u32[]{:S(2)}, u32[]{:S(2)}) %all-to-all-start) | async-done | bytes 104480 | tf_op jit(solution)/shard_map/all_to_all | solution.py:28
  35.1 2.8 scatter_custom_fusion.2
  38.8 125.7 %all-gather.3.cloned.1.call-done = f32[64,24576]{0,1:T(8,128)} async-done(((f32[64,768]{0,1:T(8,128)}), f32[64,24576]{0,1:T(8,128)}) %all-gather.3.cloned.1.call-update) | async-done | bytes 6291472 | tf_op jit(solution)/shard_map/all_gather | solution.py:77
  164.5 27.1 %fusion.34 = f32[64,256]{1,0:T(8,128)S(1)} fusion(f32[64,24576]{0,1:T(8,128)} %all-gather.3.cloned.1.call-done, f32[256,24576]{1,0:T(8,128)} %param.15), kind=kOutput, calls=%fused_computation.76 | convolution fusion | flops 4831838208 | bytes 31522816 | tf_op jit(solution)/shard_map/dot_general | solution.py:76
  192.5 4.3 all-to-all-start.1
  196.9 3.2 all-to-all-done.1
  201.8 6.3 all_gather.19
  208.1 18.3 %fusion.35 = f32[64,24576]{1,0:T(8,128)S(1)} fusion(f32[64,256]{0,1:T(8,128)S(1)} %all_gather.19, f32[256,24576]{1,0:T(8,128)} %param.15), kind=kOutput, calls=%fused_computation.77 | convolution fusion | flops 4831838208 | bytes 31522816 | tf_op jit(solution)/shard_map/dot_general | solution.py:95
  226.4 3.5 copy.128
  229.9 5.4 all-to-all-start.2
  235.7 90.5 %all-to-all-done.2 = f32[32,768,64]{1,2,0:T(8,128)} async-done(((f32[32,768,64]{1,2,0:T(8,128)}), f32[32,768,64]{1,2,0:T(8,128)}, u32[]{:S(2)}, u32[]{:S(2)}) %all-to-all-start.2) | async-done | bytes 6291488 | tf_op jit(solution)/shard_map/all_to_all | solution.py:21
  326.2 3.1 reduce_sum.47
  329.5 1.1 gather_fusion
  330.6 2.5 scatter_custom_fusion.3
  334.0 7.1 %all_gather.20 = f32[64,256]{0,1:T(8,128)S(1)} all-gather(f32[64,64]{0,1:T(8,128)S(1)} %copy.106), channel_id=1, replica_groups=mesh['band'=32,'bus'=4] {'bus'}, dimensions={1}, use_global_device_ids=true | all-gather | bytes 81920 | tf_op jit(solution)/shard_map/all_gather | solution.py:92
  341.1 124.3 %all-gather.5.cloned.1.call-done = f32[64,24576]{0,1:T(8,128)} async-done(((f32[64,768]{0,1:T(8,128)}), f32[64,24576]{0,1:T(8,128)}) %all-gather.5.cloned.1.call-update) | async-done | bytes 6291472 | tf_op jit(solution)/shard_map/all_gather | solution.py:77
  465.5 27.1 %fusion.36 = f32[64,256]{1,0:T(8,128)S(1)} fusion(f32[64,24576]{0,1:T(8,128)} %all-gather.5.cloned.1.call-done, f32[256,24576]{1,0:T(8,128)} %param.15), kind=kOutput, calls=%fused_computation.78 | convolution fusion | flops 4831838208 | bytes 31522816 | tf_op jit(solution)/shard_map/dot_general | solution.py:76
  493.5 4.3 all-to-all-start.3
  497.9 3.2 all-to-all-done.3
  502.2 6.4 all_gather.22
  508.5 18.3 %fusion.37 = f32[64,24576]{1,0:T(8,128)S(1)} fusion(f32[64,256]{0,1:T(8,128)S(1)} %all_gather.22, f32[256,24576]{1,0:T(8,128)} %param.15), kind=kOutput, calls=%fused_computation.79 | convolution fusion | flops 4831838208 | bytes 31522816 | tf_op jit(solution)/shard_map/dot_general | solution.py:95
  526.8 3.5 copy.127
  530.3 5.4 all-to-all-start.4
  536.8 89.9 %all-to-all-done.4 = f32[32,768,64]{1,2,0:T(8,128)} async-done(((f32[32,768,64]{1,2,0:T(8,128)}), f32[32,768,64]{1,2,0:T(8,128)}, u32[]{:S(2)}, u32[]{:S(2)}) %all-to-all-start.4) | async-done | bytes 6291488 | tf_op jit(solution)/shard_map/all_to_all | solution.py:21
  626.7 3.1 reduce_sum.49
  630.0 1.1 gather_fusion.1
  632.1 9.9 %all-to-all-start.5 = ((f32[128,1,192]{2,1,0:T(1,128)}), f32[128,1,192]{2,1,0:T(1,128)S(1)}, u32[]{:S(2)}, u32[]{:S(2)}) async-start(f32[128,1,192]{2,1,0:T(1,128)} %copy.114), calls=%async_computation.5 | async-start | bytes 262144 | tf_op jit(solution)/shard_map/all_to_all | solution.py:111
  642.1 6.5 all_gather.23
  649.3 2.7 all-to-all-done.5
  (73 shorter events, 17.1 us)
Async XLA Ops:
  12.9 21.5 %all-to-all-start = ((f32[128,1,204]{2,1,0:T(1,128)}), f32[128,1,204]{2,1,0:T(1,128)S(1)}, u32[]{:S(2)}, u32[]{:S(2)}) async-start(f32[128,1,204]{2,1,0:T(1,128)} %copy.92), calls=%async_computation | async-start | bytes 262144 | tf_op jit(solution)/shard_map/all_to_all | solution.py:28
  24.4 140.1 %all-gather.3.cloned.1.call-start = ((), (), s32[]{:S(2)}) async-start(), calls=%async_computation.6 | async-start | bytes 12976128 | tf_op jit(solution)/shard_map/all_gather | solution.py:77
  38.7 158.1 %copy-start.1 = (f32[256]{0:T(256)S(1)}, f32[256]{0:T(256)}, u32[]{:S(2)}) copy-start(f32[256]{0:T(256)} %param.17) | copy-start | bytes 3076
  38.8 162.8 %copy-start = (f32[64,256]{1,0:T(8,128)S(1)}, f32[64,256]{1,0:T(8,128)}, u32[]{:S(2)}) copy-start(f32[64,256]{1,0:T(8,128)} %param.16) | copy-start | bytes 196612
  192.5 7.6 %all-to-all-start.1 = ((f32[4,1,4096]{2,1,0:T(1,128)}), f32[4,1,4096]{2,1,0:T(1,128)S(1)}, u32[]{:S(2)}, u32[]{:S(2)}) async-start(f32[4,1,4096]{2,1,0:T(1,128)} %reshape.145), calls=%async_computation.1 | async-start | bytes 131072 | tf_op jit(solution)/shard_map/all_to_all | solution.py:21
  229.9 96.4 %all-to-all-start.2 = ((f32[32,768,64]{1,2,0:T(8,128)}), f32[32,768,64]{1,2,0:T(8,128)}, u32[]{:S(2)}, u32[]{:S(2)}) async-start(f32[32,768,64]{1,2,0:T(8,128)} %bitcast.81), calls=%async_computation.2 | async-start | bytes 12582912 | tf_op jit(solution)/shard_map/all_to_all | solution.py:21
  235.3 230.2 %all-gather.5.cloned.1.call-start = ((), (), s32[]{:S(2)}) async-start(), calls=%async_computation.7 | async-start | bytes 12976128 | tf_op jit(solution)/shard_map/all_gather | solution.py:77
  493.5 7.6 %all-to-all-start.3 = ((f32[4,1,4096]{2,1,0:T(1,128)}), f32[4,1,4096]{2,1,0:T(1,128)S(1)}, u32[]{:S(2)}, u32[]{:S(2)}) async-start(f32[4,1,4096]{2,1,0:T(1,128)} %reshape.147), calls=%async_computation.3 | async-start | bytes 131072 | tf_op jit(solution)/shard_map/all_to_all | solution.py:21
  530.3 96.4 %all-to-all-start.4 = ((f32[32,768,64]{1,2,0:T(8,128)}), f32[32,768,64]{1,2,0:T(8,128)}, u32[]{:S(2)}, u32[]{:S(2)}) async-start(f32[32,768,64]{1,2,0:T(8,128)} %bitcast.80), calls=%async_computation.4 | async-start | bytes 12582912 | tf_op jit(solution)/shard_map/all_to_all | solution.py:21
  632.1 19.9 %all-to-all-start.5 = ((f32[128,1,192]{2,1,0:T(1,128)}), f32[128,1,192]{2,1,0:T(1,128)S(1)}, u32[]{:S(2)}, u32[]{:S(2)}) async-start(f32[128,1,192]{2,1,0:T(1,128)} %copy.114), calls=%async_computation.5 | async-start | bytes 262144 | tf_op jit(solution)/shard_map/all_to_all | solution.py:111
Sparse Core Ops, SparseCore 0:
  38.9 125.5 all-gather.2
  334.1 131.3 all-gather.4
where the time goes:
time: 665 us; the launch traced here: 661 us
  waiting for transfers between devices  448 us (67%)
  matrix products  90.9 us (14%)
  starting transfers between devices  40.9 us (6%)
  blocking collectives  26.2 us (4%)
  local copies, waits for them, and re-layouts  22.2 us (3%)
  other arithmetic  17.6 us (3%)
  between operations  14.7 us (2%)
    all_gather x2, waiting for transfers between devices, on_device(): lax.all_gather(injection, 'band', axis=1, tiled=True)  250 us
    all_to_all x4, waiting for transfers between devices, sent_and_summed(): lax.all_to_all(blocks, axis, split_axis=0, concat_axis=0, tiled=True)  187 us
    dot_general x2, matrix products, on_device(): lax.dot_general(lax.all_gather(injection, 'band', axis=1, tiled=True), pt...  54.3 us
    dot_general x2, matrix products, on_device(): lax.dot_general(ptdf, reflected, (((0,), (1,)), ((), ())), precision=lax....  36.6 us
    all_to_all x4, starting transfers between devices, sent_and_summed(): lax.all_to_all(blocks, axis, split_axis=0, concat_axis=0, tiled=True)  19.4 us
    all_gather x2, blocking collectives, on_device(): line_price = lax.all_gather(price_next, 'bus', axis=1, tiled=True)  13.6 us
  transfers between devices with their start and end apart: 8, of which 8 were waited for; matrix products, arithmetic and copies ran while one was open for 1% of the time, Pallas kernels for 0%

commit v1 on v0

v1 whole, which is shorter than its diff:
```python
import jax
import jax.numpy as jnp
from jax import lax
from jax.experimental import pallas as pl
from jax.experimental.pallas import tpu as pltpu
from jax.sharding import PartitionSpec as P

ITERS = 2
S = 64
HALF = 32
SUB = 768
BUS_DEV = 24576
CAP = 3
DEVICES = 128
N_BUS = 4
N_BAND = 32
SLOTS = CAP * DEVICES
GEN_DEV = 160
LINES_DEV = 256
LOAD_ROWS = SUB // 128 * HALF
SLOT_ROWS = CAP * HALF

primal_step = 0.5
dual_step = 1.0

NZ, NX, NY = 2, 4, 4


def band_index(z, x, y):
    return (z * NX + x) * NY + y


def shift(dz, dx, dy):
    return [
        (band_index(z, x, y), band_index((z + dz) % NZ, (x + dx) % NX, (y + dy) % NY))
        for z in range(NZ)
        for x in range(NX)
        for y in range(NY)
    ]


def moved(a, dz, dx, dy):
    return lax.ppermute(a, "band", shift(dz, dx, dy))


def ring_x(r):
    return (0, r, 0)


def ring_y(r):
    return (0, 0, r)


def gather_band(a, b):
    both = jnp.stack([a, b])
    other = moved(both, 1, 0, 0)
    out = []
    for k, (first, second) in enumerate(((ring_x, ring_y), (ring_y, ring_x))):
        pair = jnp.concatenate([both[k], other[k]], axis=0)
        eight = jnp.concatenate(
            [pair] + [moved(pair, *first(-r)) for r in (1, 2, 3)], axis=0
        )
        out.append([eight] + [moved(eight, *second(-r)) for r in (1, 2, 3)])
    return out


def sum_band(chunks_a, chunks_b):
    pairs = []
    for chunks, first, second in (
        (chunks_a, ring_x, ring_y),
        (chunks_b, ring_y, ring_x),
    ):
        got = [moved(chunks[r], *second(r)) for r in (2, 1, 3)]
        eight = chunks[0] + got[0] + got[1] + got[2]
        n = eight.shape[0] // 4
        parts = [eight[r * n : (r + 1) * n] for r in range(4)]
        got = [moved(parts[r], *first(r)) for r in (2, 1, 3)]
        pairs.append(parts[0] + got[0] + got[1] + got[2])
    n = pairs[0].shape[0] // 2
    got = moved(jnp.stack([p[n:] for p in pairs]), 1, 0, 0)
    return pairs[0][:n] + got[0], pairs[1][:n] + got[1]


def split(v):
    hi = v.astype(jnp.bfloat16)
    lo = (v - hi.astype(jnp.float32)).astype(jnp.bfloat16)
    return hi, lo


NT = (((1,), (1,)), ((), ()))
NN = (((1,), (0,)), ((), ()))


def three_pass(x, w_hi, w_lo, dims):
    x_hi, x_lo = split(x)
    n = x.shape[0]
    y = lax.dot_general(
        jnp.concatenate([x_hi, x_lo], axis=0), w_hi, dims, preferred_element_type=jnp.float32
    )
    return y[:n] + (
        y[n:] + lax.dot_general(x_hi, w_lo, dims, preferred_element_type=jnp.float32)
    )


def lanes(ref, count):
    return jnp.concatenate(
        [ref[k * HALF : (k + 1) * HALF, :] for k in range(count)], axis=1
    )


def load_flow_kernel(idx_ref, x_ref, w_ref, o_ref):
    @pl.when(pl.program_id(0) == 0)
    def _():
        o_ref[...] = jnp.zeros_like(o_ref)

    w_hi, w_lo = split(w_ref[...])
    o_ref[...] += three_pass(lanes(x_ref, SUB // 128), w_hi, w_lo, NT)


def load_flow(x, ptdf, idx):
    steps = idx.shape[0]
    return pl.pallas_call(
        load_flow_kernel,
        grid_spec=pltpu.PrefetchScalarGridSpec(
            num_scalar_prefetch=1,
            grid=(steps,),
            in_specs=[
                pl.BlockSpec((LOAD_ROWS, 128), lambda i, idx: (i, 0)),
                pl.BlockSpec((LINES_DEV, SUB), lambda i, idx: (0, idx[i])),
            ],
            out_specs=pl.BlockSpec((HALF, LINES_DEV), lambda i, idx: (0, 0)),
        ),
        out_shape=jax.ShapeDtypeStruct((HALF, LINES_DEV), jnp.float32),
        compiler_params=pltpu.CompilerParams(vmem_limit_bytes=32 * 1024 * 1024),
        cost_estimate=pl.CostEstimate(
            flops=steps * 8 * HALF * LINES_DEV * SUB * 2,
            bytes_accessed=steps * LINES_DEV * SUB * 4,
            transcendentals=0,
        ),
        name="load_flow",
    )(idx, x, ptdf)


def slot_flow_kernel(idx_ref, x_ref, hi_ref, lo_ref, o_ref):
    @pl.when(pl.program_id(0) == 0)
    def _():
        o_ref[...] = jnp.zeros_like(o_ref)

    o_ref[...] += three_pass(lanes(x_ref, CAP), hi_ref[...], lo_ref[...], NT)


def slot_flow(x, w_hi, w_lo, idx):
    steps = idx.shape[0]
    return pl.pallas_call(
        slot_flow_kernel,
        grid_spec=pltpu.PrefetchScalarGridSpec(
            num_scalar_prefetch=1,
            grid=(steps,),
            in_specs=[
                pl.BlockSpec((SLOT_ROWS, 128), lambda i, idx: (i, 0)),
                pl.BlockSpec((LINES_DEV, SLOTS), lambda i, idx: (0, idx[i])),
                pl.BlockSpec((LINES_DEV, SLOTS), lambda i, idx: (0, idx[i])),
            ],
            out_specs=pl.BlockSpec((HALF, LINES_DEV), lambda i, idx: (0, 0)),
        ),
        out_shape=jax.ShapeDtypeStruct((HALF, LINES_DEV), jnp.float32),
        compiler_params=pltpu.CompilerParams(vmem_limit_bytes=32 * 1024 * 1024),
        cost_estimate=pl.CostEstimate(
            flops=steps * 8 * HALF * LINES_DEV * SLOTS * 2,
            bytes_accessed=steps * LINES_DEV * SLOTS * 4,
            transcendentals=0,
        ),
        name="slot_flow",
    )(idx, x, w_hi, w_lo)


def slot_price_kernel(idx_ref, x_ref, hi_ref, lo_ref, o_ref):
    p = three_pass(x_ref[...], hi_ref[...], lo_ref[...], NN)
    for r in range(CAP):
        o_ref[r * HALF : (r + 1) * HALF, :] = p[:, r * 128 : (r + 1) * 128]


def slot_price(x, w_hi, w_lo, idx):
    steps = idx.shape[0]
    return pl.pallas_call(
        slot_price_kernel,
        grid_spec=pltpu.PrefetchScalarGridSpec(
            num_scalar_prefetch=1,
            grid=(steps,),
            in_specs=[
                pl.BlockSpec((HALF, LINES_DEV), lambda i, idx: (0, 0)),
                pl.BlockSpec((LINES_DEV, SLOTS), lambda i, idx: (0, idx[i])),
                pl.BlockSpec((LINES_DEV, SLOTS), lambda i, idx: (0, idx[i])),
            ],
            out_specs=pl.BlockSpec((SLOT_ROWS, 128), lambda i, idx: (i, 0)),
        ),
        out_shape=jax.ShapeDtypeStruct((steps * SLOT_ROWS, 128), jnp.float32),
        compiler_params=pltpu.CompilerParams(vmem_limit_bytes=32 * 1024 * 1024),
        cost_estimate=pl.CostEstimate(
            flops=steps * 8 * HALF * LINES_DEV * SLOTS * 2,
            bytes_accessed=steps * LINES_DEV * SLOTS * 4,
            transcendentals=0,
        ),
        name="slot_price",
    )(idx, x, w_hi, w_lo)


def pick_kernel(idx_ref, code_ref, w_ref, hi_ref, lo_ref):
    w_hi, w_lo = split(w_ref[...])
    code = code_ref[0]
    code = jnp.concatenate([code[r : r + 1, :] for r in range(CAP)], axis=1)
    hot = lax.broadcasted_iota(jnp.int32, (SUB, SLOTS), 0).astype(jnp.float32) + 1.0 == code
    hot = hot.astype(jnp.float32).astype(jnp.bfloat16)
    picked = lax.dot_general(
        jnp.concatenate([w_hi, w_lo], axis=0), hot, NN, preferred_element_type=jnp.float32
    ).astype(jnp.bfloat16)
    hi_ref[...] = picked[:LINES_DEV]
    lo_ref[...] = picked[LINES_DEV:]


def pick(codes, ptdf, idx):
    return pl.pallas_call(
        pick_kernel,
        grid_spec=pltpu.PrefetchScalarGridSpec(
            num_scalar_prefetch=1,
            grid=(N_BAND,),
            in_specs=[
                pl.BlockSpec((1, CAP, 128), lambda i, idx: (idx[i], 0, 0)),
                pl.BlockSpec((LINES_DEV, SUB), lambda i, idx: (0, idx[i])),
            ],
            out_specs=[
                pl.BlockSpec((LINES_DEV, SLOTS), lambda i, idx: (0, i)),
                pl.BlockSpec((LINES_DEV, SLOTS), lambda i, idx: (0, i)),
            ],
        ),
        out_shape=[jax.ShapeDtypeStruct((LINES_DEV, N_BAND * SLOTS), jnp.bfloat16)] * 2,
        compiler_params=pltpu.CompilerParams(vmem_limit_bytes=32 * 1024 * 1024),
        cost_estimate=pl.CostEstimate(
            flops=N_BAND * 4 * LINES_DEV * SLOTS * SUB,
            bytes_accessed=N_BAND * LINES_DEV * (SUB + SLOTS) * 4,
            transcendentals=0,
        ),
        name="pick",
    )(idx, codes, ptdf)


def owner_slots(bus_map):
    block = bus_map // BUS_DEV
    within = bus_map % BUS_DEV
    owner = within // SUB * N_BUS + block
    local = within % SUB
    same = owner[:, None] == owner[None, :]
    earlier = lax.broadcasted_iota(jnp.int32, same.shape, 0) > lax.broadcasted_iota(
        jnp.int32, same.shape, 1
    )
    rank = jnp.sum((same & earlier).astype(jnp.int32), axis=1)
    return owner * CAP + rank, local


def on_device(
    dispatch0, cost_lin, cost_quad, gen_max, bus_map, demand, ptdf, line_price0, flow_max
):
    band = lax.axis_index("band")
    z, x, y = band // (NX * NY), band // NY % NX, band % NY
    rel = [(ry, rx, rz) for ry in range(NY) for rx in range(NX) for rz in range(NZ)]
    block_of = jnp.stack(
        [band_index((z + rz) % NZ, (x + rx) % NX, (y + ry) % NY) for ry, rx, rz in rel]
    ).astype(jnp.int32)
    place_a = [
        [ry * 8 + rx * 2 + rz for rx in range(NX) for rz in range(NZ)] for ry in range(NY)
    ]
    place_b = [
        [ry * 8 + rx * 2 + rz for ry in range(NY) for rz in range(NZ)] for rx in range(NX)
    ]
    place = (place_a, place_b)

    def const_idx(p):
        return jnp.array(p, jnp.int32)

    load = demand[:, 0, :].reshape(2, HALF, SUB // 128, 128)
    load = load.transpose(0, 2, 1, 3).reshape(2, LOAD_ROWS, 128)
    load_chunks = gather_band(load[0], load[1])

    target, local = owner_slots(bus_map)
    params = jnp.stack([(local + 1).astype(jnp.float32), cost_lin, cost_quad, gen_max], axis=1)
    total = DEVICES * CAP
    sent = jnp.zeros((total, S), jnp.float32).at[target].set(dispatch0.T)
    sent_params = jnp.zeros((total, 4), jnp.float32).at[target].set(params)
    sent = sent.reshape(DEVICES, CAP, 2, HALF).transpose(0, 2, 1, 3).reshape(DEVICES, CAP * S)
    codes = sent_params[:, 0].reshape(N_BAND, N_BUS, CAP).transpose(1, 0, 2)
    codes = jnp.broadcast_to(
        codes.reshape(1, N_BUS, N_BAND * CAP), (N_BAND, N_BUS, N_BAND * CAP)
    ).reshape(DEVICES, N_BAND * CAP)
    message = jnp.concatenate(
        [sent, sent_params.reshape(DEVICES, CAP * 4), codes], axis=1
    )
    got = lax.all_to_all(message, ("band", "bus"), split_axis=0, concat_axis=0, tiled=True).T
    slot_values = got[: CAP * S].reshape(2, CAP, HALF, 128)
    slot_params = got[CAP * S : CAP * S + CAP * 4].reshape(CAP, 4, 128)
    codes = got[CAP * S + CAP * 4 :].reshape(N_BAND, CAP, 128)
    lin = slot_params[None, :, 1:2]
    quad = slot_params[None, :, 2:3]
    top = slot_params[None, :, 3:4]

    w_hi, w_lo = pick(codes, ptdf, block_of)

    def slots_flow_of(values):
        rows = values.reshape(2, SLOT_ROWS, 128)
        chunks = gather_band(rows[0], rows[1])
        return [
            sum(
                slot_flow(chunks[k][r], w_hi, w_lo, const_idx(place[k][r])) for r in range(4)
            )
            for k in range(2)
        ]

    load_part = [
        sum(load_flow(load_chunks[k][r], ptdf, block_of[jnp.array(place[k][r])]) for r in range(4))
        for k in range(2)
    ]

    line_price = line_price0
    bound = dual_step * flow_max
    for iteration in range(ITERS):
        slot_part = slots_flow_of(slot_values)
        partial = jnp.concatenate(
            [slot_part[k] - load_part[k] for k in range(2)], axis=0
        )
        parts = lax.all_gather(partial, "bus", axis=0)
        flow = (parts[0] + parts[1]) + (parts[2] + parts[3])
        trial = line_price + dual_step * flow
        price_next = trial - jnp.clip(trial, -bound, bound)
        reflected = 2.0 * price_next - line_price
        line_price = price_next
        chunks = [
            [
                slot_price(
                    reflected[k * HALF : (k + 1) * HALF], w_hi, w_lo, const_idx(place[k][r])
                )
                for r in range(4)
            ]
            for k in range(2)
        ]
        price_a, price_b = sum_band(*chunks)
        unit = jnp.stack([price_a, price_b]).reshape(2, CAP, HALF, 128)
        slot_values = jnp.clip(
            (slot_values - primal_step * (lin + unit)) / (1.0 + primal_step * quad), 0.0, top
        )
    home = lax.all_to_all(
        slot_values.reshape(CAP * S, 128).T, ("band", "bus"), split_axis=0, concat_axis=0, tiled=True
    )
    home = home.reshape(DEVICES, 2, CAP, HALF).transpose(0, 2, 1, 3).reshape(total, S)
    return home[target].T, line_price


def solution(mesh):
    gens = P(("band", "bus"))
    in_specs = (
        P(None, ("band", "bus")),
        gens,
        gens,
        gens,
        gens,
        P(None, "bus", "band"),
        P("band", "bus"),
        P(None, "band"),
        P("band"),
    )
    out_specs = (P(None, ("band", "bus")), P(None, "band"))
    return jax.shard_map(
        on_device, mesh=mesh, in_specs=in_specs, out_specs=out_specs, check_vma=False
    )
```

time: 665 us -> 457 us (0.69)
  waiting for transfers between devices: 448 us -> 66.8 us
  Pallas kernels: 0 us -> 176 us
  matrix products: 90.9 us -> 0 us
  starting transfers between devices: 40.9 us -> 118 us
  local copies, waits for them, and re-layouts: 22.2 us -> 39.3 us
  between operations: 14.7 us -> 2.41 us
  blocking collectives: 26.2 us -> 37.5 us
    all_gather x2 -> x0, waiting for transfers between devices: 250 us -> none  [on_device(): lax.all_gather(injection, 'band', axis=1, tiled=True)]
    all_to_all x6 -> x2, waiting for transfers between devices: 198 us -> 9.96 us  [the longest x1 9.95 us: on_device(): lax.all_to_all(slot_values.reshape(CAP * S, 128).T, ('band', 'bus'), spli...]
    pallas_call x0 -> x41, Pallas kernels: none -> 176 us  [the longest x8 57.2 us: load_flow(): pl.pallas_call(load_flow_kernel, grid_spec=pltpu.PrefetchScalarGridSpec(n...]
    ppermute x0 -> x65, starting transfers between devices: none -> 93 us  [moved(): return lax.ppermute(a, 'band', shift(dz, dx, dy))]
    dot_general x4 -> x0, matrix products: 90.9 us -> none  [the longest x2 54.3 us: on_device(): lax.dot_general(lax.all_gather(injection, 'band', axis=1, tiled=True), pt...]
    ppermute x0 -> x65, waiting for transfers between devices: none -> 56.8 us  [moved(): return lax.ppermute(a, 'band', shift(dz, dx, dy))]
    all_to_all x6 -> x2, starting transfers between devices: 40.8 us -> 24.9 us  [the longest x1 13.4 us: on_device(): lax.all_to_all(slot_values.reshape(CAP * S, 128).T, ('band', 'bus'), spli...]
    unnamed x12 -> x104, local copies, waits for them, and re-layouts: 4.37 us -> 18.7 us
  transfers between devices with their start and end apart: 8 -> 67, of which waited for: 8 -> 26; matrix products, arithmetic and copies ran while one was open for 1% -> 5% of each run, Pallas kernels for 0% -> 34%
where the time goes in v1:
time: 457 us; the launch traced here: 451 us
  Pallas kernels  176 us (39%)
  starting transfers between devices  118 us (26%)
  waiting for transfers between devices  66.8 us (15%)
  local copies, waits for them, and re-layouts  39.3 us (9%)
  blocking collectives  37.5 us (8%)
  other arithmetic  11.3 us (2%)
    ppermute x65, starting transfers between devices, moved(): return lax.ppermute(a, 'band', shift(dz, dx, dy))  93 us
    pallas_call x8, Pallas kernels, load_flow(): pl.pallas_call(load_flow_kernel, grid_spec=pltpu.PrefetchScalarGridSpec(n...  57.2 us
    ppermute x65, waiting for transfers between devices, moved(): return lax.ppermute(a, 'band', shift(dz, dx, dy))  56.8 us
    pallas_call x16, Pallas kernels, slot_flow(): pl.pallas_call(slot_flow_kernel, grid_spec=pltpu.PrefetchScalarGridSpec(n...  48.9 us
    pallas_call x16, Pallas kernels, slot_price(): pl.pallas_call(slot_price_kernel, grid_spec=pltpu.PrefetchScalarGridSpec(...  39.4 us
    all_gather x2, blocking collectives, on_device(): parts = lax.all_gather(partial, 'bus', axis=0)  37.5 us
    pallas_call x1, Pallas kernels, pick(): pl.pallas_call(pick_kernel, grid_spec=pltpu.PrefetchScalarGridSpec(num_sc...  30.4 us
    unnamed x104, local copies, waits for them, and re-layouts  18.7 us
  transfers between devices with their start and end apart: 67, of which 26 were waited for; matrix products, arithmetic and copies ran while one was open for 5% of the time, Pallas kernels for 34%

profile of v1, /device:TPU:1, one launch (start us, length us, event | category | flops | bytes accessed | tf_op | source)
XLA Modules:
  0.0 450.9 jit_solution(13439995132854571903)
XLA Ops:
  7.5 11.5 %all-to-all-start = ((f32[128,1,300]{2,1,0:T(1,128)}), f32[128,1,300]{2,1,0:T(1,128)S(1)}, u32[]{:S(2)}, u32[]{:S(2)}) async-start(f32[128,1,300]{2,1,0:T(1,128)} %copy.113), calls=%async_computation | async-start | bytes 393216 | tf_op jit(solution)/shard_map/all_to_all | solution.py:297
  20.5 3.4 collective-permute-start.7
  60.1 4.3 collective-permute-done.3
  75.9 5.7 %collective-permute-done.21 = f32[384,128]{1,0:T(8,128)S(1)} collective-permute-done((f32[384,128]{1,0:T(8,128)S(1)}, f32[384,128]{1,0:T(8,128)S(1)}, u32[]{:S(2)}, u32[]{:S(2)}) %collective-permute-start.21) | collective-permute-done | bytes 196640 | tf_op jit(solution)/shard_map/ppermute | solution.py:43
  84.7 4.1 collective-permute-done.5.x_ref
  89.5 3.6 collective-permute-done.4.x_ref
  95.0 6.8 %collective-permute-start.13 = (f32[1536,128]{1,0:T(8,128)S(1)}, f32[1536,128]{1,0:T(8,128)}, u32[]{:S(2)}, u32[]{:S(2)}) collective-permute-start(f32[1536,128]{1,0:T(8,128)S(1)} %constant_dynamic-update-slice_fusion.5.x_ref), channel_id=1, source_target_pairs={{0,4},{4,8},{8,12},{12,0},{16,20},{20,24},{24,28},{28,16},{32,36},... | collective-permute-start | bytes 2359304 | tf_op jit(solution)/shard_map/ppermute | solution.py:43
  106.5 30.4 %pick.1 = (bf16[256,12288]{1,0:T(8,128)(2,1)S(1)}, bf16[256,12288]{1,0:T(8,128)(2,1)S(1)}) custom-call(s32[32]{0:T(128)S(1)} %stack.197.idx_ref, f32[32,3,128]{2,1,0:T(4,128)S(1)} %copy-done.16, f32[256,24576]{1,0:T(8,128)} %w_ref.17), custom_call_target="tpu_custom_call" | custom-call | flops 9663676416 | bytes 37748736 | tf_op jit(solution)/shard_map/pick/pallas_call | solution.py:222
  150.4 5.0 %slot_flow.20 = f32[32,256]{1,0:T(8,128)S(1)} custom-call(s32[8]{0:T(128)S(1)} %copy-done.17, f32[768,128]{1,0:T(8,128)} %constant_dynamic-update-slice_fusion.10.x_ref, bf16[256,12288]{1,0:T(8,128)(2,1)S(1)} %copy-done.1, bf16[256,12288]{1,0:T(8,128)(2,1)S(1)} %copy-done.3), custom_call_target="tpu_custom_call" | custom-call | flops 402653184 | bytes 3145728 | tf_op jit(solution)/shard_map/slot_flow/pallas_call | solution.py:154
  155.5 2.9 slot_flow.16
  158.5 7.3 %load_flow.8 = f32[32,256]{1,0:T(8,128)S(1)} custom-call(s32[8]{0:T(128)S(1)} %copy-done.28, f32[1536,128]{1,0:T(8,128)S(1)} %constant_dynamic-update-slice_fusion.5.x_ref, f32[256,24576]{1,0:T(8,128)} %w_ref.17), custom_call_target="tpu_custom_call" | custom-call | flops 805306368 | bytes 6291456 | tf_op jit(solution)/shard_map/load_flow/pallas_call | solution.py:122
  165.8 7.2 %load_flow.12 = f32[32,256]{1,0:T(8,128)S(1)} custom-call(s32[8]{0:T(128)S(1)} %copy-done.29, f32[1536,128]{1,0:T(8,128)S(1)} %constant_dynamic-update-slice_fusion.15.x_ref, f32[256,24576]{1,0:T(8,128)} %w_ref.17), custom_call_target="tpu_custom_call" | custom-call | flops 805306368 | bytes 6291456 | tf_op jit(solution)/shard_map/load_flow/pallas_call | solution.py:122
  173.1 2.9 slot_flow.23
  176.2 2.9 slot_flow.22
  179.2 2.9 slot_flow.21
  182.2 2.9 slot_flow.19
  185.1 2.9 slot_flow.18
  188.1 2.9 slot_flow.17
  191.1 7.0 %load_flow.15 = f32[32,256]{1,0:T(8,128)S(1)} custom-call(s32[8]{0:T(128)S(1)} %copy-done.27, f32[1536,128]{1,0:T(8,128)S(1)} %collective-permute-done.25.x_ref, f32[256,24576]{1,0:T(8,128)} %w_ref.17), custom_call_target="tpu_custom_call" | custom-call | flops 805306368 | bytes 6291456 | tf_op jit(solution)/shard_map/load_flow/pallas_call | solution.py:122
  198.1 7.0 %load_flow.14 = f32[32,256]{1,0:T(8,128)S(1)} custom-call(s32[8]{0:T(128)S(1)} %copy-done.26, f32[1536,128]{1,0:T(8,128)S(1)} %collective-permute-done.24.x_ref, f32[256,24576]{1,0:T(8,128)} %w_ref.17), custom_call_target="tpu_custom_call" | custom-call | flops 805306368 | bytes 6291456 | tf_op jit(solution)/shard_map/load_flow/pallas_call | solution.py:122
  205.2 7.2 %load_flow.11 = f32[32,256]{1,0:T(8,128)S(1)} custom-call(s32[8]{0:T(128)S(1)} %copy-done.25, f32[1536,128]{1,0:T(8,128)} %collective-permute-done.13.x_ref, f32[256,24576]{1,0:T(8,128)} %w_ref.17), custom_call_target="tpu_custom_call" | custom-call | flops 805306368 | bytes 6291456 | tf_op jit(solution)/shard_map/load_flow/pallas_call | solution.py:122
  212.4 7.2 %load_flow.10 = f32[32,256]{1,0:T(8,128)S(1)} custom-call(s32[8]{0:T(128)S(1)} %copy-done.24, f32[1536,128]{1,0:T(8,128)} %collective-permute-done.12.x_ref, f32[256,24576]{1,0:T(8,128)} %w_ref.17), custom_call_target="tpu_custom_call" | custom-call | flops 805306368 | bytes 6291456 | tf_op jit(solution)/shard_map/load_flow/pallas_call | solution.py:122
  219.6 7.2 %load_flow.9 = f32[32,256]{1,0:T(8,128)S(1)} custom-call(s32[8]{0:T(128)S(1)} %gather_fusion.1, f32[1536,128]{1,0:T(8,128)} %collective-permute-done.11.x_ref, f32[256,24576]{1,0:T(8,128)} %w_ref.17), custom_call_target="tpu_custom_call" | custom-call | flops 805306368 | bytes 6291456 | tf_op jit(solution)/shard_map/load_flow/pallas_call | solution.py:122
  226.9 7.0 %load_flow.13 = f32[32,256]{1,0:T(8,128)S(1)} custom-call(s32[8]{0:T(128)S(1)} %gather_fusion.5, f32[1536,128]{1,0:T(8,128)S(1)} %collective-permute-done.23.x_ref, f32[256,24576]{1,0:T(8,128)} %w_ref.17), custom_call_target="tpu_custom_call" | custom-call | flops 805306368 | bytes 6291456 | tf_op jit(solution)/shard_map/load_flow/pallas_call | solution.py:122
  234.0 20.6 %all-gather = f32[256,256]{1,0:T(8,128)S(1)} all-gather(f32[64,256]{1,0:T(8,128)S(1)} %pad_maximum_fusion.11), channel_id=2, replica_groups=mesh['band'=32,'bus'=4] {'bus'}, dimensions={0}, use_global_device_ids=true | all-gather | bytes 327680 | tf_op jit(solution)/shard_map/all_gather | solution.py:329
  285.7 5.3 %collective-permute-done.27 = f32[768,128]{1,0:T(8,128)S(1)} collective-permute-done((f32[768,128]{1,0:T(8,128)S(1)}, f32[768,128]{1,0:T(8,128)S(1)}, u32[]{:S(2)}, u32[]{:S(2)}) %collective-permute-start.27) | collective-permute-done | bytes 393248 | tf_op jit(solution)/shard_map/ppermute | solution.py:43
  302.5 11.6 %collective-permute-start.39 = (f32[2,96,128]{2,1,0:T(8,128)S(1)}, f32[2,96,128]{2,1,0:T(8,128)S(1)}, u32[]{:S(2)}, u32[]{:S(2)}) collective-permute-start(f32[2,96,128]{2,1,0:T(8,128)S(1)} %pad_maximum_fusion.7), channel_id=1, source_target_pairs={{0,64},{4,68},{8,72},{12,76},{16,80},{20,84},{24,88},{28,92},{32,9... | collective-permute-start | bytes 294920 | tf_op jit(solution)/shard_map/ppermute | solution.py:43
  358.9 16.8 %all-gather.1 = f32[256,256]{1,0:T(8,128)S(1)} all-gather(f32[64,256]{1,0:T(8,128)S(1)} %pad_maximum_fusion.12), channel_id=3, replica_groups=mesh['band'=32,'bus'=4] {'bus'}, dimensions={0}, use_global_device_ids=true | all-gather | bytes 327680 | tf_op jit(solution)/shard_map/all_gather | solution.py:329
  406.6 4.8 %collective-permute-done.53 = f32[768,128]{1,0:T(8,128)S(1)} collective-permute-done((f32[768,128]{1,0:T(8,128)S(1)}, f32[768,128]{1,0:T(8,128)S(1)}, u32[]{:S(2)}, u32[]{:S(2)}) %collective-permute-start.53) | collective-permute-done | bytes 393248 | tf_op jit(solution)/shard_map/ppermute | solution.py:43
  421.1 3.5 collective-permute-done.64
  425.4 13.4 %all-to-all-start.1 = ((f32[128,1,192]{2,1,0:T(1,128)}), f32[128,1,192]{2,1,0:T(1,128)S(1)}, u32[]{:S(2)}, u32[]{:S(2)}) async-start(f32[128,1,192]{2,1,0:T(1,128)} %copy.119), calls=%async_computation.1 | async-start | bytes 262144 | tf_op jit(solution)/shard_map/all_to_all | solution.py:349
  438.8 10.0 %all-to-all-done.1 = f32[128,1,192]{2,1,0:T(1,128)S(1)} async-done(((f32[128,1,192]{2,1,0:T(1,128)}), f32[128,1,192]{2,1,0:T(1,128)S(1)}, u32[]{:S(2)}, u32[]{:S(2)}) %all-to-all-start.1) | async-done | bytes 98336 | tf_op jit(solution)/shard_map/all_to_all | solution.py:349
  (360 shorter events, 210.0 us)
Async XLA Ops:
  7.5 30.2 %all-to-all-start = ((f32[128,1,300]{2,1,0:T(1,128)}), f32[128,1,300]{2,1,0:T(1,128)S(1)}, u32[]{:S(2)}, u32[]{:S(2)}) async-start(f32[128,1,300]{2,1,0:T(1,128)} %copy.113), calls=%async_computation | async-start | bytes 393216 | tf_op jit(solution)/shard_map/all_to_all | solution.py:297
  20.5 18.7 %collective-permute-start.7 = (f32[2,192,128]{2,1,0:T(8,128)S(1)}, f32[2,192,128]{2,1,0:T(8,128)S(1)}, u32[]{:S(2)}, u32[]{:S(2)}) collective-permute-start(f32[2,192,128]{2,1,0:T(8,128)S(1)} %pad_maximum_fusion), channel_id=1, source_target_pairs={{0,64},{4,68},{8,72},{12,76},{16,80},{20,84},{24,88},{28,92},{32,9... | collective-permute-start | bytes 589832 | tf_op jit(solution)/shard_map/ppermute | solution.py:43
  39.3 35.2 %collective-permute-start.9 = (f32[384,128]{1,0:T(8,128)S(1)}, f32[384,128]{1,0:T(8,128)S(1)}, u32[]{:S(2)}, u32[]{:S(2)}) collective-permute-start(f32[384,128]{1,0:T(8,128)S(1)} %pad_maximum_fusion.1), channel_id=1, source_target_pairs={{0,32},{4,36},{8,40},{12,44},{16,48},{20,52},{24,56},{28,60},{32,0... | collective-permute-start | bytes 589832 | tf_op jit(solution)/shard_map/ppermute | solution.py:43
  42.1 33.4 %collective-permute-start.8 = (f32[384,128]{1,0:T(8,128)S(1)}, f32[384,128]{1,0:T(8,128)S(1)}, u32[]{:S(2)}, u32[]{:S(2)}) collective-permute-start(f32[384,128]{1,0:T(8,128)S(1)} %pad_maximum_fusion.1), channel_id=1, source_target_pairs={{0,48},{4,52},{8,56},{12,60},{16,0},{20,4},{24,8},{28,12},{32,16},... | collective-permute-start | bytes 589832 | tf_op jit(solution)/shard_map/ppermute | solution.py:43
  43.0 32.6 %collective-permute-start.22 = (f32[384,128]{1,0:T(8,128)S(1)}, f32[384,128]{1,0:T(8,128)S(1)}, u32[]{:S(2)}, u32[]{:S(2)}) collective-permute-start(f32[384,128]{1,0:T(8,128)S(1)} %pad_maximum_fusion.2), channel_id=1, source_target_pairs={{0,4},{4,8},{8,12},{12,0},{16,20},{20,24},{24,28},{28,16},{32,36},... | collective-permute-start | bytes 589832 | tf_op jit(solution)/shard_map/ppermute | solution.py:43
  45.2 26.4 %collective-permute-start.16 = (f32[192,128]{1,0:T(8,128)S(1)}, f32[192,128]{1,0:T(8,128)S(1)}, u32[]{:S(2)}, u32[]{:S(2)}) collective-permute-start(f32[192,128]{1,0:T(8,128)S(1)} %pad_maximum_fusion.5), channel_id=1, source_target_pairs={{0,4},{4,8},{8,12},{12,0},{16,20},{20,24},{24,28},{28,16},{32,36},... | collective-permute-start | bytes 294920 | tf_op jit(solution)/shard_map/ppermute | solution.py:43
  69.4 14.6 %collective-permute-start.6 = (f32[768,128]{1,0:T(8,128)S(1)}, f32[768,128]{1,0:T(8,128)S(1)}, u32[]{:S(2)}, u32[]{:S(2)}) collective-permute-start(f32[768,128]{1,0:T(8,128)S(1)} %constant_dynamic-update-slice_fusion.x_ref), channel_id=1, source_target_pairs={{0,4},{4,8},{8,12},{12,0},{16,20},{20,24},{24,28},{28,16},{32,36},... | collective-permute-start | bytes 1179656 | tf_op jit(solution)/shard_map/ppermute | solution.py:43
  81.5 20.2 %collective-permute-start.18 = (f32[768,128]{1,0:T(8,128)}, f32[768,128]{1,0:T(8,128)S(1)}, u32[]{:S(2)}, u32[]{:S(2)}) collective-permute-start(f32[768,128]{1,0:T(8,128)} %constant_dynamic-update-slice_fusion.10.x_ref), channel_id=1, source_target_pairs={{0,32},{4,36},{8,40},{12,44},{16,48},{20,52},{24,56},{28,60},{32,0... | collective-permute-start | bytes 1179656 | tf_op jit(solution)/shard_map/ppermute | solution.py:43
  83.9 18.6 %collective-permute-start.17 = (f32[768,128]{1,0:T(8,128)}, f32[768,128]{1,0:T(8,128)S(1)}, u32[]{:S(2)}, u32[]{:S(2)}) collective-permute-start(f32[768,128]{1,0:T(8,128)} %constant_dynamic-update-slice_fusion.10.x_ref), channel_id=1, source_target_pairs={{0,48},{4,52},{8,56},{12,60},{16,0},{20,4},{24,8},{28,12},{32,16},... | collective-permute-start | bytes 1179656 | tf_op jit(solution)/shard_map/ppermute | solution.py:43
  89.5 86.6 %collective-permute-start.25 = (f32[1536,128]{1,0:T(8,128)S(1)}, f32[1536,128]{1,0:T(8,128)S(1)}, u32[]{:S(2)}, u32[]{:S(2)}) collective-permute-start(f32[1536,128]{1,0:T(8,128)S(1)} %constant_dynamic-update-slice_fusion.15.x_ref), channel_id=1, source_target_pairs={{0,16},{4,20},{8,24},{12,28},{16,32},{20,36},{24,40},{28,44},{32,4... | collective-permute-start | bytes 2359304 | tf_op jit(solution)/shard_map/ppermute | solution.py:43
  93.9 104.2 %collective-permute-start.24 = (f32[1536,128]{1,0:T(8,128)S(1)}, f32[1536,128]{1,0:T(8,128)S(1)}, u32[]{:S(2)}, u32[]{:S(2)}) collective-permute-start(f32[1536,128]{1,0:T(8,128)S(1)} %constant_dynamic-update-slice_fusion.15.x_ref), channel_id=1, source_target_pairs={{0,32},{4,36},{8,40},{12,44},{16,48},{20,52},{24,56},{28,60},{32,0... | collective-permute-start | bytes 2359304 | tf_op jit(solution)/shard_map/ppermute | solution.py:43
  95.0 110.2 %collective-permute-start.13 = (f32[1536,128]{1,0:T(8,128)S(1)}, f32[1536,128]{1,0:T(8,128)}, u32[]{:S(2)}, u32[]{:S(2)}) collective-permute-start(f32[1536,128]{1,0:T(8,128)S(1)} %constant_dynamic-update-slice_fusion.5.x_ref), channel_id=1, source_target_pairs={{0,4},{4,8},{8,12},{12,0},{16,20},{20,24},{24,28},{28,16},{32,36},... | collective-permute-start | bytes 2359304 | tf_op jit(solution)/shard_map/ppermute | solution.py:43
  102.5 109.9 %collective-permute-start.12 = (f32[1536,128]{1,0:T(8,128)S(1)}, f32[1536,128]{1,0:T(8,128)}, u32[]{:S(2)}, u32[]{:S(2)}) collective-permute-start(f32[1536,128]{1,0:T(8,128)S(1)} %constant_dynamic-update-slice_fusion.5.x_ref), channel_id=1, source_target_pairs={{0,8},{4,12},{8,0},{12,4},{16,24},{20,28},{24,16},{28,20},{32,40},... | collective-permute-start | bytes 2359304 | tf_op jit(solution)/shard_map/ppermute | solution.py:43
  103.3 116.4 %collective-permute-start.11 = (f32[1536,128]{1,0:T(8,128)S(1)}, f32[1536,128]{1,0:T(8,128)}, u32[]{:S(2)}, u32[]{:S(2)}) collective-permute-start(f32[1536,128]{1,0:T(8,128)S(1)} %constant_dynamic-update-slice_fusion.5.x_ref), channel_id=1, source_target_pairs={{0,12},{4,0},{8,4},{12,8},{16,28},{20,16},{24,20},{28,24},{32,44},... | collective-permute-start | bytes 2359304 | tf_op jit(solution)/shard_map/ppermute | solution.py:43
  176.1 50.8 %collective-permute-start.23 = (f32[1536,128]{1,0:T(8,128)S(1)}, f32[1536,128]{1,0:T(8,128)S(1)}, u32[]{:S(2)}, u32[]{:S(2)}) collective-permute-start(f32[1536,128]{1,0:T(8,128)S(1)} %constant_dynamic-update-slice_fusion.15.x_ref), channel_id=1, source_target_pairs={{0,48},{4,52},{8,56},{12,60},{16,0},{20,4},{24,8},{28,12},{32,16},... | collective-permute-start | bytes 2359304 | tf_op jit(solution)/shard_map/ppermute | solution.py:43
  262.1 18.5 %collective-permute-start.32 = (f32[768,128]{1,0:T(8,128)S(1)}, f32[768,128]{1,0:T(8,128)S(1)}, u32[]{:S(2)}, u32[]{:S(2)}) collective-permute-start(f32[768,128]{1,0:T(8,128)S(1)} %slot_price.21), channel_id=1, source_target_pairs={{0,32},{4,36},{8,40},{12,44},{16,48},{20,52},{24,56},{28,60},{32,0... | collective-permute-start | bytes 1179656 | tf_op jit(solution)/shard_map/ppermute | solution.py:43
  263.7 19.5 %collective-permute-start.33 = (f32[768,128]{1,0:T(8,128)S(1)}, f32[768,128]{1,0:T(8,128)S(1)}, u32[]{:S(2)}, u32[]{:S(2)}) collective-permute-start(f32[768,128]{1,0:T(8,128)S(1)} %slot_price.22), channel_id=1, source_target_pairs={{0,16},{4,20},{8,24},{12,28},{16,32},{20,36},{24,40},{28,44},{32,4... | collective-permute-start | bytes 1179656 | tf_op jit(solution)/shard_map/ppermute | solution.py:43
  264.0 19.2 %collective-permute-start.34 = (f32[768,128]{1,0:T(8,128)S(1)}, f32[768,128]{1,0:T(8,128)S(1)}, u32[]{:S(2)}, u32[]{:S(2)}) collective-permute-start(f32[768,128]{1,0:T(8,128)S(1)} %slot_price.23), channel_id=1, source_target_pairs={{0,48},{4,52},{8,56},{12,60},{16,0},{20,4},{24,8},{28,12},{32,16},... | collective-permute-start | bytes 1179656 | tf_op jit(solution)/shard_map/ppermute | solution.py:43
  268.9 16.8 %collective-permute-start.26 = (f32[768,128]{1,0:T(8,128)S(1)}, f32[768,128]{1,0:T(8,128)S(1)}, u32[]{:S(2)}, u32[]{:S(2)}) collective-permute-start(f32[768,128]{1,0:T(8,128)S(1)} %slot_price.17), channel_id=1, source_target_pairs={{0,8},{4,12},{8,0},{12,4},{16,24},{20,28},{24,16},{28,20},{32,40},... | collective-permute-start | bytes 1179656 | tf_op jit(solution)/shard_map/ppermute | solution.py:43
  272.0 19.0 %collective-permute-start.27 = (f32[768,128]{1,0:T(8,128)S(1)}, f32[768,128]{1,0:T(8,128)S(1)}, u32[]{:S(2)}, u32[]{:S(2)}) collective-permute-start(f32[768,128]{1,0:T(8,128)S(1)} %slot_price.18), channel_id=1, source_target_pairs={{0,4},{4,8},{8,12},{12,0},{16,20},{20,24},{24,28},{28,16},{32,36},... | collective-permute-start | bytes 1179656 | tf_op jit(solution)/shard_map/ppermute | solution.py:43
  302.5 14.5 %collective-permute-start.39 = (f32[2,96,128]{2,1,0:T(8,128)S(1)}, f32[2,96,128]{2,1,0:T(8,128)S(1)}, u32[]{:S(2)}, u32[]{:S(2)}) collective-permute-start(f32[2,96,128]{2,1,0:T(8,128)S(1)} %pad_maximum_fusion.7), channel_id=1, source_target_pairs={{0,64},{4,68},{8,72},{12,76},{16,80},{20,84},{24,88},{28,92},{32,9... | collective-permute-start | bytes 294920 | tf_op jit(solution)/shard_map/ppermute | solution.py:43
  325.5 18.6 %collective-permute-start.50 = (f32[768,128]{1,0:T(8,128)S(1)}, f32[768,128]{1,0:T(8,128)S(1)}, u32[]{:S(2)}, u32[]{:S(2)}) collective-permute-start(f32[768,128]{1,0:T(8,128)S(1)} %constant_dynamic-update-slice_fusion.25.x_ref), channel_id=1, source_target_pairs={{0,32},{4,36},{8,40},{12,44},{16,48},{20,52},{24,56},{28,60},{32,0... | collective-permute-start | bytes 1179656 | tf_op jit(solution)/shard_map/ppermute | solution.py:43
  327.4 19.7 %collective-permute-start.49 = (f32[768,128]{1,0:T(8,128)S(1)}, f32[768,128]{1,0:T(8,128)S(1)}, u32[]{:S(2)}, u32[]{:S(2)}) collective-permute-start(f32[768,128]{1,0:T(8,128)S(1)} %constant_dynamic-update-slice_fusion.25.x_ref), channel_id=1, source_target_pairs={{0,48},{4,52},{8,56},{12,60},{16,0},{20,4},{24,8},{28,12},{32,16},... | collective-permute-start | bytes 1179656 | tf_op jit(solution)/shard_map/ppermute | solution.py:43
  329.5 20.5 %collective-permute-start.45 = (f32[768,128]{1,0:T(8,128)S(1)}, f32[768,128]{1,0:T(8,128)S(1)}, u32[]{:S(2)}, u32[]{:S(2)}) collective-permute-start(f32[768,128]{1,0:T(8,128)S(1)} %constant_dynamic-update-slice_fusion.20.x_ref), channel_id=1, source_target_pairs={{0,4},{4,8},{8,12},{12,0},{16,20},{20,24},{24,28},{28,16},{32,36},... | collective-permute-start | bytes 1179656 | tf_op jit(solution)/shard_map/ppermute | solution.py:43
  330.5 22.4 %collective-permute-start.44 = (f32[768,128]{1,0:T(8,128)S(1)}, f32[768,128]{1,0:T(8,128)S(1)}, u32[]{:S(2)}, u32[]{:S(2)}) collective-permute-start(f32[768,128]{1,0:T(8,128)S(1)} %constant_dynamic-update-slice_fusion.20.x_ref), channel_id=1, source_target_pairs={{0,8},{4,12},{8,0},{12,4},{16,24},{20,28},{24,16},{28,20},{32,40},... | collective-permute-start | bytes 1179656 | tf_op jit(solution)/shard_map/ppermute | solution.py:43
  339.1 16.8 %collective-permute-start.43 = (f32[768,128]{1,0:T(8,128)S(1)}, f32[768,128]{1,0:T(8,128)S(1)}, u32[]{:S(2)}, u32[]{:S(2)}) collective-permute-start(f32[768,128]{1,0:T(8,128)S(1)} %constant_dynamic-update-slice_fusion.20.x_ref), channel_id=1, source_target_pairs={{0,12},{4,0},{8,4},{12,8},{16,28},{20,16},{24,20},{28,24},{32,44},... | collective-permute-start | bytes 1179656 | tf_op jit(solution)/shard_map/ppermute | solution.py:43
  381.3 20.4 %collective-permute-start.58 = (f32[768,128]{1,0:T(8,128)S(1)}, f32[768,128]{1,0:T(8,128)S(1)}, u32[]{:S(2)}, u32[]{:S(2)}) collective-permute-start(f32[768,128]{1,0:T(8,128)S(1)} %slot_price.29), channel_id=1, source_target_pairs={{0,32},{4,36},{8,40},{12,44},{16,48},{20,52},{24,56},{28,60},{32,0... | collective-permute-start | bytes 1179656 | tf_op jit(solution)/shard_map/ppermute | solution.py:43
  384.1 20.4 %collective-permute-start.59 = (f32[768,128]{1,0:T(8,128)S(1)}, f32[768,128]{1,0:T(8,128)S(1)}, u32[]{:S(2)}, u32[]{:S(2)}) collective-permute-start(f32[768,128]{1,0:T(8,128)S(1)} %slot_price.30), channel_id=1, source_target_pairs={{0,16},{4,20},{8,24},{12,28},{16,32},{20,36},{24,40},{28,44},{32,4... | collective-permute-start | bytes 1179656 | tf_op jit(solution)/shard_map/ppermute | solution.py:43
  384.2 20.2 %collective-permute-start.60 = (f32[768,128]{1,0:T(8,128)S(1)}, f32[768,128]{1,0:T(8,128)S(1)}, u32[]{:S(2)}, u32[]{:S(2)}) collective-permute-start(f32[768,128]{1,0:T(8,128)S(1)} %slot_price.31), channel_id=1, source_target_pairs={{0,48},{4,52},{8,56},{12,60},{16,0},{20,4},{24,8},{28,12},{32,16},... | collective-permute-start | bytes 1179656 | tf_op jit(solution)/shard_map/ppermute | solution.py:43
  389.3 16.5 %collective-permute-start.52 = (f32[768,128]{1,0:T(8,128)S(1)}, f32[768,128]{1,0:T(8,128)S(1)}, u32[]{:S(2)}, u32[]{:S(2)}) collective-permute-start(f32[768,128]{1,0:T(8,128)S(1)} %slot_price.25), channel_id=1, source_target_pairs={{0,8},{4,12},{8,0},{12,4},{16,24},{20,28},{24,16},{28,20},{32,40},... | collective-permute-start | bytes 1179656 | tf_op jit(solution)/shard_map/ppermute | solution.py:43
  394.2 17.2 %collective-permute-start.53 = (f32[768,128]{1,0:T(8,128)S(1)}, f32[768,128]{1,0:T(8,128)S(1)}, u32[]{:S(2)}, u32[]{:S(2)}) collective-permute-start(f32[768,128]{1,0:T(8,128)S(1)} %slot_price.26), channel_id=1, source_target_pairs={{0,4},{4,8},{8,12},{12,0},{16,20},{20,24},{24,28},{28,16},{32,36},... | collective-permute-start | bytes 1179656 | tf_op jit(solution)/shard_map/ppermute | solution.py:43
  425.4 23.4 %all-to-all-start.1 = ((f32[128,1,192]{2,1,0:T(1,128)}), f32[128,1,192]{2,1,0:T(1,128)S(1)}, u32[]{:S(2)}, u32[]{:S(2)}) async-start(f32[128,1,192]{2,1,0:T(1,128)} %copy.119), calls=%async_computation.1 | async-start | bytes 262144 | tf_op jit(solution)/shard_map/all_to_all | solution.py:349
  (76 other events, 644.2 us)

commit v2 on v0

v2 whole, which is shorter than its diff:
```python
import jax
import jax.numpy as jnp
from jax import lax
from jax.experimental import pallas as pl
from jax.experimental.pallas import tpu as pltpu
from jax.sharding import PartitionSpec as P

ITERS = 2
S = 64
SUB = 768
CAP = 3
N_BUS = 4
N_BAND = 32
SLOTS = CAP * 128
LINES_DEV = 256
LOAD_ROWS = SUB // 128 * S
SLOT_ROWS = CAP * S

primal_step = 0.5
dual_step = 1.0

NZ, NX, NY = 2, 4, 4
NT = (((1,), (1,)), ((), ()))
NN = (((1,), (0,)), ((), ()))
VMEM = 48 * 1024 * 1024


def band_index(z, x, y):
    return (z * NX + x) * NY + y


def steps_of(stage, core, r):
    if stage == "z":
        return (r, 0, 0)
    along_x = (stage == "first") == (core == 0)
    return (0, r, 0) if along_x else (0, 0, r)


def moved(a, stage, r):
    pairs = []
    for z in range(NZ):
        for x in range(NX):
            for y in range(NY):
                for j in range(N_BUS):
                    dz, dx, dy = steps_of(stage, j % 2, r)
                    to = band_index((z + dz) % NZ, (x + dx) % NX, (y + dy) % NY)
                    pairs.append((band_index(z, x, y) * N_BUS + j, to * N_BUS + j))
    return lax.ppermute(a, ("band", "bus"), pairs)


def gather_z(block):
    return jnp.concatenate([block, moved(block, "z", 1)], axis=0)


def gather_second(eight):
    one, three, two = (moved(eight, "second", -r) for r in (1, 3, 2))
    return [eight, one, two, three]


def ring_first(pair):
    one, three, two = (moved(pair, "first", -r) for r in (1, 3, 2))
    return pair, one, two, three


def gather_first(pair):
    return jnp.concatenate(ring_first(pair), axis=0)


def gather_second(eight):
    one, three, two = (moved(eight, "second", -r) for r in (1, 3, 2))
    return [eight, one, two, three]


def sum_bus(a):
    got = [
        lax.ppermute(a, "bus", [(j, j ^ k) for j in range(N_BUS)]) for k in (2, 3, 1)
    ]
    return (a + got[2]) + (got[0] + got[1])


def sum_band(chunks):
    got = [moved(chunks[r], "second", r) for r in (2, 1, 3)]
    eight = chunks[0] + got[0] + got[1] + got[2]
    n = eight.shape[0] // 4
    parts = [eight[r * n : (r + 1) * n] for r in range(4)]
    got = [moved(parts[r], "first", r) for r in (2, 1, 3)]
    return parts[0] + got[0] + got[1] + got[2]


def sum_z(pair, both):
    n = pair.shape[0] // 2
    if both:
        got = moved(pair, "z", 1)
        return pair + jnp.concatenate([got[n:], got[:n]], axis=0)
    return pair[:n] + moved(pair[n:], "z", 1)


def split(v):
    hi = v.astype(jnp.bfloat16)
    lo = (v - hi.astype(jnp.float32)).astype(jnp.bfloat16)
    return hi, lo


def three_pass(x, w, dims):
    x_hi, x_lo = split(x)
    w_hi, w_lo = split(w)
    n = x.shape[0]
    y = lax.dot_general(
        jnp.concatenate([x_hi, x_lo], axis=0), w_hi, dims, preferred_element_type=jnp.float32
    )
    return y[:n] + (
        y[n:] + lax.dot_general(x_hi, w_lo, dims, preferred_element_type=jnp.float32)
    )


def lanes(ref, count):
    n = ref.shape[0] // count
    return jnp.concatenate([ref[k * n : (k + 1) * n, :] for k in range(count)], axis=1)


def cost(us):
    return pl.CostEstimate(flops=0, bytes_accessed=int(us * 3.0e6), transcendentals=0)


BLOCK_ROWS = LOAD_ROWS + SLOT_ROWS
FIRST_STEP = 4


def first_flow_kernel(idx_ref, load_acc_ref, slot_acc_ref, x_ref, columns_ref, *refs):
    *w_refs, load_ref, slot_ref = refs

    @pl.when(pl.program_id(0) == 0)
    def _():
        load_ref[...] = load_acc_ref[...]
        slot_ref[...] = slot_acc_ref[...]

    load, slots = [], []
    for u in range(0, FIRST_STEP, NZ):
        base = u * BLOCK_ROWS
        load += [x_ref[base + k * S : base + (k + 1) * S, :] for k in range(NZ * SUB // 128)]
        base += NZ * LOAD_ROWS
        slots += [x_ref[base + k * S : base + (k + 1) * S, :] for k in range(NZ * CAP)]
    w = jnp.concatenate([ref[...] for ref in w_refs], axis=1)
    columns = columns_ref[...].reshape(FIRST_STEP * SLOTS, LINES_DEV)
    load_ref[...] -= three_pass(jnp.concatenate(load, axis=1), w, NT)
    slot_ref[...] += three_pass(jnp.concatenate(slots, axis=1), columns, NN)


def first_flow(load_acc, slot_acc, x, columns, ptdf, block_of, start):
    steps = x.shape[0] // (FIRST_STEP * BLOCK_ROWS)
    at = start // FIRST_STEP

    def sub(u):
        return pl.BlockSpec(
            (LINES_DEV, SUB), lambda i, idx: (0, idx[start + i * FIRST_STEP + u])
        )

    return pl.pallas_call(
        first_flow_kernel,
        grid_spec=pltpu.PrefetchScalarGridSpec(
            num_scalar_prefetch=1,
            grid=(steps,),
            in_specs=[
                pl.BlockSpec((S, LINES_DEV), lambda i, idx: (0, 0)),
                pl.BlockSpec((S, LINES_DEV), lambda i, idx: (0, 0)),
                pl.BlockSpec((FIRST_STEP * BLOCK_ROWS, 128), lambda i, idx: (i, 0)),
                pl.BlockSpec((FIRST_STEP, SLOTS, LINES_DEV), lambda i, idx: (at + i, 0, 0)),
            ]
            + [sub(u) for u in range(FIRST_STEP)],
            out_specs=[pl.BlockSpec((S, LINES_DEV), lambda i, idx: (0, 0))] * 2,
        ),
        out_shape=[jax.ShapeDtypeStruct((S, LINES_DEV), jnp.float32)] * 2,
        compiler_params=pltpu.CompilerParams(vmem_limit_bytes=VMEM),
        cost_estimate=cost(3.0 * steps),
        name="first_flow",
    )(block_of, load_acc, slot_acc, x, columns, *([ptdf] * FIRST_STEP))


SLOT_STEPS = 2
SLOT_STEP = 8 // SLOT_STEPS


def slot_flow_kernel(acc_ref, x_ref, w_ref, o_ref):
    @pl.when(pl.program_id(0) == 0)
    def _():
        o_ref[...] = acc_ref[...]

    w = w_ref[...].reshape(SLOT_STEP * SLOTS, LINES_DEV)
    o_ref[...] += three_pass(lanes(x_ref, SLOT_STEP * CAP), w, NN)


def slot_flow(acc, x, columns, r2):
    s = acc.shape[0]
    return pl.pallas_call(
        slot_flow_kernel,
        grid=(SLOT_STEPS,),
        in_specs=[
            pl.BlockSpec((s, LINES_DEV), lambda i: (0, 0)),
            pl.BlockSpec((SLOT_STEP * CAP * s, 128), lambda i: (i, 0)),
            pl.BlockSpec(
                (SLOT_STEP, SLOTS, LINES_DEV), lambda i: (r2 * SLOT_STEPS + i, 0, 0)
            ),
        ],
        out_specs=pl.BlockSpec((s, LINES_DEV), lambda i: (0, 0)),
        out_shape=jax.ShapeDtypeStruct((s, LINES_DEV), jnp.float32),
        compiler_params=pltpu.CompilerParams(vmem_limit_bytes=VMEM),
        cost_estimate=cost(2.0),
        name="slot_flow",
    )(acc, x, columns)


def slot_price_kernel(x_ref, w_ref, *o_refs):
    w = w_ref[...].reshape(8 * SLOTS, LINES_DEV)
    p = three_pass(x_ref[...], w, NT)
    for step, o_ref in enumerate(o_refs):

        @pl.when(pl.program_id(0) == step)
        def _():
            for k in range(8 * CAP):
                o_ref[k * S : (k + 1) * S, :] = p[:, k * 128 : (k + 1) * 128]


def slot_price(x, columns, chunks):
    n, top = len(chunks), chunks[0]
    return pl.pallas_call(
        slot_price_kernel,
        grid=(n,),
        in_specs=[
            pl.BlockSpec((S, LINES_DEV), lambda i: (0, 0)),
            pl.BlockSpec((8, SLOTS, LINES_DEV), lambda i: (top - i, 0, 0)),
        ],
        out_specs=[pl.BlockSpec((8 * SLOT_ROWS, 128), lambda i: (0, 0))] * n,
        out_shape=[jax.ShapeDtypeStruct((8 * SLOT_ROWS, 128), jnp.float32)] * n,
        compiler_params=pltpu.CompilerParams(vmem_limit_bytes=VMEM),
        cost_estimate=cost(2.0 * n),
        name="slot_price",
    )(x, columns)


PICK_STEP = 4
HOT = CAP * N_BUS


def pick_kernel(code_ref, w_ref, o_ref):
    codes = code_ref[...]
    column = lax.broadcasted_iota(jnp.int32, codes.shape, 1)
    bus = lax.broadcasted_iota(jnp.int32, (SLOTS, SUB), 1).astype(jnp.float32) + 1.0
    for u in range(PICK_STEP):
        i = pl.program_id(0) * PICK_STEP + u
        w_hi, w_lo = split(w_ref[:, u * SUB : (u + 1) * SUB])
        code = jnp.sum(jnp.where(column == i, codes, 0.0), axis=1, keepdims=True)
        hot = (bus == code).astype(jnp.float32).astype(jnp.bfloat16)
        picked = lax.dot_general(hot, w_hi, NT, preferred_element_type=jnp.float32)
        picked += lax.dot_general(hot, w_lo, NT, preferred_element_type=jnp.float32)
        for b in range(N_BAND):
            for q in range(HOT):
                o_ref[b, pl.ds(q * N_BAND + i, 1), :] = picked[b * HOT + q : b * HOT + q + 1, :]


def pick(codes, ptdf):
    return pl.pallas_call(
        pick_kernel,
        grid=(N_BAND // PICK_STEP,),
        in_specs=[
            pl.BlockSpec((SLOTS, N_BAND), lambda i: (0, 0)),
            pl.BlockSpec((LINES_DEV, PICK_STEP * SUB), lambda i: (0, i)),
        ],
        out_specs=pl.BlockSpec((N_BAND, SLOTS, LINES_DEV), lambda i: (0, 0, 0)),
        out_shape=jax.ShapeDtypeStruct((N_BAND, SLOTS, LINES_DEV), jnp.float32),
        compiler_params=pltpu.CompilerParams(vmem_limit_bytes=VMEM),
        cost_estimate=cost(30.0),
        name="pick",
    )(codes, ptdf)


def home_columns(bus_map):
    owner = bus_map // SUB
    same = owner[:, None] == owner[None, :]
    earlier = lax.broadcasted_iota(jnp.int32, same.shape, 0) > lax.broadcasted_iota(
        jnp.int32, same.shape, 1
    )
    rank = jnp.sum((same & earlier).astype(jnp.int32), axis=1)
    return owner // N_BAND * 128 + rank * N_BAND + owner % N_BAND, bus_map % SUB


def exact_dot(a, b, dims):
    return lax.dot_general(
        a, b, dims, precision=lax.Precision.HIGHEST, preferred_element_type=jnp.float32
    )


def on_device(
    dispatch0, cost_lin, cost_quad, gen_max, bus_map, demand, ptdf, line_price0, flow_max
):
    band = lax.axis_index("band")
    core = lax.axis_index("bus") % 2
    z, x, y = band // (NX * NY), band // NY % NX, band % NY
    rel = lax.iota(jnp.int32, N_BAND)
    r2, r1, rz = rel // 8, rel // 2 % 4, rel % 2
    dx, dy = jnp.where(core == 0, r1, r2), jnp.where(core == 0, r2, r1)
    block_of = band_index((z + rz) % NZ, (x + dx) % NX, (y + dy) % NY)

    at, local = home_columns(bus_map)
    where = (at[:, None] == lax.broadcasted_iota(jnp.int32, (1, N_BUS * 128), 1)).astype(
        jnp.float32
    )
    own = jnp.concatenate(
        [
            dispatch0,
            (local + 1).astype(jnp.float32)[None],
            cost_lin[None],
            cost_quad[None],
            gen_max[None],
            jnp.zeros((4, dispatch0.shape[1]), jnp.float32),
        ],
        axis=0,
    )
    rows = own.shape[0]
    message = exact_dot(own, where, NN).reshape(rows, N_BUS, 128).transpose(1, 0, 2)
    message_got = lax.all_to_all(message, "bus", split_axis=0, concat_axis=0, tiled=True)
    got = message_got
    got = got[:, :, : CAP * N_BAND].reshape(N_BUS, rows, CAP, N_BAND)
    got = got.transpose(2, 1, 0, 3).reshape(CAP, rows, 128)
    load = demand[:, 0, :].reshape(S, SUB // 128, 128).transpose(1, 0, 2)
    load = gather_z(load.reshape(LOAD_ROWS, 128))
    codes = jnp.pad(got[:, S], ((0, 8 - CAP), (0, 0)))
    codes = lax.all_to_all(
        jnp.broadcast_to(codes, (N_BAND, 8, 128)), "band", split_axis=0, concat_axis=0, tiled=True
    )
    codes = codes[:, :CAP][block_of].reshape(SLOTS, N_BAND)
    params = jnp.pad(
        got[:, S + 1 : S + 4].transpose(1, 0, 2).reshape(3 * CAP, 128), ((0, 16 - 3 * CAP), (0, 0))
    )
    slots = gather_z(
        jnp.concatenate([got[:, :S].reshape(SLOT_ROWS, 128), params], axis=0)
    ).reshape(2, SLOT_ROWS + 16, 128)
    params = slots[:, SLOT_ROWS : SLOT_ROWS + 3 * CAP].reshape(2, 3, CAP, 1, 128)
    lin, quad, top = (params[:, k] for k in range(3))
    slots = slots[:, :SLOT_ROWS].reshape(2 * SLOT_ROWS, 128)
    now = slots.reshape(2, CAP, S, 128)
    load, _ = lax.optimization_barrier((load, message_got))
    parts = []
    for at in zip(ring_first(load), ring_first(slots)):
        parts += at
    eight = jnp.concatenate(parts, axis=0)
    eight, codes = lax.optimization_barrier((eight, codes))
    columns = pick(codes, ptdf)
    one, three = moved(eight, "second", -1), moved(eight, "second", -3)
    one, three, columns = lax.optimization_barrier((one, three, columns))
    n = eight.shape[0] // 2
    two_near, two_far = moved(one[:n], "second", -1), moved(three[n:], "second", -3)
    load_part = slot_part = jnp.zeros((S, LINES_DEV), jnp.float32)
    for x, at in ((eight, 0), (one, 8), (three, 24), (two_near, 16), (two_far, 20)):
        load_part, slot_part = first_flow(
            load_part, slot_part, x, columns, ptdf, block_of, at
        )
    flow = load_part + slot_part

    bound = dual_step * flow_max
    line_price = line_price0
    for iteration in range(ITERS):
        last = iteration == ITERS - 1
        trial = line_price + dual_step * sum_bus(flow)
        price_next = trial - jnp.clip(trial, -bound, bound)
        reflected = 2.0 * price_next - line_price
        line_price = price_next
        three, two, one = slot_price(reflected, columns, (3, 2, 1))
        chunks = [*slot_price(reflected, columns, (0,)), one, two, three]
        unit = sum_z(sum_band(chunks), not last)
        unit = unit.reshape(-1, CAP, S, 128)
        k = unit.shape[0]
        before = now[:k]
        now = jnp.clip(
            (before - primal_step * (lin[:k] + unit)) / (1.0 + primal_step * quad[:k]),
            0.0,
            top[:k],
        )
        if not last:
            slots = gather_second(gather_first(now.reshape(2 * SLOT_ROWS, 128)))
            flow = load_part
            for r in (0, 1, 3, 2):
                flow = slot_flow(flow, slots[r], columns, r)
    slot_values = now[0]
    home = slot_values.reshape(CAP, S, N_BUS, N_BAND).transpose(2, 1, 0, 3)
    home = home.reshape(N_BUS, S, CAP * N_BAND)
    home = jnp.pad(home, ((0, 0), (0, 0), (0, 128 - CAP * N_BAND)))
    home = lax.all_to_all(home, "bus", split_axis=0, concat_axis=0, tiled=True)
    dispatch = exact_dot(home.transpose(1, 0, 2).reshape(S, N_BUS * 128), where, NT)
    return dispatch, line_price


def solution(mesh):
    gens = P(("band", "bus"))
    in_specs = (
        P(None, ("band", "bus")),
        gens,
        gens,
        gens,
        gens,
        P(None, "bus", "band"),
        P("band", "bus"),
        P(None, "band"),
        P("band"),
    )
    out_specs = (P(None, ("band", "bus")), P(None, "band"))
    return jax.shard_map(
        on_device, mesh=mesh, in_specs=in_specs, out_specs=out_specs, check_vma=False
    )
```

time: 665 us -> 260 us (0.39)
  waiting for transfers between devices: 448 us -> 82.1 us
  matrix products: 90.9 us -> 1.32 us
  Pallas kernels: 0 us -> 76.9 us
  starting transfers between devices: 40.9 us -> 71.3 us
  blocking collectives: 26.2 us -> 10.2 us
  other arithmetic: 17.6 us -> 3.68 us
  between operations: 14.7 us -> 1.23 us
  local copies, waits for them, and re-layouts: 22.2 us -> 12.7 us
    all_gather x2 -> x0, waiting for transfers between devices: 250 us -> none  [on_device(): lax.all_gather(injection, 'band', axis=1, tiled=True)]
    all_to_all x6 -> x2, waiting for transfers between devices: 198 us -> 0.01 us  [the longest x1 0.01 us: on_device(): lax.all_to_all(message, 'bus', split_axis=0, concat_axis=0, tiled=True)]
    dot_general x4 -> x2, matrix products: 90.9 us -> 1.32 us  [exact_dot(): lax.dot_general(a, b, dims, precision=lax.Precision.HIGHEST, preferred_el...]
    ppermute x0 -> x38, waiting for transfers between devices: none -> 82.1 us  [the longest x32 75.6 us: moved(): return lax.ppermute(a, ('band', 'bus'), pairs)]
    pallas_call x0 -> x14, Pallas kernels: none -> 76.9 us  [the longest x5 25.6 us: first_flow(): pl.pallas_call(first_flow_kernel, grid_spec=pltpu.PrefetchScalarGridSpec(...]
    ppermute x0 -> x38, starting transfers between devices: none -> 57.6 us  [the longest x32 41.2 us: moved(): return lax.ppermute(a, ('band', 'bus'), pairs)]
    all_to_all x6 -> x2, starting transfers between devices: 40.8 us -> 13.7 us  [the longest x1 9 us: on_device(): lax.all_to_all(jnp.broadcast_to(codes, (N_BAND, 8, 128)), 'band', split_a...]
    all_gather x4 -> x0, blocking collectives: 26.2 us -> none  [the longest x2 13.6 us: on_device(): line_price = lax.all_gather(price_next, 'bus', axis=1, tiled=True)]
  transfers between devices with their start and end apart: 8 -> 40, of which waited for: 8 -> 22; matrix products, arithmetic and copies ran while one was open for 1% -> 4% of each run, Pallas kernels for 0% -> 22%
where the time goes in v2:
time: 260 us; the launch traced here: 259 us
  waiting for transfers between devices  82.1 us (32%)
  Pallas kernels  76.9 us (30%)
  starting transfers between devices  71.3 us (27%)
  local copies, waits for them, and re-layouts  12.7 us (5%)
  blocking collectives  10.2 us (4%)
  other arithmetic  3.68 us (1%)
    ppermute x32, waiting for transfers between devices, moved(): return lax.ppermute(a, ('band', 'bus'), pairs)  75.6 us
    ppermute x32, starting transfers between devices, moved(): return lax.ppermute(a, ('band', 'bus'), pairs)  41.2 us
    pallas_call x5, Pallas kernels, first_flow(): pl.pallas_call(first_flow_kernel, grid_spec=pltpu.PrefetchScalarGridSpec(...  25.6 us
    pallas_call x1, Pallas kernels, pick(): pl.pallas_call(pick_kernel, grid=(N_BAND // PICK_STEP,), in_specs=[pl.Blo...  23.9 us
    pallas_call x4, Pallas kernels, slot_price(): pl.pallas_call(slot_price_kernel, grid=(n,), in_specs=[pl.BlockSpec((S, L...  18.2 us
    ppermute x6, starting transfers between devices, sum_bus(): lax.ppermute(a, 'bus', [(j, j ^ k) for j in range(N_BUS)])  16.3 us
    all_to_all x1, blocking collectives, on_device(): home = lax.all_to_all(home, 'bus', split_axis=0, concat_axis=0, tiled=True)  10.2 us
    pallas_call x4, Pallas kernels, slot_flow(): pl.pallas_call(slot_flow_kernel, grid=(SLOT_STEPS,), in_specs=[pl.BlockSp...  9.17 us
  transfers between devices with their start and end apart: 40, of which 22 were waited for; matrix products, arithmetic and copies ran while one was open for 4% of the time, Pallas kernels for 22%

profile of v2, /device:TPU:1, one launch (start us, length us, event | category | flops | bytes accessed | tf_op | source)
XLA Modules:
  0.0 259.3 jit_solution(9693337347318064136)
XLA Ops:
  4.1 4.7 %all-to-all-start = ((f32[4,72,128]{2,1,0:T(8,128)}), f32[4,72,128]{2,1,0:T(8,128)S(1)}, u32[]{:S(2)}, u32[]{:S(2)}) async-start(f32[4,72,128]{2,1,0:T(8,128)} %bitcast.70), calls=%async_computation | async-start | bytes 294912 | tf_op jit(solution)/shard_map/all_to_all | solution.py:320
  10.3 3.8 %collective-permute-start.1 = (f32[384,128]{1,0:T(8,128)S(1)}, f32[384,128]{1,0:T(8,128)S(1)}, u32[]{:S(2)}, u32[]{:S(2)}) collective-permute-start(f32[384,128]{1,0:T(8,128)S(1)} %bitcast.87), channel_id=1, source_target_pairs={{0,64},{1,65},{2,66},{3,67},{4,68},{5,69},{6,70},{7,71},{8,72},{9,... | collective-permute-start | bytes 589832 | tf_op jit(solution)/shard_map/ppermute | solution.py:48
  15.3 9.0 %all-to-all-start.1 = ((f32[32,8,128]{2,1,0:T(8,128)}), f32[32,8,128]{2,1,0:T(8,128)}, u32[]{:S(2)}, u32[]{:S(2)}) async-start(f32[32,8,128]{2,1,0:T(8,128)} %broadcast_in_dim.37), calls=%async_computation.1 | async-start | bytes 262144 | tf_op jit(solution)/shard_map/all_to_all | solution.py:327
  27.1 2.8 %collective-permute-start = (f32[208,128]{1,0:T(8,128)S(1)}, f32[208,128]{1,0:T(8,128)S(1)}, u32[]{:S(2)}, u32[]{:S(2)}) collective-permute-start(f32[208,128]{1,0:T(8,128)S(1)} %pad_maximum_fusion.3), channel_id=1, source_target_pairs={{0,64},{1,65},{2,66},{3,67},{4,68},{5,69},{6,70},{7,71},{8,72},{9,... | collective-permute-start | bytes 319496 | tf_op jit(solution)/shard_map/ppermute | solution.py:48
  42.7 2.8 %collective-permute-done.5 = f32[384,128]{1,0:T(8,128)S(1)} collective-permute-done((f32[384,128]{1,0:T(8,128)S(1)}, f32[384,128]{1,0:T(8,128)S(1)}, u32[]{:S(2)}, u32[]{:S(2)}) %collective-permute-start.5) | collective-permute-done | bytes 196640 | tf_op jit(solution)/shard_map/ppermute | solution.py:48
  50.2 23.9 %pick.1.columns_ref.w_ref = f32[32,384,256]{2,1,0:T(8,128)} custom-call(f32[384,32]{1,0:T(8,128)S(1)} %reshape.361.code_ref, f32[256,24576]{1,0:T(8,128)} %refs_3_.9), custom_call_target="tpu_custom_call" | custom-call | bytes 90000000 | tf_op jit(solution)/shard_map/pick/pallas_call | solution.py:261
  76.8 2.7 %collective-permute-start.10 = (f32[2304,128]{1,0:T(8,128)S(1)}, f32[2304,128]{1,0:T(8,128)S(1)}, u32[]{:S(2)}, u32[]{:S(2)}) collective-permute-start(f32[2304,128]{1,0:T(8,128)S(1)} %slice.100), channel_id=1, source_target_pairs={{0,12},{1,49},{2,14},{3,51},{4,0},{5,53},{6,2},{7,55},{8,4},{9,57}... | collective-permute-start | bytes 3538952 | tf_op jit(solution)/shard_map/ppermute | solution.py:48
  79.9 5.7 %first_flow.5 = (f32[64,256]{1,0:T(8,128)S(1)}, f32[64,256]{1,0:T(8,128)S(1)}) custom-call(s32[32]{0:T(128)S(1)} %fusion.27.idx_ref, f32[64,256]{1,0:T(8,128)S(1)} %broadcast_in_dim.36.load_acc_ref.slot_acc_ref, f32[64,256]{1,0:T(8,128)S(1)} %broadcast_in_dim.36.load_acc_ref.slot_acc_ref, f32[4608,128]{1,0:T(8,128)S(1)} %constant_dynamic-update-slice_fusion.x_ref, ...), custom_call_target="tpu_custom_call" | custom-call | bytes 18000000 | tf_op jit(solution)/shard_map/first_flow/pallas_call | solution.py:158
  85.6 5.9 %first_flow.6 = (f32[64,256]{1,0:T(8,128)S(1)}, f32[64,256]{1,0:T(8,128)S(1)}) custom-call(s32[32]{0:T(128)S(1)} %fusion.27.idx_ref, f32[64,256]{1,0:T(8,128)S(1)} %get-tuple-element.28.load_acc_ref, f32[64,256]{1,0:T(8,128)S(1)} %get-tuple-element.29.slot_acc_ref, f32[4608,128]{1,0:T(8,128)S(1)} %collective-permute-done.8.x_ref, ...), custom_call_target="tpu_custom_call" | custom-call | bytes 18000000 | tf_op jit(solution)/shard_map/first_flow/pallas_call | solution.py:158
  91.5 5.7 %first_flow.7 = (f32[64,256]{1,0:T(8,128)S(1)}, f32[64,256]{1,0:T(8,128)S(1)}) custom-call(s32[32]{0:T(128)S(1)} %fusion.27.idx_ref, f32[64,256]{1,0:T(8,128)S(1)} %get-tuple-element.31.load_acc_ref, f32[64,256]{1,0:T(8,128)S(1)} %get-tuple-element.32.slot_acc_ref, f32[4608,128]{1,0:T(8,128)S(1)} %collective-permute-done.9.x_ref, ...), custom_call_target="tpu_custom_call" | custom-call | bytes 18000000 | tf_op jit(solution)/shard_map/first_flow/pallas_call | solution.py:158
  97.2 4.2 %first_flow.8 = (f32[64,256]{1,0:T(8,128)S(1)}, f32[64,256]{1,0:T(8,128)S(1)}) custom-call(s32[32]{0:T(128)S(1)} %fusion.27.idx_ref, f32[64,256]{1,0:T(8,128)S(1)} %get-tuple-element.34.load_acc_ref, f32[64,256]{1,0:T(8,128)S(1)} %get-tuple-element.35.slot_acc_ref, f32[2304,128]{1,0:T(8,128)S(1)} %collective-permute-done.10.x_ref, ...), custom_call_target="tpu_custom_call" | custom-call | bytes 9000000 | tf_op jit(solution)/shard_map/first_flow/pallas_call | solution.py:158
  101.4 4.2 %first_flow.9 = (f32[64,256]{1,0:T(8,128)S(1)}, f32[64,256]{1,0:T(8,128)S(1)}) custom-call(s32[32]{0:T(128)S(1)} %fusion.27.idx_ref, f32[64,256]{1,0:T(8,128)S(1)} %get-tuple-element.36.load_acc_ref, f32[64,256]{1,0:T(8,128)S(1)} %get-tuple-element.37.slot_acc_ref, f32[2304,128]{1,0:T(8,128)S(1)} %collective-permute-done.11.x_ref, ...), custom_call_target="tpu_custom_call" | custom-call | bytes 9000000 | tf_op jit(solution)/shard_map/first_flow/pallas_call | solution.py:158
  105.6 4.0 %collective-permute-start.14 = (f32[64,256]{1,0:T(8,128)S(1)}, f32[64,256]{1,0:T(8,128)S(1)}, u32[]{:S(2)}, u32[]{:S(2)}) collective-permute-start(f32[64,256]{1,0:T(8,128)S(1)} %add.379), channel_id=1, source_target_pairs={{0,3},{1,2},{2,1},{3,0},{4,7},{5,6},{6,5},{7,4},{8,11},{9,10},{10,... | collective-permute-start | bytes 196616 | tf_op jit(solution)/shard_map/ppermute | solution.py:76
  111.7 3.2 %collective-permute-done.13 = f32[64,256]{1,0:T(8,128)S(1)} collective-permute-done((f32[64,256]{1,0:T(8,128)S(1)}, f32[64,256]{1,0:T(8,128)S(1)}, u32[]{:S(2)}, u32[]{:S(2)}) %collective-permute-start.13) | collective-permute-done | bytes 65568 | tf_op jit(solution)/shard_map/ppermute | solution.py:76
  115.0 6.1 %slot_price.5 = (f32[1536,128]{1,0:T(8,128)S(1)}, f32[1536,128]{1,0:T(8,128)S(1)}, f32[1536,128]{1,0:T(8,128)S(1)}) custom-call(f32[64,256]{1,0:T(8,128)S(1)} %get-tuple-element.50.x_ref, f32[32,384,256]{2,1,0:T(8,128)} %pick.1.columns_ref.w_ref), custom_call_target="tpu_custom_call" | custom-call | bytes 18000000 | tf_op jit(solution)/shard_map/slot_price/pallas_call | solution.py:225
  123.9 3.0 %slot_price.4 = f32[1536,128]{1,0:T(8,128)S(1)} custom-call(f32[64,256]{1,0:T(8,128)S(1)} %get-tuple-element.50.x_ref, f32[32,384,256]{2,1,0:T(8,128)} %pick.1.columns_ref.w_ref), custom_call_target="tpu_custom_call" | custom-call | bytes 6000000 | tf_op jit(solution)/shard_map/slot_price/pallas_call | solution.py:225
  126.9 6.9 %collective-permute-done.15 = f32[1536,128]{1,0:T(8,128)S(1)} collective-permute-done((f32[1536,128]{1,0:T(8,128)S(1)}, f32[1536,128]{1,0:T(8,128)S(1)}, u32[]{:S(2)}, u32[]{:S(2)}) %collective-permute-start.15) | collective-permute-done | bytes 786464 | tf_op jit(solution)/shard_map/ppermute | solution.py:48
  133.8 8.2 %collective-permute-done.16 = f32[1536,128]{1,0:T(8,128)S(1)} collective-permute-done((f32[1536,128]{1,0:T(8,128)S(1)}, f32[1536,128]{1,0:T(8,128)S(1)}, u32[]{:S(2)}, u32[]{:S(2)}) %collective-permute-start.16) | collective-permute-done | bytes 786464 | tf_op jit(solution)/shard_map/ppermute | solution.py:48
  148.3 3.0 %collective-permute-done.20 = f32[384,128]{1,0:T(8,128)S(1)} collective-permute-done((f32[384,128]{1,0:T(8,128)S(1)}, f32[384,128]{1,0:T(8,128)S(1)}, u32[]{:S(2)}, u32[]{:S(2)}) %collective-permute-start.20) | collective-permute-done | bytes 196640 | tf_op jit(solution)/shard_map/ppermute | solution.py:48
  153.8 3.7 %collective-permute-done.21 = f32[384,128]{1,0:T(8,128)S(1)} collective-permute-done((f32[384,128]{1,0:T(8,128)S(1)}, f32[384,128]{1,0:T(8,128)S(1)}, u32[]{:S(2)}, u32[]{:S(2)}) %collective-permute-start.21) | collective-permute-done | bytes 196640 | tf_op jit(solution)/shard_map/ppermute | solution.py:48
  157.7 3.3 %collective-permute-start.23 = (f32[384,128]{1,0:T(8,128)S(1)}, f32[384,128]{1,0:T(8,128)S(1)}, u32[]{:S(2)}, u32[]{:S(2)}) collective-permute-start(f32[384,128]{1,0:T(8,128)S(1)} %get-tuple-element.48), channel_id=1, source_target_pairs={{0,32},{1,9},{2,34},{3,11},{4,36},{5,13},{6,38},{7,15},{8,40},{9,1... | collective-permute-start | bytes 589832 | tf_op jit(solution)/shard_map/ppermute | solution.py:48
  163.4 3.0 %collective-permute-done.23 = f32[384,128]{1,0:T(8,128)S(1)} collective-permute-done((f32[384,128]{1,0:T(8,128)S(1)}, f32[384,128]{1,0:T(8,128)S(1)}, u32[]{:S(2)}, u32[]{:S(2)}) %collective-permute-start.23) | collective-permute-done | bytes 196640 | tf_op jit(solution)/shard_map/ppermute | solution.py:48
  170.6 8.4 %collective-permute-done.25.x_ref = f32[1536,128]{1,0:T(8,128)S(1)} collective-permute-done((f32[1536,128]{1,0:T(8,128)S(1)}, f32[1536,128]{1,0:T(8,128)S(1)}, u32[]{:S(2)}, u32[]{:S(2)}) %collective-permute-start.25) | collective-permute-done | bytes 786464 | tf_op jit(solution)/shard_map/ppermute | solution.py:48
  181.3 6.5 %collective-permute-done.26.x_ref = f32[1536,128]{1,0:T(8,128)S(1)} collective-permute-done((f32[1536,128]{1,0:T(8,128)S(1)}, f32[1536,128]{1,0:T(8,128)S(1)}, u32[]{:S(2)}, u32[]{:S(2)}) %collective-permute-start.26) | collective-permute-done | bytes 786464 | tf_op jit(solution)/shard_map/ppermute | solution.py:48
  192.4 8.4 %collective-permute-start.30 = (f32[64,256]{1,0:T(8,128)S(1)}, f32[64,256]{1,0:T(8,128)S(1)}, u32[]{:S(2)}, u32[]{:S(2)}) collective-permute-start(f32[64,256]{1,0:T(8,128)S(1)} %slot_flow.7), channel_id=1, source_target_pairs={{0,3},{1,2},{2,1},{3,0},{4,7},{5,6},{6,5},{7,4},{8,11},{9,10},{10,... | collective-permute-start | bytes 196616 | tf_op jit(solution)/shard_map/ppermute | solution.py:76
  202.7 3.2 %collective-permute-done.29 = f32[64,256]{1,0:T(8,128)S(1)} collective-permute-done((f32[64,256]{1,0:T(8,128)S(1)}, f32[64,256]{1,0:T(8,128)S(1)}, u32[]{:S(2)}, u32[]{:S(2)}) %collective-permute-start.29) | collective-permute-done | bytes 65568 | tf_op jit(solution)/shard_map/ppermute | solution.py:76
  206.6 6.1 %slot_price.7 = (f32[1536,128]{1,0:T(8,128)S(1)}, f32[1536,128]{1,0:T(8,128)S(1)}, f32[1536,128]{1,0:T(8,128)S(1)}) custom-call(f32[64,256]{1,0:T(8,128)S(1)} %get-tuple-element.46.x_ref, f32[32,384,256]{2,1,0:T(8,128)} %pick.1.columns_ref.w_ref), custom_call_target="tpu_custom_call" | custom-call | bytes 18000000 | tf_op jit(solution)/shard_map/slot_price/pallas_call | solution.py:225
  216.1 3.0 %slot_price.6 = f32[1536,128]{1,0:T(8,128)S(1)} custom-call(f32[64,256]{1,0:T(8,128)S(1)} %get-tuple-element.46.x_ref, f32[32,384,256]{2,1,0:T(8,128)} %pick.1.columns_ref.w_ref), custom_call_target="tpu_custom_call" | custom-call | bytes 6000000 | tf_op jit(solution)/shard_map/slot_price/pallas_call | solution.py:225
  219.1 6.4 %collective-permute-done.31 = f32[1536,128]{1,0:T(8,128)S(1)} collective-permute-done((f32[1536,128]{1,0:T(8,128)S(1)}, f32[1536,128]{1,0:T(8,128)S(1)}, u32[]{:S(2)}, u32[]{:S(2)}) %collective-permute-start.31) | collective-permute-done | bytes 786464 | tf_op jit(solution)/shard_map/ppermute | solution.py:48
  225.5 8.4 %collective-permute-done.32 = f32[1536,128]{1,0:T(8,128)S(1)} collective-permute-done((f32[1536,128]{1,0:T(8,128)S(1)}, f32[1536,128]{1,0:T(8,128)S(1)}, u32[]{:S(2)}, u32[]{:S(2)}) %collective-permute-start.32) | collective-permute-done | bytes 786464 | tf_op jit(solution)/shard_map/ppermute | solution.py:48
  237.1 3.7 %collective-permute-done.34 = f32[384,128]{1,0:T(8,128)S(1)} collective-permute-done((f32[384,128]{1,0:T(8,128)S(1)}, f32[384,128]{1,0:T(8,128)S(1)}, u32[]{:S(2)}, u32[]{:S(2)}) %collective-permute-start.34) | collective-permute-done | bytes 196640 | tf_op jit(solution)/shard_map/ppermute | solution.py:48
  248.1 10.2 %all_to_all.15 = f32[4,64,128]{2,1,0:T(8,128)S(1)} all-to-all(f32[4,64,128]{2,1,0:T(8,128)S(1)} %pad.14.clone), channel_id=1, replica_groups=mesh['band'=32,'bus'=4] {'bus'}, dimensions={0} | all-to-all | bytes 262144 | tf_op jit(solution)/shard_map/all_to_all | solution.py:387
  (151 shorter events, 74.0 us)
Async XLA Ops:
  4.1 10.0 %all-to-all-start = ((f32[4,72,128]{2,1,0:T(8,128)}), f32[4,72,128]{2,1,0:T(8,128)S(1)}, u32[]{:S(2)}, u32[]{:S(2)}) async-start(f32[4,72,128]{2,1,0:T(8,128)} %bitcast.70), calls=%async_computation | async-start | bytes 294912 | tf_op jit(solution)/shard_map/all_to_all | solution.py:320
  10.3 14.2 %collective-permute-start.1 = (f32[384,128]{1,0:T(8,128)S(1)}, f32[384,128]{1,0:T(8,128)S(1)}, u32[]{:S(2)}, u32[]{:S(2)}) collective-permute-start(f32[384,128]{1,0:T(8,128)S(1)} %bitcast.87), channel_id=1, source_target_pairs={{0,64},{1,65},{2,66},{3,67},{4,68},{5,69},{6,70},{7,71},{8,72},{9,... | collective-permute-start | bytes 589832 | tf_op jit(solution)/shard_map/ppermute | solution.py:48
  15.3 20.6 %all-to-all-start.1 = ((f32[32,8,128]{2,1,0:T(8,128)}), f32[32,8,128]{2,1,0:T(8,128)}, u32[]{:S(2)}, u32[]{:S(2)}) async-start(f32[32,8,128]{2,1,0:T(8,128)} %broadcast_in_dim.37), calls=%async_computation.1 | async-start | bytes 262144 | tf_op jit(solution)/shard_map/all_to_all | solution.py:327
  24.6 14.4 %collective-permute-start.2 = (f32[768,128]{1,0:T(8,128)S(1)}, f32[768,128]{1,0:T(8,128)}, u32[]{:S(2)}, u32[]{:S(2)}) collective-permute-start(f32[768,128]{1,0:T(8,128)S(1)} %pad_maximum_fusion.1), channel_id=1, source_target_pairs={{0,48},{1,13},{2,50},{3,15},{4,52},{5,1},{6,54},{7,3},{8,56},{9,5}... | collective-permute-start | bytes 1179656 | tf_op jit(solution)/shard_map/ppermute | solution.py:48
  27.1 6.0 %collective-permute-start = (f32[208,128]{1,0:T(8,128)S(1)}, f32[208,128]{1,0:T(8,128)S(1)}, u32[]{:S(2)}, u32[]{:S(2)}) collective-permute-start(f32[208,128]{1,0:T(8,128)S(1)} %pad_maximum_fusion.3), channel_id=1, source_target_pairs={{0,64},{1,65},{2,66},{3,67},{4,68},{5,69},{6,70},{7,71},{8,72},{9,... | collective-permute-start | bytes 319496 | tf_op jit(solution)/shard_map/ppermute | solution.py:48
  29.8 15.7 %collective-permute-start.6 = (f32[768,128]{1,0:T(8,128)S(1)}, f32[768,128]{1,0:T(8,128)S(1)}, u32[]{:S(2)}, u32[]{:S(2)}) collective-permute-start(f32[768,128]{1,0:T(8,128)S(1)} %pad_maximum_fusion.1), channel_id=1, source_target_pairs={{0,16},{1,5},{2,18},{3,7},{4,20},{5,9},{6,22},{7,11},{8,24},{9,13}... | collective-permute-start | bytes 1179656 | tf_op jit(solution)/shard_map/ppermute | solution.py:48
  29.8 11.9 %collective-permute-start.4 = (f32[768,128]{1,0:T(8,128)S(1)}, f32[768,128]{1,0:T(8,128)}, u32[]{:S(2)}, u32[]{:S(2)}) collective-permute-start(f32[768,128]{1,0:T(8,128)S(1)} %pad_maximum_fusion.1), channel_id=1, source_target_pairs={{0,32},{1,9},{2,34},{3,11},{4,36},{5,13},{6,38},{7,15},{8,40},{9,1... | collective-permute-start | bytes 1179656 | tf_op jit(solution)/shard_map/ppermute | solution.py:48
  33.2 13.3 %collective-permute-start.7 = (f32[384,128]{1,0:T(8,128)S(1)}, f32[384,128]{1,0:T(8,128)}, u32[]{:S(2)}, u32[]{:S(2)}) collective-permute-start(f32[384,128]{1,0:T(8,128)S(1)} %bitcast.77), channel_id=1, source_target_pairs={{0,16},{1,5},{2,18},{3,7},{4,20},{5,9},{6,22},{7,11},{8,24},{9,13}... | collective-permute-start | bytes 589832 | tf_op jit(solution)/shard_map/ppermute | solution.py:48
  33.8 7.0 %collective-permute-start.3 = (f32[384,128]{1,0:T(8,128)S(1)}, f32[384,128]{1,0:T(8,128)}, u32[]{:S(2)}, u32[]{:S(2)}) collective-permute-start(f32[384,128]{1,0:T(8,128)S(1)} %bitcast.78), channel_id=1, source_target_pairs={{0,48},{1,13},{2,50},{3,15},{4,52},{5,1},{6,54},{7,3},{8,56},{9,5}... | collective-permute-start | bytes 589832 | tf_op jit(solution)/shard_map/ppermute | solution.py:48
  39.1 6.5 %collective-permute-start.5 = (f32[384,128]{1,0:T(8,128)S(1)}, f32[384,128]{1,0:T(8,128)S(1)}, u32[]{:S(2)}, u32[]{:S(2)}) collective-permute-start(f32[384,128]{1,0:T(8,128)S(1)} %bitcast.80), channel_id=1, source_target_pairs={{0,32},{1,9},{2,34},{3,11},{4,36},{5,13},{6,38},{7,15},{8,40},{9,1... | collective-permute-start | bytes 589832 | tf_op jit(solution)/shard_map/ppermute | solution.py:48
  47.4 29.3 %collective-permute-start.9 = (f32[4608,128]{1,0:T(8,128)S(1)}, f32[4608,128]{1,0:T(8,128)S(1)}, u32[]{:S(2)}, u32[]{:S(2)}) collective-permute-start(f32[4608,128]{1,0:T(8,128)S(1)} %constant_dynamic-update-slice_fusion.x_ref), channel_id=1, source_target_pairs={{0,4},{1,17},{2,6},{3,19},{4,8},{5,21},{6,10},{7,23},{8,12},{9,25}... | collective-permute-start | bytes 7077896 | tf_op jit(solution)/shard_map/ppermute | solution.py:48
  48.7 28.1 %collective-permute-start.8 = (f32[4608,128]{1,0:T(8,128)S(1)}, f32[4608,128]{1,0:T(8,128)S(1)}, u32[]{:S(2)}, u32[]{:S(2)}) collective-permute-start(f32[4608,128]{1,0:T(8,128)S(1)} %constant_dynamic-update-slice_fusion.x_ref), channel_id=1, source_target_pairs={{0,12},{1,49},{2,14},{3,51},{4,0},{5,53},{6,2},{7,55},{8,4},{9,57}... | collective-permute-start | bytes 7077896 | tf_op jit(solution)/shard_map/ppermute | solution.py:48
  76.8 20.4 %collective-permute-start.10 = (f32[2304,128]{1,0:T(8,128)S(1)}, f32[2304,128]{1,0:T(8,128)S(1)}, u32[]{:S(2)}, u32[]{:S(2)}) collective-permute-start(f32[2304,128]{1,0:T(8,128)S(1)} %slice.100), channel_id=1, source_target_pairs={{0,12},{1,49},{2,14},{3,51},{4,0},{5,53},{6,2},{7,55},{8,4},{9,57}... | collective-permute-start | bytes 3538952 | tf_op jit(solution)/shard_map/ppermute | solution.py:48
  79.6 21.7 %collective-permute-start.11 = (f32[2304,128]{1,0:T(8,128)S(1)}, f32[2304,128]{1,0:T(8,128)S(1)}, u32[]{:S(2)}, u32[]{:S(2)}) collective-permute-start(f32[2304,128]{1,0:T(8,128)S(1)} %slice.101), channel_id=1, source_target_pairs={{0,4},{1,17},{2,6},{3,19},{4,8},{5,21},{6,10},{7,23},{8,12},{9,25}... | collective-permute-start | bytes 3538952 | tf_op jit(solution)/shard_map/ppermute | solution.py:48
  105.6 6.1 %collective-permute-start.14 = (f32[64,256]{1,0:T(8,128)S(1)}, f32[64,256]{1,0:T(8,128)S(1)}, u32[]{:S(2)}, u32[]{:S(2)}) collective-permute-start(f32[64,256]{1,0:T(8,128)S(1)} %add.379), channel_id=1, source_target_pairs={{0,3},{1,2},{2,1},{3,0},{4,7},{5,6},{6,5},{7,4},{8,11},{9,10},{10,... | collective-permute-start | bytes 196616 | tf_op jit(solution)/shard_map/ppermute | solution.py:76
  121.1 12.8 %collective-permute-start.15 = (f32[1536,128]{1,0:T(8,128)S(1)}, f32[1536,128]{1,0:T(8,128)S(1)}, u32[]{:S(2)}, u32[]{:S(2)}) collective-permute-start(f32[1536,128]{1,0:T(8,128)S(1)} %get-tuple-element.40), channel_id=1, source_target_pairs={{0,8},{1,33},{2,10},{3,35},{4,12},{5,37},{6,14},{7,39},{8,0},{9,41... | collective-permute-start | bytes 2359304 | tf_op jit(solution)/shard_map/ppermute | solution.py:48
  121.2 20.8 %collective-permute-start.16 = (f32[1536,128]{1,0:T(8,128)S(1)}, f32[1536,128]{1,0:T(8,128)S(1)}, u32[]{:S(2)}, u32[]{:S(2)}) collective-permute-start(f32[1536,128]{1,0:T(8,128)S(1)} %get-tuple-element.41), channel_id=1, source_target_pairs={{0,4},{1,17},{2,6},{3,19},{4,8},{5,21},{6,10},{7,23},{8,12},{9,25}... | collective-permute-start | bytes 2359304 | tf_op jit(solution)/shard_map/ppermute | solution.py:48
  121.6 20.4 %collective-permute-start.17 = (f32[1536,128]{1,0:T(8,128)S(1)}, f32[1536,128]{1,0:T(8,128)S(1)}, u32[]{:S(2)}, u32[]{:S(2)}) collective-permute-start(f32[1536,128]{1,0:T(8,128)S(1)} %get-tuple-element.42), channel_id=1, source_target_pairs={{0,12},{1,49},{2,14},{3,51},{4,0},{5,53},{6,2},{7,55},{8,4},{9,57}... | collective-permute-start | bytes 2359304 | tf_op jit(solution)/shard_map/ppermute | solution.py:48
  142.2 6.1 %collective-permute-start.18 = (f32[384,128]{1,0:T(8,128)S(1)}, f32[384,128]{1,0:T(8,128)S(1)}, u32[]{:S(2)}, u32[]{:S(2)}) collective-permute-start(f32[384,128]{1,0:T(8,128)S(1)} %get-tuple-element.55), channel_id=1, source_target_pairs={{0,32},{1,9},{2,34},{3,11},{4,36},{5,13},{6,38},{7,15},{8,40},{9,1... | collective-permute-start | bytes 589832 | tf_op jit(solution)/shard_map/ppermute | solution.py:48
  143.7 7.6 %collective-permute-start.20 = (f32[384,128]{1,0:T(8,128)S(1)}, f32[384,128]{1,0:T(8,128)S(1)}, u32[]{:S(2)}, u32[]{:S(2)}) collective-permute-start(f32[384,128]{1,0:T(8,128)S(1)} %get-tuple-element.56), channel_id=1, source_target_pairs={{0,48},{1,13},{2,50},{3,15},{4,52},{5,1},{6,54},{7,3},{8,56},{9,5}... | collective-permute-start | bytes 589832 | tf_op jit(solution)/shard_map/ppermute | solution.py:48
  145.3 6.0 %collective-permute-start.19 = (f32[384,128]{1,0:T(8,128)S(1)}, f32[384,128]{1,0:T(8,128)S(1)}, u32[]{:S(2)}, u32[]{:S(2)}) collective-permute-start(f32[384,128]{1,0:T(8,128)S(1)} %get-tuple-element.57), channel_id=1, source_target_pairs={{0,16},{1,5},{2,18},{3,7},{4,20},{5,9},{6,22},{7,11},{8,24},{9,13}... | collective-permute-start | bytes 589832 | tf_op jit(solution)/shard_map/ppermute | solution.py:48
  151.4 6.1 %collective-permute-start.21 = (f32[384,128]{1,0:T(8,128)S(1)}, f32[384,128]{1,0:T(8,128)S(1)}, u32[]{:S(2)}, u32[]{:S(2)}) collective-permute-start(f32[384,128]{1,0:T(8,128)S(1)} %fusion.4), channel_id=1, source_target_pairs={{0,64},{1,65},{2,66},{3,67},{4,68},{5,69},{6,70},{7,71},{8,72},{9,... | collective-permute-start | bytes 589832 | tf_op jit(solution)/shard_map/ppermute | solution.py:48
  157.7 8.7 %collective-permute-start.23 = (f32[384,128]{1,0:T(8,128)S(1)}, f32[384,128]{1,0:T(8,128)S(1)}, u32[]{:S(2)}, u32[]{:S(2)}) collective-permute-start(f32[384,128]{1,0:T(8,128)S(1)} %get-tuple-element.48), channel_id=1, source_target_pairs={{0,32},{1,9},{2,34},{3,11},{4,36},{5,13},{6,38},{7,15},{8,40},{9,1... | collective-permute-start | bytes 589832 | tf_op jit(solution)/shard_map/ppermute | solution.py:48
  166.5 12.5 %collective-permute-start.25 = (f32[1536,128]{1,0:T(8,128)S(1)}, f32[1536,128]{1,0:T(8,128)S(1)}, u32[]{:S(2)}, u32[]{:S(2)}) collective-permute-start(f32[1536,128]{1,0:T(8,128)S(1)} %pad_maximum_fusion.x_ref), channel_id=1, source_target_pairs={{0,12},{1,49},{2,14},{3,51},{4,0},{5,53},{6,2},{7,55},{8,4},{9,57}... | collective-permute-start | bytes 2359304 | tf_op jit(solution)/shard_map/ppermute | solution.py:48
  167.0 20.8 %collective-permute-start.26 = (f32[1536,128]{1,0:T(8,128)S(1)}, f32[1536,128]{1,0:T(8,128)S(1)}, u32[]{:S(2)}, u32[]{:S(2)}) collective-permute-start(f32[1536,128]{1,0:T(8,128)S(1)} %pad_maximum_fusion.x_ref), channel_id=1, source_target_pairs={{0,4},{1,17},{2,6},{3,19},{4,8},{5,21},{6,10},{7,23},{8,12},{9,25}... | collective-permute-start | bytes 2359304 | tf_op jit(solution)/shard_map/ppermute | solution.py:48
  168.3 21.9 %collective-permute-start.27 = (f32[1536,128]{1,0:T(8,128)S(1)}, f32[1536,128]{1,0:T(8,128)S(1)}, u32[]{:S(2)}, u32[]{:S(2)}) collective-permute-start(f32[1536,128]{1,0:T(8,128)S(1)} %pad_maximum_fusion.x_ref), channel_id=1, source_target_pairs={{0,8},{1,33},{2,10},{3,35},{4,12},{5,37},{6,14},{7,39},{8,0},{9,41... | collective-permute-start | bytes 2359304 | tf_op jit(solution)/shard_map/ppermute | solution.py:48
  192.4 10.3 %collective-permute-start.30 = (f32[64,256]{1,0:T(8,128)S(1)}, f32[64,256]{1,0:T(8,128)S(1)}, u32[]{:S(2)}, u32[]{:S(2)}) collective-permute-start(f32[64,256]{1,0:T(8,128)S(1)} %slot_flow.7), channel_id=1, source_target_pairs={{0,3},{1,2},{2,1},{3,0},{4,7},{5,6},{6,5},{7,4},{8,11},{9,10},{10,... | collective-permute-start | bytes 196616 | tf_op jit(solution)/shard_map/ppermute | solution.py:76
  212.7 12.8 %collective-permute-start.31 = (f32[1536,128]{1,0:T(8,128)S(1)}, f32[1536,128]{1,0:T(8,128)S(1)}, u32[]{:S(2)}, u32[]{:S(2)}) collective-permute-start(f32[1536,128]{1,0:T(8,128)S(1)} %get-tuple-element.43), channel_id=1, source_target_pairs={{0,8},{1,33},{2,10},{3,35},{4,12},{5,37},{6,14},{7,39},{8,0},{9,41... | collective-permute-start | bytes 2359304 | tf_op jit(solution)/shard_map/ppermute | solution.py:48
  213.4 20.5 %collective-permute-start.32 = (f32[1536,128]{1,0:T(8,128)S(1)}, f32[1536,128]{1,0:T(8,128)S(1)}, u32[]{:S(2)}, u32[]{:S(2)}) collective-permute-start(f32[1536,128]{1,0:T(8,128)S(1)} %get-tuple-element.44), channel_id=1, source_target_pairs={{0,4},{1,17},{2,6},{3,19},{4,8},{5,21},{6,10},{7,23},{8,12},{9,25}... | collective-permute-start | bytes 2359304 | tf_op jit(solution)/shard_map/ppermute | solution.py:48
  216.1 18.1 %collective-permute-start.33 = (f32[1536,128]{1,0:T(8,128)S(1)}, f32[1536,128]{1,0:T(8,128)S(1)}, u32[]{:S(2)}, u32[]{:S(2)}) collective-permute-start(f32[1536,128]{1,0:T(8,128)S(1)} %get-tuple-element.45), channel_id=1, source_target_pairs={{0,12},{1,49},{2,14},{3,51},{4,0},{5,53},{6,2},{7,55},{8,4},{9,57}... | collective-permute-start | bytes 2359304 | tf_op jit(solution)/shard_map/ppermute | solution.py:48
  234.4 6.4 %collective-permute-start.34 = (f32[384,128]{1,0:T(8,128)S(1)}, f32[384,128]{1,0:T(8,128)S(1)}, u32[]{:S(2)}, u32[]{:S(2)}) collective-permute-start(f32[384,128]{1,0:T(8,128)S(1)} %get-tuple-element.52), channel_id=1, source_target_pairs={{0,32},{1,9},{2,34},{3,11},{4,36},{5,13},{6,38},{7,15},{8,40},{9,1... | collective-permute-start | bytes 589832 | tf_op jit(solution)/shard_map/ppermute | solution.py:48
  234.5 8.1 %collective-permute-start.36 = (f32[384,128]{1,0:T(8,128)S(1)}, f32[384,128]{1,0:T(8,128)S(1)}, u32[]{:S(2)}, u32[]{:S(2)}) collective-permute-start(f32[384,128]{1,0:T(8,128)S(1)} %get-tuple-element.53), channel_id=1, source_target_pairs={{0,48},{1,13},{2,50},{3,15},{4,52},{5,1},{6,54},{7,3},{8,56},{9,5}... | collective-permute-start | bytes 589832 | tf_op jit(solution)/shard_map/ppermute | solution.py:48
  (15 other events, 162.0 us)

commit v3 on v2

--- a/solution.py
+++ b/solution.py
@@ -1,3 +1,5 @@
+import functools
+
 import jax
 import jax.numpy as jnp
 from jax import lax
@@ -126,54 +128,76 @@
 FIRST_STEP = 4
 
 
-def first_flow_kernel(idx_ref, load_acc_ref, slot_acc_ref, x_ref, columns_ref, *refs):
-    *w_refs, load_ref, slot_ref = refs
-
-    @pl.when(pl.program_id(0) == 0)
+def first_flow_kernel(steps, idx_ref, at_ref, load_acc_ref, slot_acc_ref, columns_ref, *refs):
+    *refs, load_ref, slot_ref = refs
+    w_refs, x_refs = refs[:FIRST_STEP], refs[FIRST_STEP:]
+    i = pl.program_id(0)
+
+    @pl.when(i == 0)
     def _():
         load_ref[...] = load_acc_ref[...]
         slot_ref[...] = slot_acc_ref[...]
 
-    load, slots = [], []
-    for u in range(0, FIRST_STEP, NZ):
-        base = u * BLOCK_ROWS
-        load += [x_ref[base + k * S : base + (k + 1) * S, :] for k in range(NZ * SUB // 128)]
-        base += NZ * LOAD_ROWS
-        slots += [x_ref[base + k * S : base + (k + 1) * S, :] for k in range(NZ * CAP)]
-    w = jnp.concatenate([ref[...] for ref in w_refs], axis=1)
-    columns = columns_ref[...].reshape(FIRST_STEP * SLOTS, LINES_DEV)
-    load_ref[...] -= three_pass(jnp.concatenate(load, axis=1), w, NT)
-    slot_ref[...] += three_pass(jnp.concatenate(slots, axis=1), columns, NN)
-
-
-def first_flow(load_acc, slot_acc, x, columns, ptdf, block_of, start):
-    steps = x.shape[0] // (FIRST_STEP * BLOCK_ROWS)
-    at = start // FIRST_STEP
+    def add(x_ref):
+        load, slots = [], []
+        for u in range(0, FIRST_STEP, NZ):
+            base = u * BLOCK_ROWS
+            load += [x_ref[base + k * S : base + (k + 1) * S, :] for k in range(NZ * SUB // 128)]
+            base += NZ * LOAD_ROWS
+            slots += [x_ref[base + k * S : base + (k + 1) * S, :] for k in range(NZ * CAP)]
+        w = jnp.concatenate([ref[...] for ref in w_refs], axis=1)
+        columns = columns_ref[...].reshape(FIRST_STEP * SLOTS, LINES_DEV)
+        load_ref[...] -= three_pass(jnp.concatenate(load, axis=1), w, NT)
+        slot_ref[...] += three_pass(jnp.concatenate(slots, axis=1), columns, NN)
+
+    for k, x_ref in enumerate(x_refs):
+        pl.when(i // steps == k)(lambda x_ref=x_ref: add(x_ref))
+
+
+def first_flow(load_acc, slot_acc, xs, columns, ptdf, block_of, starts):
+    steps = xs[0].shape[0] // (FIRST_STEP * BLOCK_ROWS)
+    places = [start // FIRST_STEP + i for start in starts for i in range(steps)]
+    order = jnp.concatenate(
+        [block_of[start : start + steps * FIRST_STEP] for start in starts]
+    )
 
     def sub(u):
+        return pl.BlockSpec((LINES_DEV, SUB), lambda i, idx, at: (0, idx[i * FIRST_STEP + u]))
+
+    def piece(k):
         return pl.BlockSpec(
-            (LINES_DEV, SUB), lambda i, idx: (0, idx[start + i * FIRST_STEP + u])
+            (FIRST_STEP * BLOCK_ROWS, 128),
+            lambda i, idx, at: (jnp.clip(i - k * steps, 0, steps - 1), 0),
         )
 
+    whole = pl.BlockSpec((S, LINES_DEV), lambda i, idx, at: (0, 0))
     return pl.pallas_call(
-        first_flow_kernel,
+        functools.partial(first_flow_kernel, steps),
         grid_spec=pltpu.PrefetchScalarGridSpec(
-            num_scalar_prefetch=1,
-            grid=(steps,),
+            num_scalar_prefetch=2,
+            grid=(len(places),),
             in_specs=[
-                pl.BlockSpec((S, LINES_DEV), lambda i, idx: (0, 0)),
-                pl.BlockSpec((S, LINES_DEV), lambda i, idx: (0, 0)),
-                pl.BlockSpec((FIRST_STEP * BLOCK_ROWS, 128), lambda i, idx: (i, 0)),
-                pl.BlockSpec((FIRST_STEP, SLOTS, LINES_DEV), lambda i, idx: (at + i, 0, 0)),
+                whole,
+                whole,
+                pl.BlockSpec((FIRST_STEP, SLOTS, LINES_DEV), lambda i, idx, at: (at[i], 0, 0)),
             ]
-            + [sub(u) for u in range(FIRST_STEP)],
-            out_specs=[pl.BlockSpec((S, LINES_DEV), lambda i, idx: (0, 0))] * 2,
+            + [sub(u) for u in range(FIRST_STEP)]
+            + [piece(k) for k in range(len(xs))],
+            out_specs=[whole] * 2,
         ),
         out_shape=[jax.ShapeDtypeStruct((S, LINES_DEV), jnp.float32)] * 2,
         compiler_params=pltpu.CompilerParams(vmem_limit_bytes=VMEM),
-        cost_estimate=cost(3.0 * steps),
+        cost_estimate=cost(3.0 * len(places)),
         name="first_flow",
-    )(block_of, load_acc, slot_acc, x, columns, *([ptdf] * FIRST_STEP))
+    )(
+        order,
+        jnp.array(places, jnp.int32),
+        load_acc,
+        slot_acc,
+        columns,
+        *([ptdf] * FIRST_STEP),
+        *xs,
+    )
 
 
 SLOT_STEPS = 2
@@ -324,6 +348,7 @@
     load = demand[:, 0, :].reshape(S, SUB // 128, 128).transpose(1, 0, 2)
     load = gather_z(load.reshape(LOAD_ROWS, 128))
     codes = jnp.pad(got[:, S], ((0, 8 - CAP), (0, 0)))
+    codes, load = lax.optimization_barrier((codes, load))
     codes = lax.all_to_all(
         jnp.broadcast_to(codes, (N_BAND, 8, 128)), "band", split_axis=0, concat_axis=0, tiled=True
     )
@@ -350,9 +375,9 @@
     n = eight.shape[0] // 2
     two_near, two_far = moved(one[:n], "second", -1), moved(three[n:], "second", -3)
     load_part = slot_part = jnp.zeros((S, LINES_DEV), jnp.float32)
-    for x, at in ((eight, 0), (one, 8), (three, 24), (two_near, 16), (two_far, 20)):
+    for xs, starts in (((eight, one, three), (0, 8, 24)), ((two_near, two_far), (16, 20))):
         load_part, slot_part = first_flow(
-            load_part, slot_part, x, columns, ptdf, block_of, at
+            load_part, slot_part, xs, columns, ptdf, block_of, starts
         )
     flow = load_part + slot_part
 

time: 260 us -> 259 us (level)
  waiting for transfers between devices: 82.1 us -> 96.5 us
  starting transfers between devices: 71.3 us -> 63.9 us
  Pallas kernels: 76.9 us -> 71.2 us
    ppermute x32, waiting for transfers between devices: 75.6 us -> 83.8 us  [moved(): return lax.ppermute(a, ('band', 'bus'), pairs)]
    all_to_all x1, waiting for transfers between devices: 0.01 us -> 6.04 us  [on_device(): lax.all_to_all(jnp.broadcast_to(codes, (N_BAND, 8, 128)), 'band', split_a...]
    pallas_call x5 -> x2, Pallas kernels: 25.6 us -> 19.9 us  [first_flow(): pl.pallas_call(functools.partial(first_flow_kernel, steps), grid_spec=plt...]
    ppermute x32, starting transfers between devices: 41.2 us -> 36.7 us  [moved(): return lax.ppermute(a, ('band', 'bus'), pairs)]
    all_to_all x1, starting transfers between devices: 9 us -> 5.9 us  [on_device(): lax.all_to_all(jnp.broadcast_to(codes, (N_BAND, 8, 128)), 'band', split_a...]
    unnamed x25 -> x21, local copies, waits for them, and re-layouts: 3.84 us -> 5.52 us
  transfers between devices with their start and end apart: 40 -> 40, of which waited for: 22 -> 23; matrix products, arithmetic and copies ran while one was open for 4% -> 3% of each run, Pallas kernels for 22% -> 20%
where the time goes in v3:
time: 259 us; the launch traced here: 258 us
  waiting for transfers between devices  96.5 us (37%)
  Pallas kernels  71.2 us (27%)
  starting transfers between devices  63.9 us (25%)
  local copies, waits for them, and re-layouts  11.3 us (4%)
  blocking collectives  9.22 us (4%)
  other arithmetic  3.73 us (1%)
    ppermute x32, waiting for transfers between devices, moved(): return lax.ppermute(a, ('band', 'bus'), pairs)  83.8 us
    ppermute x32, starting transfers between devices, moved(): return lax.ppermute(a, ('band', 'bus'), pairs)  36.7 us
    pallas_call x1, Pallas kernels, pick(): pl.pallas_call(pick_kernel, grid=(N_BAND // PICK_STEP,), in_specs=[pl.Blo...  23.9 us
    pallas_call x2, Pallas kernels, first_flow(): pl.pallas_call(functools.partial(first_flow_kernel, steps), grid_spec=plt...  19.9 us
    pallas_call x4, Pallas kernels, slot_price(): pl.pallas_call(slot_price_kernel, grid=(n,), in_specs=[pl.BlockSpec((S, L...  18.2 us
    ppermute x6, starting transfers between devices, sum_bus(): lax.ppermute(a, 'bus', [(j, j ^ k) for j in range(N_BUS)])  16.6 us
    all_to_all x1, blocking collectives, on_device(): home = lax.all_to_all(home, 'bus', split_axis=0, concat_axis=0, tiled=True)  9.22 us
    pallas_call x4, Pallas kernels, slot_flow(): pl.pallas_call(slot_flow_kernel, grid=(SLOT_STEPS,), in_specs=[pl.BlockSp...  9.16 us
  transfers between devices with their start and end apart: 40, of which 23 were waited for; matrix products, arithmetic and copies ran while one was open for 3% of the time, Pallas kernels for 20%

profile of v3, /device:TPU:1, one launch (start us, length us, event | category | flops | bytes accessed | tf_op | source)
XLA Modules:
  0.0 258.3 jit_solution(15041401051498427209)
XLA Ops:
  4.1 4.7 %all-to-all-start = ((f32[4,72,128]{2,1,0:T(8,128)}), f32[4,72,128]{2,1,0:T(8,128)S(1)}, u32[]{:S(2)}, u32[]{:S(2)}) async-start(f32[4,72,128]{2,1,0:T(8,128)} %bitcast.70), calls=%async_computation | async-start | bytes 294912 | tf_op jit(solution)/shard_map/all_to_all | solution.py:344
  10.3 3.8 %collective-permute-start.1 = (f32[384,128]{1,0:T(8,128)S(1)}, f32[384,128]{1,0:T(8,128)S(1)}, u32[]{:S(2)}, u32[]{:S(2)}) collective-permute-start(f32[384,128]{1,0:T(8,128)S(1)} %bitcast.88), channel_id=1, source_target_pairs={{0,64},{1,65},{2,66},{3,67},{4,68},{5,69},{6,70},{7,71},{8,72},{9,... | collective-permute-start | bytes 589832 | tf_op jit(solution)/shard_map/ppermute | solution.py:50
  14.9 4.7 %collective-permute-done.1 = f32[384,128]{1,0:T(8,128)S(1)} collective-permute-done((f32[384,128]{1,0:T(8,128)S(1)}, f32[384,128]{1,0:T(8,128)S(1)}, u32[]{:S(2)}, u32[]{:S(2)}) %collective-permute-start.1) | collective-permute-done | bytes 196640 | tf_op jit(solution)/shard_map/ppermute | solution.py:50
  19.6 2.8 %collective-permute-start.2 = (f32[768,128]{1,0:T(8,128)S(1)}, f32[768,128]{1,0:T(8,128)}, u32[]{:S(2)}, u32[]{:S(2)}) collective-permute-start(f32[768,128]{1,0:T(8,128)S(1)} %pad_maximum_fusion.1), channel_id=1, source_target_pairs={{0,48},{1,13},{2,50},{3,15},{4,52},{5,1},{6,54},{7,3},{8,56},{9,5}... | collective-permute-start | bytes 1179656 | tf_op jit(solution)/shard_map/ppermute | solution.py:50
  22.4 2.6 %collective-permute-start = (f32[208,128]{1,0:T(8,128)S(1)}, f32[208,128]{1,0:T(8,128)S(1)}, u32[]{:S(2)}, u32[]{:S(2)}) collective-permute-start(f32[208,128]{1,0:T(8,128)S(1)} %pad_maximum_fusion.3), channel_id=1, source_target_pairs={{0,64},{1,65},{2,66},{3,67},{4,68},{5,69},{6,70},{7,71},{8,72},{9,... | collective-permute-start | bytes 319496 | tf_op jit(solution)/shard_map/ppermute | solution.py:50
  27.3 5.9 %all-to-all-start.1 = ((f32[32,8,128]{2,1,0:T(8,128)}), f32[32,8,128]{2,1,0:T(8,128)S(1)}, u32[]{:S(2)}, u32[]{:S(2)}) async-start(f32[32,8,128]{2,1,0:T(8,128)} %broadcast_in_dim.37), calls=%async_computation.1 | async-start | bytes 262144 | tf_op jit(solution)/shard_map/all_to_all | solution.py:352
  36.1 6.0 %all-to-all-done.1 = f32[32,8,128]{2,1,0:T(8,128)S(1)} async-done(((f32[32,8,128]{2,1,0:T(8,128)}), f32[32,8,128]{2,1,0:T(8,128)S(1)}, u32[]{:S(2)}, u32[]{:S(2)}) %all-to-all-start.1) | async-done | bytes 131104 | tf_op jit(solution)/shard_map/all_to_all | solution.py:352
  51.4 2.3 collective-permute-start.8
  53.7 23.9 %pick.1.columns_ref.w_ref = f32[32,384,256]{2,1,0:T(8,128)} custom-call(f32[384,32]{1,0:T(8,128)S(1)} %reshape.361.code_ref, f32[256,24576]{1,0:T(8,128)} %refs_3_.3), custom_call_target="tpu_custom_call" | custom-call | bytes 90000000 | tf_op jit(solution)/shard_map/pick/pallas_call | solution.py:285
  77.6 2.6 %collective-permute-done.9.refs_6_ = f32[4608,128]{1,0:T(8,128)S(1)} collective-permute-done((f32[4608,128]{1,0:T(8,128)S(1)}, f32[4608,128]{1,0:T(8,128)S(1)}, u32[]{:S(2)}, u32[]{:S(2)}) %collective-permute-start.9) | collective-permute-done | bytes 2359328 | tf_op jit(solution)/shard_map/ppermute | solution.py:50
  83.4 14.2 %first_flow.2 = (f32[64,256]{1,0:T(8,128)S(1)}, f32[64,256]{1,0:T(8,128)S(1)}) custom-call(s32[24]{0:T(128)S(1)} %pad_add_fusion.idx_ref, s32[6]{0:T(128)S(1)} %copy-done.1, f32[64,256]{1,0:T(8,128)S(1)} %broadcast_in_dim.36.load_acc_ref.slot_acc_ref, f32[64,256]{1,0:T(8,128)S(1)} %broadcast_in_dim.36.load_acc_ref.slot_acc_ref, ...), custom_call_target="tpu_custom_call" | custom-call | bytes 54000000 | tf_op jit(solution)/shard_map/first_flow/pallas_call | solution.py:174
  99.7 5.7 %first_flow.3 = (f32[64,256]{1,0:T(8,128)S(1)}, f32[64,256]{1,0:T(8,128)S(1)}) custom-call(s32[8]{0:T(128)S(1)} %get-tuple-element.61.idx_ref, s32[2]{0:T(128)S(1)} %copy-done, f32[64,256]{1,0:T(8,128)S(1)} %get-tuple-element.28.load_acc_ref, f32[64,256]{1,0:T(8,128)S(1)} %get-tuple-element.29.slot_acc_ref, f32[32,384,256]{2,1,0:T(8,128)} %pick.1.columns_ref.w_ref, ...), custom_call_target="tpu_custom_call" | custom-call | bytes 18000000 | tf_op jit(solution)/shard_map/first_flow/pallas_call | solution.py:174
  105.5 7.3 %collective-permute-start.14 = (f32[64,256]{1,0:T(8,128)S(1)}, f32[64,256]{1,0:T(8,128)S(1)}, u32[]{:S(2)}, u32[]{:S(2)}) collective-permute-start(f32[64,256]{1,0:T(8,128)S(1)} %add.386), channel_id=1, source_target_pairs={{0,3},{1,2},{2,1},{3,0},{4,7},{5,6},{6,5},{7,4},{8,11},{9,10},{10,... | collective-permute-start | bytes 196616 | tf_op jit(solution)/shard_map/ppermute | solution.py:78
  116.9 6.1 %slot_price.5 = (f32[1536,128]{1,0:T(8,128)S(1)}, f32[1536,128]{1,0:T(8,128)S(1)}, f32[1536,128]{1,0:T(8,128)S(1)}) custom-call(f32[64,256]{1,0:T(8,128)S(1)} %get-tuple-element.42.x_ref, f32[32,384,256]{2,1,0:T(8,128)} %pick.1.columns_ref.w_ref), custom_call_target="tpu_custom_call" | custom-call | bytes 18000000 | tf_op jit(solution)/shard_map/slot_price/pallas_call | solution.py:249
  126.9 3.0 %slot_price.4 = f32[1536,128]{1,0:T(8,128)S(1)} custom-call(f32[64,256]{1,0:T(8,128)S(1)} %get-tuple-element.42.x_ref, f32[32,384,256]{2,1,0:T(8,128)} %pick.1.columns_ref.w_ref), custom_call_target="tpu_custom_call" | custom-call | bytes 6000000 | tf_op jit(solution)/shard_map/slot_price/pallas_call | solution.py:249
  129.9 5.9 %collective-permute-done.15 = f32[1536,128]{1,0:T(8,128)S(1)} collective-permute-done((f32[1536,128]{1,0:T(8,128)S(1)}, f32[1536,128]{1,0:T(8,128)S(1)}, u32[]{:S(2)}, u32[]{:S(2)}) %collective-permute-start.15) | collective-permute-done | bytes 786464 | tf_op jit(solution)/shard_map/ppermute | solution.py:50
  135.8 8.4 %collective-permute-done.16 = f32[1536,128]{1,0:T(8,128)S(1)} collective-permute-done((f32[1536,128]{1,0:T(8,128)S(1)}, f32[1536,128]{1,0:T(8,128)S(1)}, u32[]{:S(2)}, u32[]{:S(2)}) %collective-permute-start.16) | collective-permute-done | bytes 786464 | tf_op jit(solution)/shard_map/ppermute | solution.py:50
  146.0 4.8 %collective-permute-done.18 = f32[384,128]{1,0:T(8,128)S(1)} collective-permute-done((f32[384,128]{1,0:T(8,128)S(1)}, f32[384,128]{1,0:T(8,128)S(1)}, u32[]{:S(2)}, u32[]{:S(2)}) %collective-permute-start.18) | collective-permute-done | bytes 196640 | tf_op jit(solution)/shard_map/ppermute | solution.py:50
  154.0 4.7 %collective-permute-done.21 = f32[384,128]{1,0:T(8,128)S(1)} collective-permute-done((f32[384,128]{1,0:T(8,128)S(1)}, f32[384,128]{1,0:T(8,128)S(1)}, u32[]{:S(2)}, u32[]{:S(2)}) %collective-permute-start.21) | collective-permute-done | bytes 196640 | tf_op jit(solution)/shard_map/ppermute | solution.py:50
  161.6 5.2 %collective-permute-done.24 = f32[384,128]{1,0:T(8,128)S(1)} collective-permute-done((f32[384,128]{1,0:T(8,128)S(1)}, f32[384,128]{1,0:T(8,128)S(1)}, u32[]{:S(2)}, u32[]{:S(2)}) %collective-permute-start.24) | collective-permute-done | bytes 196640 | tf_op jit(solution)/shard_map/ppermute | solution.py:50
  172.7 8.3 %collective-permute-done.25.x_ref = f32[1536,128]{1,0:T(8,128)S(1)} collective-permute-done((f32[1536,128]{1,0:T(8,128)S(1)}, f32[1536,128]{1,0:T(8,128)S(1)}, u32[]{:S(2)}, u32[]{:S(2)}) %collective-permute-start.25) | collective-permute-done | bytes 786464 | tf_op jit(solution)/shard_map/ppermute | solution.py:50
  183.3 6.4 %collective-permute-done.26.x_ref = f32[1536,128]{1,0:T(8,128)S(1)} collective-permute-done((f32[1536,128]{1,0:T(8,128)S(1)}, f32[1536,128]{1,0:T(8,128)S(1)}, u32[]{:S(2)}, u32[]{:S(2)}) %collective-permute-start.26) | collective-permute-done | bytes 786464 | tf_op jit(solution)/shard_map/ppermute | solution.py:50
  192.1 2.3 slot_flow.7
  194.4 7.7 %collective-permute-start.30 = (f32[64,256]{1,0:T(8,128)S(1)}, f32[64,256]{1,0:T(8,128)S(1)}, u32[]{:S(2)}, u32[]{:S(2)}) collective-permute-start(f32[64,256]{1,0:T(8,128)S(1)} %slot_flow.7), channel_id=1, source_target_pairs={{0,3},{1,2},{2,1},{3,0},{4,7},{5,6},{6,5},{7,4},{8,11},{9,10},{10,... | collective-permute-start | bytes 196616 | tf_op jit(solution)/shard_map/ppermute | solution.py:78
  206.8 6.1 %slot_price.7 = (f32[1536,128]{1,0:T(8,128)S(1)}, f32[1536,128]{1,0:T(8,128)S(1)}, f32[1536,128]{1,0:T(8,128)S(1)}) custom-call(f32[64,256]{1,0:T(8,128)S(1)} %get-tuple-element.38.x_ref, f32[32,384,256]{2,1,0:T(8,128)} %pick.1.columns_ref.w_ref), custom_call_target="tpu_custom_call" | custom-call | bytes 18000000 | tf_op jit(solution)/shard_map/slot_price/pallas_call | solution.py:249
  213.0 2.5 collective-permute-start.32
  215.8 3.0 %slot_price.6 = f32[1536,128]{1,0:T(8,128)S(1)} custom-call(f32[64,256]{1,0:T(8,128)S(1)} %get-tuple-element.38.x_ref, f32[32,384,256]{2,1,0:T(8,128)} %pick.1.columns_ref.w_ref), custom_call_target="tpu_custom_call" | custom-call | bytes 6000000 | tf_op jit(solution)/shard_map/slot_price/pallas_call | solution.py:249
  218.8 6.9 %collective-permute-done.31 = f32[1536,128]{1,0:T(8,128)S(1)} collective-permute-done((f32[1536,128]{1,0:T(8,128)S(1)}, f32[1536,128]{1,0:T(8,128)S(1)}, u32[]{:S(2)}, u32[]{:S(2)}) %collective-permute-start.31) | collective-permute-done | bytes 786464 | tf_op jit(solution)/shard_map/ppermute | solution.py:50
  225.7 8.2 %collective-permute-done.32 = f32[1536,128]{1,0:T(8,128)S(1)} collective-permute-done((f32[1536,128]{1,0:T(8,128)S(1)}, f32[1536,128]{1,0:T(8,128)S(1)}, u32[]{:S(2)}, u32[]{:S(2)}) %collective-permute-start.32) | collective-permute-done | bytes 786464 | tf_op jit(solution)/shard_map/ppermute | solution.py:50
  235.7 4.8 %collective-permute-done.34 = f32[384,128]{1,0:T(8,128)S(1)} collective-permute-done((f32[384,128]{1,0:T(8,128)S(1)}, f32[384,128]{1,0:T(8,128)S(1)}, u32[]{:S(2)}, u32[]{:S(2)}) %collective-permute-start.34) | collective-permute-done | bytes 196640 | tf_op jit(solution)/shard_map/ppermute | solution.py:50
  243.6 4.1 %collective-permute-done.37 = f32[192,128]{1,0:T(8,128)S(1)} collective-permute-done((f32[192,128]{1,0:T(8,128)S(1)}, f32[192,128]{1,0:T(8,128)S(1)}, u32[]{:S(2)}, u32[]{:S(2)}) %collective-permute-start.37) | collective-permute-done | bytes 98336 | tf_op jit(solution)/shard_map/ppermute | solution.py:50
  248.1 9.2 %all_to_all.15 = f32[4,64,128]{2,1,0:T(8,128)S(1)} all-to-all(f32[4,64,128]{2,1,0:T(8,128)S(1)} %pad.14.clone), channel_id=1, replica_groups=mesh['band'=32,'bus'=4] {'bus'}, dimensions={0} | all-to-all | bytes 262144 | tf_op jit(solution)/shard_map/all_to_all | solution.py:412
  (146 shorter events, 63.1 us)
Async XLA Ops:
  4.1 10.0 %all-to-all-start = ((f32[4,72,128]{2,1,0:T(8,128)}), f32[4,72,128]{2,1,0:T(8,128)S(1)}, u32[]{:S(2)}, u32[]{:S(2)}) async-start(f32[4,72,128]{2,1,0:T(8,128)} %bitcast.70), calls=%async_computation | async-start | bytes 294912 | tf_op jit(solution)/shard_map/all_to_all | solution.py:344
  10.3 9.2 %collective-permute-start.1 = (f32[384,128]{1,0:T(8,128)S(1)}, f32[384,128]{1,0:T(8,128)S(1)}, u32[]{:S(2)}, u32[]{:S(2)}) collective-permute-start(f32[384,128]{1,0:T(8,128)S(1)} %bitcast.88), channel_id=1, source_target_pairs={{0,64},{1,65},{2,66},{3,67},{4,68},{5,69},{6,70},{7,71},{8,72},{9,... | collective-permute-start | bytes 589832 | tf_op jit(solution)/shard_map/ppermute | solution.py:50
  19.6 23.3 %collective-permute-start.2 = (f32[768,128]{1,0:T(8,128)S(1)}, f32[768,128]{1,0:T(8,128)}, u32[]{:S(2)}, u32[]{:S(2)}) collective-permute-start(f32[768,128]{1,0:T(8,128)S(1)} %pad_maximum_fusion.1), channel_id=1, source_target_pairs={{0,48},{1,13},{2,50},{3,15},{4,52},{5,1},{6,54},{7,3},{8,56},{9,5}... | collective-permute-start | bytes 1179656 | tf_op jit(solution)/shard_map/ppermute | solution.py:50
  22.4 10.8 %collective-permute-start = (f32[208,128]{1,0:T(8,128)S(1)}, f32[208,128]{1,0:T(8,128)S(1)}, u32[]{:S(2)}, u32[]{:S(2)}) collective-permute-start(f32[208,128]{1,0:T(8,128)S(1)} %pad_maximum_fusion.3), channel_id=1, source_target_pairs={{0,64},{1,65},{2,66},{3,67},{4,68},{5,69},{6,70},{7,71},{8,72},{9,... | collective-permute-start | bytes 319496 | tf_op jit(solution)/shard_map/ppermute | solution.py:50
  25.0 24.0 %collective-permute-start.6 = (f32[768,128]{1,0:T(8,128)S(1)}, f32[768,128]{1,0:T(8,128)}, u32[]{:S(2)}, u32[]{:S(2)}) collective-permute-start(f32[768,128]{1,0:T(8,128)S(1)} %pad_maximum_fusion.1), channel_id=1, source_target_pairs={{0,16},{1,5},{2,18},{3,7},{4,20},{5,9},{6,22},{7,11},{8,24},{9,13}... | collective-permute-start | bytes 1179656 | tf_op jit(solution)/shard_map/ppermute | solution.py:50
  25.0 20.9 %collective-permute-start.4 = (f32[768,128]{1,0:T(8,128)S(1)}, f32[768,128]{1,0:T(8,128)}, u32[]{:S(2)}, u32[]{:S(2)}) collective-permute-start(f32[768,128]{1,0:T(8,128)S(1)} %pad_maximum_fusion.1), channel_id=1, source_target_pairs={{0,32},{1,9},{2,34},{3,11},{4,36},{5,13},{6,38},{7,15},{8,40},{9,1... | collective-permute-start | bytes 1179656 | tf_op jit(solution)/shard_map/ppermute | solution.py:50
  27.3 14.8 %all-to-all-start.1 = ((f32[32,8,128]{2,1,0:T(8,128)}), f32[32,8,128]{2,1,0:T(8,128)S(1)}, u32[]{:S(2)}, u32[]{:S(2)}) async-start(f32[32,8,128]{2,1,0:T(8,128)} %broadcast_in_dim.37), calls=%async_computation.1 | async-start | bytes 262144 | tf_op jit(solution)/shard_map/all_to_all | solution.py:352
  33.3 16.7 %collective-permute-start.7 = (f32[384,128]{1,0:T(8,128)S(1)}, f32[384,128]{1,0:T(8,128)}, u32[]{:S(2)}, u32[]{:S(2)}) collective-permute-start(f32[384,128]{1,0:T(8,128)S(1)} %bitcast.78), channel_id=1, source_target_pairs={{0,16},{1,5},{2,18},{3,7},{4,20},{5,9},{6,22},{7,11},{8,24},{9,13}... | collective-permute-start | bytes 589832 | tf_op jit(solution)/shard_map/ppermute | solution.py:50
  34.6 10.4 %collective-permute-start.3 = (f32[384,128]{1,0:T(8,128)S(1)}, f32[384,128]{1,0:T(8,128)}, u32[]{:S(2)}, u32[]{:S(2)}) collective-permute-start(f32[384,128]{1,0:T(8,128)S(1)} %bitcast.79), channel_id=1, source_target_pairs={{0,48},{1,13},{2,50},{3,15},{4,52},{5,1},{6,54},{7,3},{8,56},{9,5}... | collective-permute-start | bytes 589832 | tf_op jit(solution)/shard_map/ppermute | solution.py:50
  51.0 29.3 %collective-permute-start.9 = (f32[4608,128]{1,0:T(8,128)S(1)}, f32[4608,128]{1,0:T(8,128)S(1)}, u32[]{:S(2)}, u32[]{:S(2)}) collective-permute-start(f32[4608,128]{1,0:T(8,128)S(1)} %constant_dynamic-update-slice_fusion.refs_4_), channel_id=1, source_target_pairs={{0,4},{1,17},{2,6},{3,19},{4,8},{5,21},{6,10},{7,23},{8,12},{9,25}... | collective-permute-start | bytes 7077896 | tf_op jit(solution)/shard_map/ppermute | solution.py:50
  51.4 28.8 %collective-permute-start.8 = (f32[4608,128]{1,0:T(8,128)S(1)}, f32[4608,128]{1,0:T(8,128)S(1)}, u32[]{:S(2)}, u32[]{:S(2)}) collective-permute-start(f32[4608,128]{1,0:T(8,128)S(1)} %constant_dynamic-update-slice_fusion.refs_4_), channel_id=1, source_target_pairs={{0,12},{1,49},{2,14},{3,51},{4,0},{5,53},{6,2},{7,55},{8,4},{9,57}... | collective-permute-start | bytes 7077896 | tf_op jit(solution)/shard_map/ppermute | solution.py:50
  81.6 15.9 %collective-permute-start.10 = (f32[2304,128]{1,0:T(8,128)S(1)}, f32[2304,128]{1,0:T(8,128)S(1)}, u32[]{:S(2)}, u32[]{:S(2)}) collective-permute-start(f32[2304,128]{1,0:T(8,128)S(1)} %slice.113), channel_id=1, source_target_pairs={{0,12},{1,49},{2,14},{3,51},{4,0},{5,53},{6,2},{7,55},{8,4},{9,57}... | collective-permute-start | bytes 3538952 | tf_op jit(solution)/shard_map/ppermute | solution.py:50
  83.2 16.6 %collective-permute-start.11 = (f32[2304,128]{1,0:T(8,128)S(1)}, f32[2304,128]{1,0:T(8,128)S(1)}, u32[]{:S(2)}, u32[]{:S(2)}) collective-permute-start(f32[2304,128]{1,0:T(8,128)S(1)} %slice.114), channel_id=1, source_target_pairs={{0,4},{1,17},{2,6},{3,19},{4,8},{5,21},{6,10},{7,23},{8,12},{9,25}... | collective-permute-start | bytes 3538952 | tf_op jit(solution)/shard_map/ppermute | solution.py:50
  105.5 10.0 %collective-permute-start.14 = (f32[64,256]{1,0:T(8,128)S(1)}, f32[64,256]{1,0:T(8,128)S(1)}, u32[]{:S(2)}, u32[]{:S(2)}) collective-permute-start(f32[64,256]{1,0:T(8,128)S(1)} %add.386), channel_id=1, source_target_pairs={{0,3},{1,2},{2,1},{3,0},{4,7},{5,6},{6,5},{7,4},{8,11},{9,10},{10,... | collective-permute-start | bytes 196616 | tf_op jit(solution)/shard_map/ppermute | solution.py:78
  123.0 12.8 %collective-permute-start.15 = (f32[1536,128]{1,0:T(8,128)S(1)}, f32[1536,128]{1,0:T(8,128)S(1)}, u32[]{:S(2)}, u32[]{:S(2)}) collective-permute-start(f32[1536,128]{1,0:T(8,128)S(1)} %get-tuple-element.32), channel_id=1, source_target_pairs={{0,8},{1,33},{2,10},{3,35},{4,12},{5,37},{6,14},{7,39},{8,0},{9,41... | collective-permute-start | bytes 2359304 | tf_op jit(solution)/shard_map/ppermute | solution.py:50
  124.3 19.9 %collective-permute-start.16 = (f32[1536,128]{1,0:T(8,128)S(1)}, f32[1536,128]{1,0:T(8,128)S(1)}, u32[]{:S(2)}, u32[]{:S(2)}) collective-permute-start(f32[1536,128]{1,0:T(8,128)S(1)} %get-tuple-element.33), channel_id=1, source_target_pairs={{0,4},{1,17},{2,6},{3,19},{4,8},{5,21},{6,10},{7,23},{8,12},{9,25}... | collective-permute-start | bytes 2359304 | tf_op jit(solution)/shard_map/ppermute | solution.py:50
  124.7 19.5 %collective-permute-start.17 = (f32[1536,128]{1,0:T(8,128)S(1)}, f32[1536,128]{1,0:T(8,128)S(1)}, u32[]{:S(2)}, u32[]{:S(2)}) collective-permute-start(f32[1536,128]{1,0:T(8,128)S(1)} %get-tuple-element.34), channel_id=1, source_target_pairs={{0,12},{1,49},{2,14},{3,51},{4,0},{5,53},{6,2},{7,55},{8,4},{9,57}... | collective-permute-start | bytes 2359304 | tf_op jit(solution)/shard_map/ppermute | solution.py:50
  144.4 6.4 %collective-permute-start.18 = (f32[384,128]{1,0:T(8,128)S(1)}, f32[384,128]{1,0:T(8,128)S(1)}, u32[]{:S(2)}, u32[]{:S(2)}) collective-permute-start(f32[384,128]{1,0:T(8,128)S(1)} %get-tuple-element.47), channel_id=1, source_target_pairs={{0,32},{1,9},{2,34},{3,11},{4,36},{5,13},{6,38},{7,15},{8,40},{9,1... | collective-permute-start | bytes 589832 | tf_op jit(solution)/shard_map/ppermute | solution.py:50
  145.1 7.5 %collective-permute-start.19 = (f32[384,128]{1,0:T(8,128)S(1)}, f32[384,128]{1,0:T(8,128)S(1)}, u32[]{:S(2)}, u32[]{:S(2)}) collective-permute-start(f32[384,128]{1,0:T(8,128)S(1)} %get-tuple-element.49), channel_id=1, source_target_pairs={{0,16},{1,5},{2,18},{3,7},{4,20},{5,9},{6,22},{7,11},{8,24},{9,13}... | collective-permute-start | bytes 589832 | tf_op jit(solution)/shard_map/ppermute | solution.py:50
  158.8 7.9 %collective-permute-start.24 = (f32[384,128]{1,0:T(8,128)S(1)}, f32[384,128]{1,0:T(8,128)S(1)}, u32[]{:S(2)}, u32[]{:S(2)}) collective-permute-start(f32[384,128]{1,0:T(8,128)S(1)} %get-tuple-element.40), channel_id=1, source_target_pairs={{0,16},{1,5},{2,18},{3,7},{4,20},{5,9},{6,22},{7,11},{8,24},{9,13}... | collective-permute-start | bytes 589832 | tf_op jit(solution)/shard_map/ppermute | solution.py:50
  158.9 7.8 %collective-permute-start.23 = (f32[384,128]{1,0:T(8,128)S(1)}, f32[384,128]{1,0:T(8,128)S(1)}, u32[]{:S(2)}, u32[]{:S(2)}) collective-permute-start(f32[384,128]{1,0:T(8,128)S(1)} %get-tuple-element.40), channel_id=1, source_target_pairs={{0,32},{1,9},{2,34},{3,11},{4,36},{5,13},{6,38},{7,15},{8,40},{9,1... | collective-permute-start | bytes 589832 | tf_op jit(solution)/shard_map/ppermute | solution.py:50
  160.7 7.0 %collective-permute-start.22 = (f32[384,128]{1,0:T(8,128)S(1)}, f32[384,128]{1,0:T(8,128)S(1)}, u32[]{:S(2)}, u32[]{:S(2)}) collective-permute-start(f32[384,128]{1,0:T(8,128)S(1)} %get-tuple-element.40), channel_id=1, source_target_pairs={{0,48},{1,13},{2,50},{3,15},{4,52},{5,1},{6,54},{7,3},{8,56},{9,5}... | collective-permute-start | bytes 589832 | tf_op jit(solution)/shard_map/ppermute | solution.py:50
  167.7 13.3 %collective-permute-start.25 = (f32[1536,128]{1,0:T(8,128)S(1)}, f32[1536,128]{1,0:T(8,128)S(1)}, u32[]{:S(2)}, u32[]{:S(2)}) collective-permute-start(f32[1536,128]{1,0:T(8,128)S(1)} %pad_maximum_fusion.x_ref), channel_id=1, source_target_pairs={{0,12},{1,49},{2,14},{3,51},{4,0},{5,53},{6,2},{7,55},{8,4},{9,57}... | collective-permute-start | bytes 2359304 | tf_op jit(solution)/shard_map/ppermute | solution.py:50
  169.0 20.8 %collective-permute-start.26 = (f32[1536,128]{1,0:T(8,128)S(1)}, f32[1536,128]{1,0:T(8,128)S(1)}, u32[]{:S(2)}, u32[]{:S(2)}) collective-permute-start(f32[1536,128]{1,0:T(8,128)S(1)} %pad_maximum_fusion.x_ref), channel_id=1, source_target_pairs={{0,4},{1,17},{2,6},{3,19},{4,8},{5,21},{6,10},{7,23},{8,12},{9,25}... | collective-permute-start | bytes 2359304 | tf_op jit(solution)/shard_map/ppermute | solution.py:50
  169.5 22.6 %collective-permute-start.27 = (f32[1536,128]{1,0:T(8,128)S(1)}, f32[1536,128]{1,0:T(8,128)S(1)}, u32[]{:S(2)}, u32[]{:S(2)}) collective-permute-start(f32[1536,128]{1,0:T(8,128)S(1)} %pad_maximum_fusion.x_ref), channel_id=1, source_target_pairs={{0,8},{1,33},{2,10},{3,35},{4,12},{5,37},{6,14},{7,39},{8,0},{9,41... | collective-permute-start | bytes 2359304 | tf_op jit(solution)/shard_map/ppermute | solution.py:50
  194.4 10.3 %collective-permute-start.30 = (f32[64,256]{1,0:T(8,128)S(1)}, f32[64,256]{1,0:T(8,128)S(1)}, u32[]{:S(2)}, u32[]{:S(2)}) collective-permute-start(f32[64,256]{1,0:T(8,128)S(1)} %slot_flow.7), channel_id=1, source_target_pairs={{0,3},{1,2},{2,1},{3,0},{4,7},{5,6},{6,5},{7,4},{8,11},{9,10},{10,... | collective-permute-start | bytes 196616 | tf_op jit(solution)/shard_map/ppermute | solution.py:78
  212.9 12.8 %collective-permute-start.31 = (f32[1536,128]{1,0:T(8,128)S(1)}, f32[1536,128]{1,0:T(8,128)S(1)}, u32[]{:S(2)}, u32[]{:S(2)}) collective-permute-start(f32[1536,128]{1,0:T(8,128)S(1)} %get-tuple-element.35), channel_id=1, source_target_pairs={{0,8},{1,33},{2,10},{3,35},{4,12},{5,37},{6,14},{7,39},{8,0},{9,41... | collective-permute-start | bytes 2359304 | tf_op jit(solution)/shard_map/ppermute | solution.py:50
  213.0 20.8 %collective-permute-start.32 = (f32[1536,128]{1,0:T(8,128)S(1)}, f32[1536,128]{1,0:T(8,128)S(1)}, u32[]{:S(2)}, u32[]{:S(2)}) collective-permute-start(f32[1536,128]{1,0:T(8,128)S(1)} %get-tuple-element.36), channel_id=1, source_target_pairs={{0,4},{1,17},{2,6},{3,19},{4,8},{5,21},{6,10},{7,23},{8,12},{9,25}... | collective-permute-start | bytes 2359304 | tf_op jit(solution)/shard_map/ppermute | solution.py:50
  215.5 18.4 %collective-permute-start.33 = (f32[1536,128]{1,0:T(8,128)S(1)}, f32[1536,128]{1,0:T(8,128)S(1)}, u32[]{:S(2)}, u32[]{:S(2)}) collective-permute-start(f32[1536,128]{1,0:T(8,128)S(1)} %get-tuple-element.37), channel_id=1, source_target_pairs={{0,12},{1,49},{2,14},{3,51},{4,0},{5,53},{6,2},{7,55},{8,4},{9,57}... | collective-permute-start | bytes 2359304 | tf_op jit(solution)/shard_map/ppermute | solution.py:50
  234.1 6.4 %collective-permute-start.34 = (f32[384,128]{1,0:T(8,128)S(1)}, f32[384,128]{1,0:T(8,128)S(1)}, u32[]{:S(2)}, u32[]{:S(2)}) collective-permute-start(f32[384,128]{1,0:T(8,128)S(1)} %get-tuple-element.44), channel_id=1, source_target_pairs={{0,32},{1,9},{2,34},{3,11},{4,36},{5,13},{6,38},{7,15},{8,40},{9,1... | collective-permute-start | bytes 589832 | tf_op jit(solution)/shard_map/ppermute | solution.py:50
  234.2 6.3 %collective-permute-start.36 = (f32[384,128]{1,0:T(8,128)S(1)}, f32[384,128]{1,0:T(8,128)S(1)}, u32[]{:S(2)}, u32[]{:S(2)}) collective-permute-start(f32[384,128]{1,0:T(8,128)S(1)} %get-tuple-element.45), channel_id=1, source_target_pairs={{0,48},{1,13},{2,50},{3,15},{4,52},{5,1},{6,54},{7,3},{8,56},{9,5}... | collective-permute-start | bytes 589832 | tf_op jit(solution)/shard_map/ppermute | solution.py:50
  234.2 8.3 %collective-permute-start.35 = (f32[384,128]{1,0:T(8,128)S(1)}, f32[384,128]{1,0:T(8,128)S(1)}, u32[]{:S(2)}, u32[]{:S(2)}) collective-permute-start(f32[384,128]{1,0:T(8,128)S(1)} %get-tuple-element.46), channel_id=1, source_target_pairs={{0,16},{1,5},{2,18},{3,7},{4,20},{5,9},{6,22},{7,11},{8,24},{9,13}... | collective-permute-start | bytes 589832 | tf_op jit(solution)/shard_map/ppermute | solution.py:50
  (13 other events, 92.8 us)

commit v4 on v3

--- a/solution.py
+++ b/solution.py
@@ -140,11 +140,11 @@
 
     def add(x_ref):
         load, slots = [], []
-        for u in range(0, FIRST_STEP, NZ):
+        for u in range(FIRST_STEP):
             base = u * BLOCK_ROWS
-            load += [x_ref[base + k * S : base + (k + 1) * S, :] for k in range(NZ * SUB // 128)]
-            base += NZ * LOAD_ROWS
-            slots += [x_ref[base + k * S : base + (k + 1) * S, :] for k in range(NZ * CAP)]
+            load += [x_ref[base + k * S : base + (k + 1) * S, :] for k in range(SUB // 128)]
+            base += LOAD_ROWS
+            slots += [x_ref[base + k * S : base + (k + 1) * S, :] for k in range(CAP)]
         w = jnp.concatenate([ref[...] for ref in w_refs], axis=1)
         columns = columns_ref[...].reshape(FIRST_STEP * SLOTS, LINES_DEV)
         load_ref[...] -= three_pass(jnp.concatenate(load, axis=1), w, NT)
@@ -341,33 +341,31 @@
     )
     rows = own.shape[0]
     message = exact_dot(own, where, NN).reshape(rows, N_BUS, 128).transpose(1, 0, 2)
-    message_got = lax.all_to_all(message, "bus", split_axis=0, concat_axis=0, tiled=True)
-    got = message_got
+    got = lax.all_to_all(message, "bus", split_axis=0, concat_axis=0, tiled=True)
     got = got[:, :, : CAP * N_BAND].reshape(N_BUS, rows, CAP, N_BAND)
     got = got.transpose(2, 1, 0, 3).reshape(CAP, rows, 128)
     load = demand[:, 0, :].reshape(S, SUB // 128, 128).transpose(1, 0, 2)
-    load = gather_z(load.reshape(LOAD_ROWS, 128))
+    params = got[:, S + 1 : S + 4].transpose(1, 0, 2).reshape(3 * CAP, 128)
+    both = gather_z(
+        jnp.concatenate(
+            [
+                load.reshape(LOAD_ROWS, 128),
+                got[:, :S].reshape(SLOT_ROWS, 128),
+                jnp.pad(params, ((0, 16 - 3 * CAP), (0, 0))),
+            ],
+            axis=0,
+        )
+    )
     codes = jnp.pad(got[:, S], ((0, 8 - CAP), (0, 0)))
-    codes, load = lax.optimization_barrier((codes, load))
     codes = lax.all_to_all(
         jnp.broadcast_to(codes, (N_BAND, 8, 128)), "band", split_axis=0, concat_axis=0, tiled=True
     )
     codes = codes[:, :CAP][block_of].reshape(SLOTS, N_BAND)
-    params = jnp.pad(
-        got[:, S + 1 : S + 4].transpose(1, 0, 2).reshape(3 * CAP, 128), ((0, 16 - 3 * CAP), (0, 0))
-    )
-    slots = gather_z(
-        jnp.concatenate([got[:, :S].reshape(SLOT_ROWS, 128), params], axis=0)
-    ).reshape(2, SLOT_ROWS + 16, 128)
-    params = slots[:, SLOT_ROWS : SLOT_ROWS + 3 * CAP].reshape(2, 3, CAP, 1, 128)
+    both = both.reshape(2, BLOCK_ROWS + 16, 128)
+    params = both[:, BLOCK_ROWS : BLOCK_ROWS + 3 * CAP].reshape(2, 3, CAP, 1, 128)
     lin, quad, top = (params[:, k] for k in range(3))
-    slots = slots[:, :SLOT_ROWS].reshape(2 * SLOT_ROWS, 128)
-    now = slots.reshape(2, CAP, S, 128)
-    load, _ = lax.optimization_barrier((load, message_got))
-    parts = []
-    for at in zip(ring_first(load), ring_first(slots)):
-        parts += at
-    eight = jnp.concatenate(parts, axis=0)
+    now = both[:, LOAD_ROWS:BLOCK_ROWS].reshape(2, CAP, S, 128)
+    eight = gather_first(both[:, :BLOCK_ROWS].reshape(2 * BLOCK_ROWS, 128))
     eight, codes = lax.optimization_barrier((eight, codes))
     columns = pick(codes, ptdf)
     one, three = moved(eight, "second", -1), moved(eight, "second", -3)

time: 259 us -> 257 us (level)
  local copies, waits for them, and re-layouts: 11.3 us -> 6.33 us
  waiting for transfers between devices: 96.5 us -> 101 us
    unnamed x21 -> x14, local copies, waits for them, and re-layouts: 5.52 us -> 1.44 us
    ppermute x32 -> x28, starting transfers between devices: 36.7 us -> 33 us  [moved(): return lax.ppermute(a, ('band', 'bus'), pairs)]
    all_to_all x1, waiting for transfers between devices: 6.04 us -> 9.54 us  [on_device(): lax.all_to_all(jnp.broadcast_to(codes, (N_BAND, 8, 128)), 'band', split_a...]
    ppermute x32 -> x28, waiting for transfers between devices: 83.8 us -> 82.8 us  [moved(): return lax.ppermute(a, ('band', 'bus'), pairs)]
  transfers between devices with their start and end apart: 40 -> 36, of which waited for: 23 -> 24; matrix products, arithmetic and copies ran while one was open for 3% -> 1% of each run, Pallas kernels for 20% -> 20%
where the time goes in v4:
time: 257 us
  waiting for transfers between devices  101 us (39%)
  Pallas kernels  71.2 us (28%)
  starting transfers between devices  62.5 us (24%)
  blocking collectives  9.23 us (4%)
  local copies, waits for them, and re-layouts  6.33 us (2%)
  other arithmetic  3.9 us (2%)
    ppermute x28, waiting for transfers between devices, moved(): return lax.ppermute(a, ('band', 'bus'), pairs)  82.8 us
    ppermute x28, starting transfers between devices, moved(): return lax.ppermute(a, ('band', 'bus'), pairs)  33 us
    pallas_call x1, Pallas kernels, pick(): pl.pallas_call(pick_kernel, grid=(N_BAND // PICK_STEP,), in_specs=[pl.Blo...  23.9 us
    pallas_call x2, Pallas kernels, first_flow(): pl.pallas_call(functools.partial(first_flow_kernel, steps), grid_spec=plt...  19.9 us
    pallas_call x4, Pallas kernels, slot_price(): pl.pallas_call(slot_price_kernel, grid=(n,), in_specs=[pl.BlockSpec((S, L...  18.2 us
    ppermute x6, starting transfers between devices, sum_bus(): lax.ppermute(a, 'bus', [(j, j ^ k) for j in range(N_BUS)])  17.9 us
    all_to_all x1, waiting for transfers between devices, on_device(): lax.all_to_all(jnp.broadcast_to(codes, (N_BAND, 8, 128)), 'band', split_a...  9.54 us
    all_to_all x1, blocking collectives, on_device(): home = lax.all_to_all(home, 'bus', split_axis=0, concat_axis=0, tiled=True)  9.23 us
  transfers between devices with their start and end apart: 36, of which 24 were waited for; matrix products, arithmetic and copies ran while one was open for 1% of the time, Pallas kernels for 20%

profile of v4, /device:TPU:1, one launch (start us, length us, event | category | flops | bytes accessed | tf_op | source)
XLA Modules:
  0.0 256.7 jit_solution(14810017119238395715)
XLA Ops:
  4.1 4.7 %all-to-all-start = ((f32[4,72,128]{2,1,0:T(8,128)}), f32[4,72,128]{2,1,0:T(8,128)S(1)}, u32[]{:S(2)}, u32[]{:S(2)}) async-start(f32[4,72,128]{2,1,0:T(8,128)} %bitcast.71), calls=%async_computation | async-start | bytes 294912 | tf_op jit(solution)/shard_map/all_to_all | solution.py:344
  13.1 3.8 %collective-permute-start = (f32[592,128]{1,0:T(8,128)S(1)}, f32[592,128]{1,0:T(8,128)S(1)}, u32[]{:S(2)}, u32[]{:S(2)}) collective-permute-start(f32[592,128]{1,0:T(8,128)S(1)} %pad_maximum_fusion.3), channel_id=1, source_target_pairs={{0,64},{1,65},{2,66},{3,67},{4,68},{5,69},{6,70},{7,71},{8,72},{9,... | collective-permute-start | bytes 909320 | tf_op jit(solution)/shard_map/ppermute | solution.py:50
  16.9 6.4 %collective-permute-done = f32[592,128]{1,0:T(8,128)S(1)} collective-permute-done((f32[592,128]{1,0:T(8,128)S(1)}, f32[592,128]{1,0:T(8,128)S(1)}, u32[]{:S(2)}, u32[]{:S(2)}) %collective-permute-start) | collective-permute-done | bytes 303136 | tf_op jit(solution)/shard_map/ppermute | solution.py:50
  24.8 2.6 %collective-permute-start.2 = (f32[1152,128]{1,0:T(8,128)S(1)}, f32[1152,128]{1,0:T(8,128)S(1)}, u32[]{:S(2)}, u32[]{:S(2)}) collective-permute-start(f32[1152,128]{1,0:T(8,128)S(1)} %bitcast.83), channel_id=1, source_target_pairs={{0,32},{1,9},{2,34},{3,11},{4,36},{5,13},{6,38},{7,15},{8,40},{9,1... | collective-permute-start | bytes 1769480 | tf_op jit(solution)/shard_map/ppermute | solution.py:50
  29.4 6.9 %all-to-all-start.1 = ((f32[32,8,128]{2,1,0:T(8,128)}), f32[32,8,128]{2,1,0:T(8,128)S(1)}, u32[]{:S(2)}, u32[]{:S(2)}) async-start(f32[32,8,128]{2,1,0:T(8,128)} %broadcast_in_dim.37), calls=%async_computation.1 | async-start | bytes 262144 | tf_op jit(solution)/shard_map/all_to_all | solution.py:360
  36.3 9.5 %all-to-all-done.1 = f32[32,8,128]{2,1,0:T(8,128)S(1)} async-done(((f32[32,8,128]{2,1,0:T(8,128)}), f32[32,8,128]{2,1,0:T(8,128)S(1)}, u32[]{:S(2)}, u32[]{:S(2)}) %all-to-all-start.1) | async-done | bytes 131104 | tf_op jit(solution)/shard_map/all_to_all | solution.py:360
  47.1 2.4 collective-permute-start.4
  49.5 23.9 %pick.1.columns_ref.w_ref = f32[32,384,256]{2,1,0:T(8,128)} custom-call(f32[384,32]{1,0:T(8,128)S(1)} %reshape.367.code_ref, f32[256,24576]{1,0:T(8,128)} %refs_3_.3), custom_call_target="tpu_custom_call" | custom-call | bytes 90000000 | tf_op jit(solution)/shard_map/pick/pallas_call | solution.py:285
  73.4 2.6 %collective-permute-done.5.refs_6_ = f32[4608,128]{1,0:T(8,128)S(1)} collective-permute-done((f32[4608,128]{1,0:T(8,128)S(1)}, f32[4608,128]{1,0:T(8,128)S(1)}, u32[]{:S(2)}, u32[]{:S(2)}) %collective-permute-start.5) | collective-permute-done | bytes 2359328 | tf_op jit(solution)/shard_map/ppermute | solution.py:50
  79.2 14.2 %first_flow.2 = (f32[64,256]{1,0:T(8,128)S(1)}, f32[64,256]{1,0:T(8,128)S(1)}) custom-call(s32[24]{0:T(128)S(1)} %pad_add_fusion.idx_ref, s32[6]{0:T(128)S(1)} %copy-done.1, f32[64,256]{1,0:T(8,128)S(1)} %broadcast_in_dim.36.load_acc_ref.slot_acc_ref, f32[64,256]{1,0:T(8,128)S(1)} %broadcast_in_dim.36.load_acc_ref.slot_acc_ref, ...), custom_call_target="tpu_custom_call" | custom-call | bytes 54000000 | tf_op jit(solution)/shard_map/first_flow/pallas_call | solution.py:174
  95.5 5.7 %first_flow.3 = (f32[64,256]{1,0:T(8,128)S(1)}, f32[64,256]{1,0:T(8,128)S(1)}) custom-call(s32[8]{0:T(128)S(1)} %get-tuple-element.55.idx_ref, s32[2]{0:T(128)S(1)} %copy-done, f32[64,256]{1,0:T(8,128)S(1)} %get-tuple-element.22.load_acc_ref, f32[64,256]{1,0:T(8,128)S(1)} %get-tuple-element.23.slot_acc_ref, f32[32,384,256]{2,1,0:T(8,128)} %pick.1.columns_ref.w_ref, ...), custom_call_target="tpu_custom_call" | custom-call | bytes 18000000 | tf_op jit(solution)/shard_map/first_flow/pallas_call | solution.py:174
  101.3 6.4 %collective-permute-start.10 = (f32[64,256]{1,0:T(8,128)S(1)}, f32[64,256]{1,0:T(8,128)S(1)}, u32[]{:S(2)}, u32[]{:S(2)}) collective-permute-start(f32[64,256]{1,0:T(8,128)S(1)} %add.386), channel_id=1, source_target_pairs={{0,3},{1,2},{2,1},{3,0},{4,7},{5,6},{6,5},{7,4},{8,11},{9,10},{10,... | collective-permute-start | bytes 196616 | tf_op jit(solution)/shard_map/ppermute | solution.py:78
  109.7 2.8 %collective-permute-done.9 = f32[64,256]{1,0:T(8,128)S(1)} collective-permute-done((f32[64,256]{1,0:T(8,128)S(1)}, f32[64,256]{1,0:T(8,128)S(1)}, u32[]{:S(2)}, u32[]{:S(2)}) %collective-permute-start.9) | collective-permute-done | bytes 65568 | tf_op jit(solution)/shard_map/ppermute | solution.py:78
  112.5 6.1 %slot_price.5 = (f32[1536,128]{1,0:T(8,128)S(1)}, f32[1536,128]{1,0:T(8,128)S(1)}, f32[1536,128]{1,0:T(8,128)S(1)}) custom-call(f32[64,256]{1,0:T(8,128)S(1)} %get-tuple-element.36.x_ref, f32[32,384,256]{2,1,0:T(8,128)} %pick.1.columns_ref.w_ref), custom_call_target="tpu_custom_call" | custom-call | bytes 18000000 | tf_op jit(solution)/shard_map/slot_price/pallas_call | solution.py:249
  118.7 2.8 %collective-permute-start.11 = (f32[1536,128]{1,0:T(8,128)S(1)}, f32[1536,128]{1,0:T(8,128)S(1)}, u32[]{:S(2)}, u32[]{:S(2)}) collective-permute-start(f32[1536,128]{1,0:T(8,128)S(1)} %get-tuple-element.26), channel_id=1, source_target_pairs={{0,8},{1,33},{2,10},{3,35},{4,12},{5,37},{6,14},{7,39},{8,0},{9,41... | collective-permute-start | bytes 2359304 | tf_op jit(solution)/shard_map/ppermute | solution.py:50
  124.1 3.0 %slot_price.4 = f32[1536,128]{1,0:T(8,128)S(1)} custom-call(f32[64,256]{1,0:T(8,128)S(1)} %get-tuple-element.36.x_ref, f32[32,384,256]{2,1,0:T(8,128)} %pick.1.columns_ref.w_ref), custom_call_target="tpu_custom_call" | custom-call | bytes 6000000 | tf_op jit(solution)/shard_map/slot_price/pallas_call | solution.py:249
  127.1 4.3 %collective-permute-done.11 = f32[1536,128]{1,0:T(8,128)S(1)} collective-permute-done((f32[1536,128]{1,0:T(8,128)S(1)}, f32[1536,128]{1,0:T(8,128)S(1)}, u32[]{:S(2)}, u32[]{:S(2)}) %collective-permute-start.11) | collective-permute-done | bytes 786464 | tf_op jit(solution)/shard_map/ppermute | solution.py:50
  131.4 8.4 %collective-permute-done.12 = f32[1536,128]{1,0:T(8,128)S(1)} collective-permute-done((f32[1536,128]{1,0:T(8,128)S(1)}, f32[1536,128]{1,0:T(8,128)S(1)}, u32[]{:S(2)}, u32[]{:S(2)}) %collective-permute-start.12) | collective-permute-done | bytes 786464 | tf_op jit(solution)/shard_map/ppermute | solution.py:50
  141.7 4.7 %collective-permute-done.14 = f32[384,128]{1,0:T(8,128)S(1)} collective-permute-done((f32[384,128]{1,0:T(8,128)S(1)}, f32[384,128]{1,0:T(8,128)S(1)}, u32[]{:S(2)}, u32[]{:S(2)}) %collective-permute-start.14) | collective-permute-done | bytes 196640 | tf_op jit(solution)/shard_map/ppermute | solution.py:50
  148.8 5.6 %collective-permute-done.17 = f32[384,128]{1,0:T(8,128)S(1)} collective-permute-done((f32[384,128]{1,0:T(8,128)S(1)}, f32[384,128]{1,0:T(8,128)S(1)}, u32[]{:S(2)}, u32[]{:S(2)}) %collective-permute-start.17) | collective-permute-done | bytes 196640 | tf_op jit(solution)/shard_map/ppermute | solution.py:50
  157.2 5.2 %collective-permute-done.20 = f32[384,128]{1,0:T(8,128)S(1)} collective-permute-done((f32[384,128]{1,0:T(8,128)S(1)}, f32[384,128]{1,0:T(8,128)S(1)}, u32[]{:S(2)}, u32[]{:S(2)}) %collective-permute-start.20) | collective-permute-done | bytes 196640 | tf_op jit(solution)/shard_map/ppermute | solution.py:50
  163.1 2.9 %collective-permute-start.21 = (f32[1536,128]{1,0:T(8,128)S(1)}, f32[1536,128]{1,0:T(8,128)S(1)}, u32[]{:S(2)}, u32[]{:S(2)}) collective-permute-start(f32[1536,128]{1,0:T(8,128)S(1)} %pad_maximum_fusion.1.x_ref), channel_id=1, source_target_pairs={{0,12},{1,49},{2,14},{3,51},{4,0},{5,53},{6,2},{7,55},{8,4},{9,57}... | collective-permute-start | bytes 2359304 | tf_op jit(solution)/shard_map/ppermute | solution.py:50
  169.9 8.4 %collective-permute-done.21.x_ref = f32[1536,128]{1,0:T(8,128)S(1)} collective-permute-done((f32[1536,128]{1,0:T(8,128)S(1)}, f32[1536,128]{1,0:T(8,128)S(1)}, u32[]{:S(2)}, u32[]{:S(2)}) %collective-permute-start.21) | collective-permute-done | bytes 786464 | tf_op jit(solution)/shard_map/ppermute | solution.py:50
  180.6 6.2 %collective-permute-done.22.x_ref = f32[1536,128]{1,0:T(8,128)S(1)} collective-permute-done((f32[1536,128]{1,0:T(8,128)S(1)}, f32[1536,128]{1,0:T(8,128)S(1)}, u32[]{:S(2)}, u32[]{:S(2)}) %collective-permute-start.22) | collective-permute-done | bytes 786464 | tf_op jit(solution)/shard_map/ppermute | solution.py:50
  191.4 9.1 %collective-permute-start.26 = (f32[64,256]{1,0:T(8,128)S(1)}, f32[64,256]{1,0:T(8,128)S(1)}, u32[]{:S(2)}, u32[]{:S(2)}) collective-permute-start(f32[64,256]{1,0:T(8,128)S(1)} %slot_flow.7), channel_id=1, source_target_pairs={{0,3},{1,2},{2,1},{3,0},{4,7},{5,6},{6,5},{7,4},{8,11},{9,10},{10,... | collective-permute-start | bytes 196616 | tf_op jit(solution)/shard_map/ppermute | solution.py:78
  205.3 6.1 %slot_price.7 = (f32[1536,128]{1,0:T(8,128)S(1)}, f32[1536,128]{1,0:T(8,128)S(1)}, f32[1536,128]{1,0:T(8,128)S(1)}) custom-call(f32[64,256]{1,0:T(8,128)S(1)} %get-tuple-element.32.x_ref, f32[32,384,256]{2,1,0:T(8,128)} %pick.1.columns_ref.w_ref), custom_call_target="tpu_custom_call" | custom-call | bytes 18000000 | tf_op jit(solution)/shard_map/slot_price/pallas_call | solution.py:249
  214.2 3.0 %slot_price.6 = f32[1536,128]{1,0:T(8,128)S(1)} custom-call(f32[64,256]{1,0:T(8,128)S(1)} %get-tuple-element.32.x_ref, f32[32,384,256]{2,1,0:T(8,128)} %pick.1.columns_ref.w_ref), custom_call_target="tpu_custom_call" | custom-call | bytes 6000000 | tf_op jit(solution)/shard_map/slot_price/pallas_call | solution.py:249
  217.2 6.9 %collective-permute-done.27 = f32[1536,128]{1,0:T(8,128)S(1)} collective-permute-done((f32[1536,128]{1,0:T(8,128)S(1)}, f32[1536,128]{1,0:T(8,128)S(1)}, u32[]{:S(2)}, u32[]{:S(2)}) %collective-permute-start.27) | collective-permute-done | bytes 786464 | tf_op jit(solution)/shard_map/ppermute | solution.py:50
  224.1 8.2 %collective-permute-done.28 = f32[1536,128]{1,0:T(8,128)S(1)} collective-permute-done((f32[1536,128]{1,0:T(8,128)S(1)}, f32[1536,128]{1,0:T(8,128)S(1)}, u32[]{:S(2)}, u32[]{:S(2)}) %collective-permute-start.28) | collective-permute-done | bytes 786464 | tf_op jit(solution)/shard_map/ppermute | solution.py:50
  234.1 4.8 %collective-permute-done.30 = f32[384,128]{1,0:T(8,128)S(1)} collective-permute-done((f32[384,128]{1,0:T(8,128)S(1)}, f32[384,128]{1,0:T(8,128)S(1)}, u32[]{:S(2)}, u32[]{:S(2)}) %collective-permute-start.30) | collective-permute-done | bytes 196640 | tf_op jit(solution)/shard_map/ppermute | solution.py:50
  241.8 4.4 %collective-permute-done.33 = f32[192,128]{1,0:T(8,128)S(1)} collective-permute-done((f32[192,128]{1,0:T(8,128)S(1)}, f32[192,128]{1,0:T(8,128)S(1)}, u32[]{:S(2)}, u32[]{:S(2)}) %collective-permute-start.33) | collective-permute-done | bytes 98336 | tf_op jit(solution)/shard_map/ppermute | solution.py:50
  246.5 9.2 %all_to_all.15 = f32[4,64,128]{2,1,0:T(8,128)S(1)} all-to-all(f32[4,64,128]{2,1,0:T(8,128)S(1)} %pad.14.clone), channel_id=1, replica_groups=mesh['band'=32,'bus'=4] {'bus'}, dimensions={0} | all-to-all | bytes 262144 | tf_op jit(solution)/shard_map/all_to_all | solution.py:410
  (131 shorter events, 54.3 us)
Async XLA Ops:
  4.1 8.5 %all-to-all-start = ((f32[4,72,128]{2,1,0:T(8,128)}), f32[4,72,128]{2,1,0:T(8,128)S(1)}, u32[]{:S(2)}, u32[]{:S(2)}) async-start(f32[4,72,128]{2,1,0:T(8,128)} %bitcast.71), calls=%async_computation | async-start | bytes 294912 | tf_op jit(solution)/shard_map/all_to_all | solution.py:344
  13.1 10.2 %collective-permute-start = (f32[592,128]{1,0:T(8,128)S(1)}, f32[592,128]{1,0:T(8,128)S(1)}, u32[]{:S(2)}, u32[]{:S(2)}) collective-permute-start(f32[592,128]{1,0:T(8,128)S(1)} %pad_maximum_fusion.3), channel_id=1, source_target_pairs={{0,64},{1,65},{2,66},{3,67},{4,68},{5,69},{6,70},{7,71},{8,72},{9,... | collective-permute-start | bytes 909320 | tf_op jit(solution)/shard_map/ppermute | solution.py:50
  23.4 23.2 %collective-permute-start.3 = (f32[1152,128]{1,0:T(8,128)S(1)}, f32[1152,128]{1,0:T(8,128)S(1)}, u32[]{:S(2)}, u32[]{:S(2)}) collective-permute-start(f32[1152,128]{1,0:T(8,128)S(1)} %bitcast.82), channel_id=1, source_target_pairs={{0,16},{1,5},{2,18},{3,7},{4,20},{5,9},{6,22},{7,11},{8,24},{9,13}... | collective-permute-start | bytes 1769480 | tf_op jit(solution)/shard_map/ppermute | solution.py:50
  24.8 21.8 %collective-permute-start.2 = (f32[1152,128]{1,0:T(8,128)S(1)}, f32[1152,128]{1,0:T(8,128)S(1)}, u32[]{:S(2)}, u32[]{:S(2)}) collective-permute-start(f32[1152,128]{1,0:T(8,128)S(1)} %bitcast.83), channel_id=1, source_target_pairs={{0,32},{1,9},{2,34},{3,11},{4,36},{5,13},{6,38},{7,15},{8,40},{9,1... | collective-permute-start | bytes 1769480 | tf_op jit(solution)/shard_map/ppermute | solution.py:50
  27.4 19.2 %collective-permute-start.1 = (f32[1152,128]{1,0:T(8,128)S(1)}, f32[1152,128]{1,0:T(8,128)S(1)}, u32[]{:S(2)}, u32[]{:S(2)}) collective-permute-start(f32[1152,128]{1,0:T(8,128)S(1)} %bitcast.84), channel_id=1, source_target_pairs={{0,48},{1,13},{2,50},{3,15},{4,52},{5,1},{6,54},{7,3},{8,56},{9,5}... | collective-permute-start | bytes 1769480 | tf_op jit(solution)/shard_map/ppermute | solution.py:50
  29.4 16.5 %all-to-all-start.1 = ((f32[32,8,128]{2,1,0:T(8,128)}), f32[32,8,128]{2,1,0:T(8,128)S(1)}, u32[]{:S(2)}, u32[]{:S(2)}) async-start(f32[32,8,128]{2,1,0:T(8,128)} %broadcast_in_dim.37), calls=%async_computation.1 | async-start | bytes 262144 | tf_op jit(solution)/shard_map/all_to_all | solution.py:360
  46.8 29.3 %collective-permute-start.5 = (f32[4608,128]{1,0:T(8,128)S(1)}, f32[4608,128]{1,0:T(8,128)S(1)}, u32[]{:S(2)}, u32[]{:S(2)}) collective-permute-start(f32[4608,128]{1,0:T(8,128)S(1)} %pad_maximum_fusion.refs_4_), channel_id=1, source_target_pairs={{0,4},{1,17},{2,6},{3,19},{4,8},{5,21},{6,10},{7,23},{8,12},{9,25}... | collective-permute-start | bytes 7077896 | tf_op jit(solution)/shard_map/ppermute | solution.py:50
  47.1 28.9 %collective-permute-start.4 = (f32[4608,128]{1,0:T(8,128)S(1)}, f32[4608,128]{1,0:T(8,128)S(1)}, u32[]{:S(2)}, u32[]{:S(2)}) collective-permute-start(f32[4608,128]{1,0:T(8,128)S(1)} %pad_maximum_fusion.refs_4_), channel_id=1, source_target_pairs={{0,12},{1,49},{2,14},{3,51},{4,0},{5,53},{6,2},{7,55},{8,4},{9,57}... | collective-permute-start | bytes 7077896 | tf_op jit(solution)/shard_map/ppermute | solution.py:50
  77.4 16.0 %collective-permute-start.6 = (f32[2304,128]{1,0:T(8,128)S(1)}, f32[2304,128]{1,0:T(8,128)S(1)}, u32[]{:S(2)}, u32[]{:S(2)}) collective-permute-start(f32[2304,128]{1,0:T(8,128)S(1)} %slice.117), channel_id=1, source_target_pairs={{0,12},{1,49},{2,14},{3,51},{4,0},{5,53},{6,2},{7,55},{8,4},{9,57}... | collective-permute-start | bytes 3538952 | tf_op jit(solution)/shard_map/ppermute | solution.py:50
  79.0 16.6 %collective-permute-start.7 = (f32[2304,128]{1,0:T(8,128)S(1)}, f32[2304,128]{1,0:T(8,128)S(1)}, u32[]{:S(2)}, u32[]{:S(2)}) collective-permute-start(f32[2304,128]{1,0:T(8,128)S(1)} %slice.118), channel_id=1, source_target_pairs={{0,4},{1,17},{2,6},{3,19},{4,8},{5,21},{6,10},{7,23},{8,12},{9,25}... | collective-permute-start | bytes 3538952 | tf_op jit(solution)/shard_map/ppermute | solution.py:50
  101.3 8.4 %collective-permute-start.10 = (f32[64,256]{1,0:T(8,128)S(1)}, f32[64,256]{1,0:T(8,128)S(1)}, u32[]{:S(2)}, u32[]{:S(2)}) collective-permute-start(f32[64,256]{1,0:T(8,128)S(1)} %add.386), channel_id=1, source_target_pairs={{0,3},{1,2},{2,1},{3,0},{4,7},{5,6},{6,5},{7,4},{8,11},{9,10},{10,... | collective-permute-start | bytes 196616 | tf_op jit(solution)/shard_map/ppermute | solution.py:78
  118.7 12.8 %collective-permute-start.11 = (f32[1536,128]{1,0:T(8,128)S(1)}, f32[1536,128]{1,0:T(8,128)S(1)}, u32[]{:S(2)}, u32[]{:S(2)}) collective-permute-start(f32[1536,128]{1,0:T(8,128)S(1)} %get-tuple-element.26), channel_id=1, source_target_pairs={{0,8},{1,33},{2,10},{3,35},{4,12},{5,37},{6,14},{7,39},{8,0},{9,41... | collective-permute-start | bytes 2359304 | tf_op jit(solution)/shard_map/ppermute | solution.py:50
  121.4 18.4 %collective-permute-start.12 = (f32[1536,128]{1,0:T(8,128)S(1)}, f32[1536,128]{1,0:T(8,128)S(1)}, u32[]{:S(2)}, u32[]{:S(2)}) collective-permute-start(f32[1536,128]{1,0:T(8,128)S(1)} %get-tuple-element.27), channel_id=1, source_target_pairs={{0,4},{1,17},{2,6},{3,19},{4,8},{5,21},{6,10},{7,23},{8,12},{9,25}... | collective-permute-start | bytes 2359304 | tf_op jit(solution)/shard_map/ppermute | solution.py:50
  121.7 18.1 %collective-permute-start.13 = (f32[1536,128]{1,0:T(8,128)S(1)}, f32[1536,128]{1,0:T(8,128)S(1)}, u32[]{:S(2)}, u32[]{:S(2)}) collective-permute-start(f32[1536,128]{1,0:T(8,128)S(1)} %get-tuple-element.28), channel_id=1, source_target_pairs={{0,12},{1,49},{2,14},{3,51},{4,0},{5,53},{6,2},{7,55},{8,4},{9,57}... | collective-permute-start | bytes 2359304 | tf_op jit(solution)/shard_map/ppermute | solution.py:50
  140.1 6.4 %collective-permute-start.14 = (f32[384,128]{1,0:T(8,128)S(1)}, f32[384,128]{1,0:T(8,128)S(1)}, u32[]{:S(2)}, u32[]{:S(2)}) collective-permute-start(f32[384,128]{1,0:T(8,128)S(1)} %get-tuple-element.41), channel_id=1, source_target_pairs={{0,32},{1,9},{2,34},{3,11},{4,36},{5,13},{6,38},{7,15},{8,40},{9,1... | collective-permute-start | bytes 589832 | tf_op jit(solution)/shard_map/ppermute | solution.py:50
  140.2 6.3 %collective-permute-start.16 = (f32[384,128]{1,0:T(8,128)S(1)}, f32[384,128]{1,0:T(8,128)S(1)}, u32[]{:S(2)}, u32[]{:S(2)}) collective-permute-start(f32[384,128]{1,0:T(8,128)S(1)} %get-tuple-element.42), channel_id=1, source_target_pairs={{0,48},{1,13},{2,50},{3,15},{4,52},{5,1},{6,54},{7,3},{8,56},{9,5}... | collective-permute-start | bytes 589832 | tf_op jit(solution)/shard_map/ppermute | solution.py:50
  141.1 7.2 %collective-permute-start.15 = (f32[384,128]{1,0:T(8,128)S(1)}, f32[384,128]{1,0:T(8,128)S(1)}, u32[]{:S(2)}, u32[]{:S(2)}) collective-permute-start(f32[384,128]{1,0:T(8,128)S(1)} %get-tuple-element.43), channel_id=1, source_target_pairs={{0,16},{1,5},{2,18},{3,7},{4,20},{5,9},{6,22},{7,11},{8,24},{9,13}... | collective-permute-start | bytes 589832 | tf_op jit(solution)/shard_map/ppermute | solution.py:50
  148.3 6.1 %collective-permute-start.17 = (f32[384,128]{1,0:T(8,128)S(1)}, f32[384,128]{1,0:T(8,128)S(1)}, u32[]{:S(2)}, u32[]{:S(2)}) collective-permute-start(f32[384,128]{1,0:T(8,128)S(1)} %fusion.4), channel_id=1, source_target_pairs={{0,64},{1,65},{2,66},{3,67},{4,68},{5,69},{6,70},{7,71},{8,72},{9,... | collective-permute-start | bytes 589832 | tf_op jit(solution)/shard_map/ppermute | solution.py:50
  154.5 7.9 %collective-permute-start.20 = (f32[384,128]{1,0:T(8,128)S(1)}, f32[384,128]{1,0:T(8,128)S(1)}, u32[]{:S(2)}, u32[]{:S(2)}) collective-permute-start(f32[384,128]{1,0:T(8,128)S(1)} %get-tuple-element.34), channel_id=1, source_target_pairs={{0,16},{1,5},{2,18},{3,7},{4,20},{5,9},{6,22},{7,11},{8,24},{9,13}... | collective-permute-start | bytes 589832 | tf_op jit(solution)/shard_map/ppermute | solution.py:50
  154.6 7.8 %collective-permute-start.19 = (f32[384,128]{1,0:T(8,128)S(1)}, f32[384,128]{1,0:T(8,128)S(1)}, u32[]{:S(2)}, u32[]{:S(2)}) collective-permute-start(f32[384,128]{1,0:T(8,128)S(1)} %get-tuple-element.34), channel_id=1, source_target_pairs={{0,32},{1,9},{2,34},{3,11},{4,36},{5,13},{6,38},{7,15},{8,40},{9,1... | collective-permute-start | bytes 589832 | tf_op jit(solution)/shard_map/ppermute | solution.py:50
  156.3 6.7 %collective-permute-start.18 = (f32[384,128]{1,0:T(8,128)S(1)}, f32[384,128]{1,0:T(8,128)S(1)}, u32[]{:S(2)}, u32[]{:S(2)}) collective-permute-start(f32[384,128]{1,0:T(8,128)S(1)} %get-tuple-element.34), channel_id=1, source_target_pairs={{0,48},{1,13},{2,50},{3,15},{4,52},{5,1},{6,54},{7,3},{8,56},{9,5}... | collective-permute-start | bytes 589832 | tf_op jit(solution)/shard_map/ppermute | solution.py:50
  163.1 15.2 %collective-permute-start.21 = (f32[1536,128]{1,0:T(8,128)S(1)}, f32[1536,128]{1,0:T(8,128)S(1)}, u32[]{:S(2)}, u32[]{:S(2)}) collective-permute-start(f32[1536,128]{1,0:T(8,128)S(1)} %pad_maximum_fusion.1.x_ref), channel_id=1, source_target_pairs={{0,12},{1,49},{2,14},{3,51},{4,0},{5,53},{6,2},{7,55},{8,4},{9,57}... | collective-permute-start | bytes 2359304 | tf_op jit(solution)/shard_map/ppermute | solution.py:50
  166.0 20.8 %collective-permute-start.22 = (f32[1536,128]{1,0:T(8,128)S(1)}, f32[1536,128]{1,0:T(8,128)S(1)}, u32[]{:S(2)}, u32[]{:S(2)}) collective-permute-start(f32[1536,128]{1,0:T(8,128)S(1)} %pad_maximum_fusion.1.x_ref), channel_id=1, source_target_pairs={{0,4},{1,17},{2,6},{3,19},{4,8},{5,21},{6,10},{7,23},{8,12},{9,25}... | collective-permute-start | bytes 2359304 | tf_op jit(solution)/shard_map/ppermute | solution.py:50
  166.0 23.1 %collective-permute-start.23 = (f32[1536,128]{1,0:T(8,128)S(1)}, f32[1536,128]{1,0:T(8,128)S(1)}, u32[]{:S(2)}, u32[]{:S(2)}) collective-permute-start(f32[1536,128]{1,0:T(8,128)S(1)} %pad_maximum_fusion.1.x_ref), channel_id=1, source_target_pairs={{0,8},{1,33},{2,10},{3,35},{4,12},{5,37},{6,14},{7,39},{8,0},{9,41... | collective-permute-start | bytes 2359304 | tf_op jit(solution)/shard_map/ppermute | solution.py:50
  191.4 11.5 %collective-permute-start.26 = (f32[64,256]{1,0:T(8,128)S(1)}, f32[64,256]{1,0:T(8,128)S(1)}, u32[]{:S(2)}, u32[]{:S(2)}) collective-permute-start(f32[64,256]{1,0:T(8,128)S(1)} %slot_flow.7), channel_id=1, source_target_pairs={{0,3},{1,2},{2,1},{3,0},{4,7},{5,6},{6,5},{7,4},{8,11},{9,10},{10,... | collective-permute-start | bytes 196616 | tf_op jit(solution)/shard_map/ppermute | solution.py:78
  211.4 12.8 %collective-permute-start.27 = (f32[1536,128]{1,0:T(8,128)S(1)}, f32[1536,128]{1,0:T(8,128)S(1)}, u32[]{:S(2)}, u32[]{:S(2)}) collective-permute-start(f32[1536,128]{1,0:T(8,128)S(1)} %get-tuple-element.29), channel_id=1, source_target_pairs={{0,8},{1,33},{2,10},{3,35},{4,12},{5,37},{6,14},{7,39},{8,0},{9,41... | collective-permute-start | bytes 2359304 | tf_op jit(solution)/shard_map/ppermute | solution.py:50
  211.5 20.8 %collective-permute-start.28 = (f32[1536,128]{1,0:T(8,128)S(1)}, f32[1536,128]{1,0:T(8,128)S(1)}, u32[]{:S(2)}, u32[]{:S(2)}) collective-permute-start(f32[1536,128]{1,0:T(8,128)S(1)} %get-tuple-element.30), channel_id=1, source_target_pairs={{0,4},{1,17},{2,6},{3,19},{4,8},{5,21},{6,10},{7,23},{8,12},{9,25}... | collective-permute-start | bytes 2359304 | tf_op jit(solution)/shard_map/ppermute | solution.py:50
  212.4 19.9 %collective-permute-start.29 = (f32[1536,128]{1,0:T(8,128)S(1)}, f32[1536,128]{1,0:T(8,128)S(1)}, u32[]{:S(2)}, u32[]{:S(2)}) collective-permute-start(f32[1536,128]{1,0:T(8,128)S(1)} %get-tuple-element.31), channel_id=1, source_target_pairs={{0,12},{1,49},{2,14},{3,51},{4,0},{5,53},{6,2},{7,55},{8,4},{9,57}... | collective-permute-start | bytes 2359304 | tf_op jit(solution)/shard_map/ppermute | solution.py:50
  232.5 6.4 %collective-permute-start.30 = (f32[384,128]{1,0:T(8,128)S(1)}, f32[384,128]{1,0:T(8,128)S(1)}, u32[]{:S(2)}, u32[]{:S(2)}) collective-permute-start(f32[384,128]{1,0:T(8,128)S(1)} %get-tuple-element.38), channel_id=1, source_target_pairs={{0,32},{1,9},{2,34},{3,11},{4,36},{5,13},{6,38},{7,15},{8,40},{9,1... | collective-permute-start | bytes 589832 | tf_op jit(solution)/shard_map/ppermute | solution.py:50
  232.6 6.3 %collective-permute-start.32 = (f32[384,128]{1,0:T(8,128)S(1)}, f32[384,128]{1,0:T(8,128)S(1)}, u32[]{:S(2)}, u32[]{:S(2)}) collective-permute-start(f32[384,128]{1,0:T(8,128)S(1)} %get-tuple-element.39), channel_id=1, source_target_pairs={{0,48},{1,13},{2,50},{3,15},{4,52},{5,1},{6,54},{7,3},{8,56},{9,5}... | collective-permute-start | bytes 589832 | tf_op jit(solution)/shard_map/ppermute | solution.py:50
  232.7 8.3 %collective-permute-start.31 = (f32[384,128]{1,0:T(8,128)S(1)}, f32[384,128]{1,0:T(8,128)S(1)}, u32[]{:S(2)}, u32[]{:S(2)}) collective-permute-start(f32[384,128]{1,0:T(8,128)S(1)} %get-tuple-element.40), channel_id=1, source_target_pairs={{0,16},{1,5},{2,18},{3,7},{4,20},{5,9},{6,22},{7,11},{8,24},{9,13}... | collective-permute-start | bytes 589832 | tf_op jit(solution)/shard_map/ppermute | solution.py:50
  241.1 5.1 %collective-permute-start.33 = (f32[192,128]{1,0:T(8,128)S(1)}, f32[192,128]{1,0:T(8,128)S(1)}, u32[]{:S(2)}, u32[]{:S(2)}) collective-permute-start(f32[192,128]{1,0:T(8,128)S(1)} %slice.166), channel_id=1, source_target_pairs={{0,64},{1,65},{2,66},{3,67},{4,68},{5,69},{6,70},{7,71},{8,72},{9,... | collective-permute-start | bytes 294920 | tf_op jit(solution)/shard_map/ppermute | solution.py:50
  (9 other events, 69.6 us)

commit v5 on v4

--- a/solution.py
+++ b/solution.py
@@ -297,14 +297,20 @@
     )(codes, ptdf)
 
 
-def home_columns(bus_map):
+def exchange_bus(parts):
+    return [parts[0]] + [
+        lax.ppermute(parts[k], "bus", [(j, j ^ k) for j in range(N_BUS)]) for k in (1, 2, 3)
+    ]
+
+
+def home_columns(bus_map, place):
     owner = bus_map // SUB
     same = owner[:, None] == owner[None, :]
     earlier = lax.broadcasted_iota(jnp.int32, same.shape, 0) > lax.broadcasted_iota(
         jnp.int32, same.shape, 1
     )
     rank = jnp.sum((same & earlier).astype(jnp.int32), axis=1)
-    return owner // N_BAND * 128 + rank * N_BAND + owner % N_BAND, bus_map % SUB
+    return (owner // N_BAND ^ place) * 128 + rank * N_BAND + owner % N_BAND, bus_map % SUB
 
 
 def exact_dot(a, b, dims):
@@ -317,14 +323,15 @@
     dispatch0, cost_lin, cost_quad, gen_max, bus_map, demand, ptdf, line_price0, flow_max
 ):
     band = lax.axis_index("band")
-    core = lax.axis_index("bus") % 2
+    place = lax.axis_index("bus")
+    core = place % 2
     z, x, y = band // (NX * NY), band // NY % NX, band % NY
     rel = lax.iota(jnp.int32, N_BAND)
     r2, r1, rz = rel // 8, rel // 2 % 4, rel % 2
     dx, dy = jnp.where(core == 0, r1, r2), jnp.where(core == 0, r2, r1)
     block_of = band_index((z + rz) % NZ, (x + dx) % NX, (y + dy) % NY)
 
-    at, local = home_columns(bus_map)
+    at, local = home_columns(bus_map, place)
     where = (at[:, None] == lax.broadcasted_iota(jnp.int32, (1, N_BUS * 128), 1)).astype(
         jnp.float32
     )
@@ -340,8 +347,8 @@
         axis=0,
     )
     rows = own.shape[0]
-    message = exact_dot(own, where, NN).reshape(rows, N_BUS, 128).transpose(1, 0, 2)
-    got = lax.all_to_all(message, "bus", split_axis=0, concat_axis=0, tiled=True)
+    message = exact_dot(own, where, NN)
+    got = jnp.stack(exchange_bus([message[:, k * 128 : (k + 1) * 128] for k in range(N_BUS)]))
     got = got[:, :, : CAP * N_BAND].reshape(N_BUS, rows, CAP, N_BAND)
     got = got.transpose(2, 1, 0, 3).reshape(CAP, rows, 128)
     load = demand[:, 0, :].reshape(S, SUB // 128, 128).transpose(1, 0, 2)
@@ -361,6 +368,7 @@
         jnp.broadcast_to(codes, (N_BAND, 8, 128)), "band", split_axis=0, concat_axis=0, tiled=True
     )
     codes = codes[:, :CAP][block_of].reshape(SLOTS, N_BAND)
+    both, codes = lax.optimization_barrier((both, codes))
     both = both.reshape(2, BLOCK_ROWS + 16, 128)
     params = both[:, BLOCK_ROWS : BLOCK_ROWS + 3 * CAP].reshape(2, 3, CAP, 1, 128)
     lin, quad, top = (params[:, k] for k in range(3))
@@ -407,8 +415,8 @@
     home = slot_values.reshape(CAP, S, N_BUS, N_BAND).transpose(2, 1, 0, 3)
     home = home.reshape(N_BUS, S, CAP * N_BAND)
     home = jnp.pad(home, ((0, 0), (0, 0), (0, 128 - CAP * N_BAND)))
-    home = lax.all_to_all(home, "bus", split_axis=0, concat_axis=0, tiled=True)
-    dispatch = exact_dot(home.transpose(1, 0, 2).reshape(S, N_BUS * 128), where, NT)
+    home = jnp.concatenate(exchange_bus([home[k] for k in range(N_BUS)]), axis=1)
+    dispatch = exact_dot(home, where, NT)
     return dispatch, line_price
 
 

time: 257 us -> 256 us (level)
  waiting for transfers between devices: 101 us -> 113 us
  blocking collectives: 9.23 us -> 0 us
  starting transfers between devices: 62.5 us -> 59.3 us
    ppermute x28, waiting for transfers between devices: 82.8 us -> 92.7 us  [moved(): return lax.ppermute(a, ('band', 'bus'), pairs)]
    all_to_all x1 -> x0, blocking collectives: 9.23 us -> none  [on_device(): home = lax.all_to_all(home, 'bus', split_axis=0, concat_axis=0, tiled=True)]
    ppermute x0 -> x6, starting transfers between devices: none -> 8.65 us  [exchange_bus(): lax.ppermute(parts[k], 'bus', [(j, j ^ k) for j in range(N_BUS)])]
    all_to_all x1 -> x0, starting transfers between devices: 4.72 us -> none  [on_device(): lax.all_to_all(message, 'bus', split_axis=0, concat_axis=0, tiled=True)]
    ppermute x0 -> x6, waiting for transfers between devices: none -> 4.71 us  [exchange_bus(): lax.ppermute(parts[k], 'bus', [(j, j ^ k) for j in range(N_BUS)])]
    ppermute x28, starting transfers between devices: 33 us -> 28.4 us  [moved(): return lax.ppermute(a, ('band', 'bus'), pairs)]
    ppermute x6, starting transfers between devices: 17.9 us -> 15.2 us  [sum_bus(): lax.ppermute(a, 'bus', [(j, j ^ k) for j in range(N_BUS)])]
  transfers between devices with their start and end apart: 36 -> 41, of which waited for: 24 -> 26; matrix products, arithmetic and copies ran while one was open for 1% -> 1% of each run, Pallas kernels for 20% -> 20%
where the time goes in v5:
time: 256 us
  waiting for transfers between devices  113 us (44%)
  Pallas kernels  71.2 us (28%)
  starting transfers between devices  59.3 us (23%)
  local copies, waits for them, and re-layouts  5.61 us (2%)
  other arithmetic  3.92 us (2%)
    ppermute x28, waiting for transfers between devices, moved(): return lax.ppermute(a, ('band', 'bus'), pairs)  92.7 us
    ppermute x28, starting transfers between devices, moved(): return lax.ppermute(a, ('band', 'bus'), pairs)  28.4 us
    pallas_call x1, Pallas kernels, pick(): pl.pallas_call(pick_kernel, grid=(N_BAND // PICK_STEP,), in_specs=[pl.Blo...  23.9 us
    pallas_call x2, Pallas kernels, first_flow(): pl.pallas_call(functools.partial(first_flow_kernel, steps), grid_spec=plt...  19.9 us
    pallas_call x4, Pallas kernels, slot_price(): pl.pallas_call(slot_price_kernel, grid=(n,), in_specs=[pl.BlockSpec((S, L...  18.2 us
    ppermute x6, starting transfers between devices, sum_bus(): lax.ppermute(a, 'bus', [(j, j ^ k) for j in range(N_BUS)])  15.2 us
    pallas_call x4, Pallas kernels, slot_flow(): pl.pallas_call(slot_flow_kernel, grid=(SLOT_STEPS,), in_specs=[pl.BlockSp...  9.16 us
    all_to_all x1, waiting for transfers between devices, on_device(): lax.all_to_all(jnp.broadcast_to(codes, (N_BAND, 8, 128)), 'band', split_a...  8.9 us
  transfers between devices with their start and end apart: 41, of which 26 were waited for; matrix products, arithmetic and copies ran while one was open for 1% of the time, Pallas kernels for 20%

profile of v5, /device:TPU:1, one launch (start us, length us, event | category | flops | bytes accessed | tf_op | source)
XLA Modules:
  0.0 255.9 jit_solution(17880299968270534294)
XLA Ops:
  3.5 3.1 %collective-permute-start.2 = (f32[72,128]{1,0:T(8,128)S(1)}, f32[72,128]{1,0:T(8,128)S(1)}, u32[]{:S(2)}, u32[]{:S(2)}) collective-permute-start(f32[72,128]{1,0:T(8,128)S(1)} %get-tuple-element.55), channel_id=1, source_target_pairs={{0,3},{1,2},{2,1},{3,0},{4,7},{5,6},{6,5},{7,4},{8,11},{9,10},{10,... | collective-permute-start | bytes 110600 | tf_op jit(solution)/shard_map/ppermute | solution.py:302
  10.3 3.4 %collective-permute-start.3 = (f32[592,128]{1,0:T(8,128)S(1)}, f32[592,128]{1,0:T(8,128)S(1)}, u32[]{:S(2)}, u32[]{:S(2)}) collective-permute-start(f32[592,128]{1,0:T(8,128)S(1)} %pad_maximum_fusion.3), channel_id=1, source_target_pairs={{0,64},{1,65},{2,66},{3,67},{4,68},{5,69},{6,70},{7,71},{8,72},{9,... | collective-permute-start | bytes 909320 | tf_op jit(solution)/shard_map/ppermute | solution.py:50
  14.6 7.0 %all-to-all-start = ((f32[32,8,128]{2,1,0:T(8,128)}), f32[32,8,128]{2,1,0:T(8,128)S(1)}, u32[]{:S(2)}, u32[]{:S(2)}) async-start(f32[32,8,128]{2,1,0:T(8,128)} %broadcast_in_dim.36), calls=%async_computation | async-start | bytes 262144 | tf_op jit(solution)/shard_map/all_to_all | solution.py:367
  21.7 8.9 %all-to-all-done = f32[32,8,128]{2,1,0:T(8,128)S(1)} async-done(((f32[32,8,128]{2,1,0:T(8,128)}), f32[32,8,128]{2,1,0:T(8,128)S(1)}, u32[]{:S(2)}, u32[]{:S(2)}) %all-to-all-start) | async-done | bytes 131104 | tf_op jit(solution)/shard_map/all_to_all | solution.py:367
  34.6 13.5 %collective-permute-done.6 = f32[1152,128]{1,0:T(8,128)S(1)} collective-permute-done((f32[1152,128]{1,0:T(8,128)S(1)}, f32[1152,128]{1,0:T(8,128)S(1)}, u32[]{:S(2)}, u32[]{:S(2)}) %collective-permute-start.6) | collective-permute-done | bytes 589856 | tf_op jit(solution)/shard_map/ppermute | solution.py:50
  49.3 2.4 collective-permute-start.7
  51.6 23.9 %pick.1.columns_ref.w_ref = f32[32,384,256]{2,1,0:T(8,128)} custom-call(f32[384,32]{1,0:T(8,128)S(1)} %reshape.356.code_ref, f32[256,24576]{1,0:T(8,128)} %refs_3_.3), custom_call_target="tpu_custom_call" | custom-call | bytes 90000000 | tf_op jit(solution)/shard_map/pick/pallas_call | solution.py:285
  75.6 2.6 %collective-permute-done.8.refs_6_ = f32[4608,128]{1,0:T(8,128)S(1)} collective-permute-done((f32[4608,128]{1,0:T(8,128)S(1)}, f32[4608,128]{1,0:T(8,128)S(1)}, u32[]{:S(2)}, u32[]{:S(2)}) %collective-permute-start.8) | collective-permute-done | bytes 2359328 | tf_op jit(solution)/shard_map/ppermute | solution.py:50
  81.3 14.2 %first_flow.2 = (f32[64,256]{1,0:T(8,128)S(1)}, f32[64,256]{1,0:T(8,128)S(1)}) custom-call(s32[24]{0:T(128)S(1)} %pad_add_fusion.idx_ref, s32[6]{0:T(128)S(1)} %copy-done.1, f32[64,256]{1,0:T(8,128)S(1)} %broadcast_in_dim.37.load_acc_ref.slot_acc_ref, f32[64,256]{1,0:T(8,128)S(1)} %broadcast_in_dim.37.load_acc_ref.slot_acc_ref, ...), custom_call_target="tpu_custom_call" | custom-call | bytes 54000000 | tf_op jit(solution)/shard_map/first_flow/pallas_call | solution.py:174
  97.7 5.7 %first_flow.3 = (f32[64,256]{1,0:T(8,128)S(1)}, f32[64,256]{1,0:T(8,128)S(1)}) custom-call(s32[8]{0:T(128)S(1)} %get-tuple-element.67.idx_ref, s32[2]{0:T(128)S(1)} %copy-done, f32[64,256]{1,0:T(8,128)S(1)} %get-tuple-element.26.load_acc_ref, f32[64,256]{1,0:T(8,128)S(1)} %get-tuple-element.27.slot_acc_ref, f32[32,384,256]{2,1,0:T(8,128)} %pick.1.columns_ref.w_ref, ...), custom_call_target="tpu_custom_call" | custom-call | bytes 18000000 | tf_op jit(solution)/shard_map/first_flow/pallas_call | solution.py:174
  103.4 5.9 %collective-permute-start.13 = (f32[64,256]{1,0:T(8,128)S(1)}, f32[64,256]{1,0:T(8,128)S(1)}, u32[]{:S(2)}, u32[]{:S(2)}) collective-permute-start(f32[64,256]{1,0:T(8,128)S(1)} %add.386), channel_id=1, source_target_pairs={{0,3},{1,2},{2,1},{3,0},{4,7},{5,6},{6,5},{7,4},{8,11},{9,10},{10,... | collective-permute-start | bytes 196616 | tf_op jit(solution)/shard_map/ppermute | solution.py:78
  111.3 2.6 %collective-permute-done.12 = f32[64,256]{1,0:T(8,128)S(1)} collective-permute-done((f32[64,256]{1,0:T(8,128)S(1)}, f32[64,256]{1,0:T(8,128)S(1)}, u32[]{:S(2)}, u32[]{:S(2)}) %collective-permute-start.12) | collective-permute-done | bytes 65568 | tf_op jit(solution)/shard_map/ppermute | solution.py:78
  113.9 6.1 %slot_price.5 = (f32[1536,128]{1,0:T(8,128)S(1)}, f32[1536,128]{1,0:T(8,128)S(1)}, f32[1536,128]{1,0:T(8,128)S(1)}) custom-call(f32[64,256]{1,0:T(8,128)S(1)} %get-tuple-element.40.x_ref, f32[32,384,256]{2,1,0:T(8,128)} %pick.1.columns_ref.w_ref), custom_call_target="tpu_custom_call" | custom-call | bytes 18000000 | tf_op jit(solution)/shard_map/slot_price/pallas_call | solution.py:249
  124.0 3.0 %slot_price.4 = f32[1536,128]{1,0:T(8,128)S(1)} custom-call(f32[64,256]{1,0:T(8,128)S(1)} %get-tuple-element.40.x_ref, f32[32,384,256]{2,1,0:T(8,128)} %pick.1.columns_ref.w_ref), custom_call_target="tpu_custom_call" | custom-call | bytes 6000000 | tf_op jit(solution)/shard_map/slot_price/pallas_call | solution.py:249
  127.0 5.8 %collective-permute-done.14 = f32[1536,128]{1,0:T(8,128)S(1)} collective-permute-done((f32[1536,128]{1,0:T(8,128)S(1)}, f32[1536,128]{1,0:T(8,128)S(1)}, u32[]{:S(2)}, u32[]{:S(2)}) %collective-permute-start.14) | collective-permute-done | bytes 786464 | tf_op jit(solution)/shard_map/ppermute | solution.py:50
  132.8 8.4 %collective-permute-done.15 = f32[1536,128]{1,0:T(8,128)S(1)} collective-permute-done((f32[1536,128]{1,0:T(8,128)S(1)}, f32[1536,128]{1,0:T(8,128)S(1)}, u32[]{:S(2)}, u32[]{:S(2)}) %collective-permute-start.15) | collective-permute-done | bytes 786464 | tf_op jit(solution)/shard_map/ppermute | solution.py:50
  143.0 4.7 %collective-permute-done.17 = f32[384,128]{1,0:T(8,128)S(1)} collective-permute-done((f32[384,128]{1,0:T(8,128)S(1)}, f32[384,128]{1,0:T(8,128)S(1)}, u32[]{:S(2)}, u32[]{:S(2)}) %collective-permute-start.17) | collective-permute-done | bytes 196640 | tf_op jit(solution)/shard_map/ppermute | solution.py:50
  150.2 5.5 %collective-permute-done.20 = f32[384,128]{1,0:T(8,128)S(1)} collective-permute-done((f32[384,128]{1,0:T(8,128)S(1)}, f32[384,128]{1,0:T(8,128)S(1)}, u32[]{:S(2)}, u32[]{:S(2)}) %collective-permute-start.20) | collective-permute-done | bytes 196640 | tf_op jit(solution)/shard_map/ppermute | solution.py:50
  158.6 5.2 %collective-permute-done.23 = f32[384,128]{1,0:T(8,128)S(1)} collective-permute-done((f32[384,128]{1,0:T(8,128)S(1)}, f32[384,128]{1,0:T(8,128)S(1)}, u32[]{:S(2)}, u32[]{:S(2)}) %collective-permute-start.23) | collective-permute-done | bytes 196640 | tf_op jit(solution)/shard_map/ppermute | solution.py:50
  164.4 2.9 %collective-permute-start.24 = (f32[1536,128]{1,0:T(8,128)S(1)}, f32[1536,128]{1,0:T(8,128)S(1)}, u32[]{:S(2)}, u32[]{:S(2)}) collective-permute-start(f32[1536,128]{1,0:T(8,128)S(1)} %pad_maximum_fusion.1.x_ref), channel_id=1, source_target_pairs={{0,12},{1,49},{2,14},{3,51},{4,0},{5,53},{6,2},{7,55},{8,4},{9,57}... | collective-permute-start | bytes 2359304 | tf_op jit(solution)/shard_map/ppermute | solution.py:50
  170.9 7.3 %collective-permute-done.24.x_ref = f32[1536,128]{1,0:T(8,128)S(1)} collective-permute-done((f32[1536,128]{1,0:T(8,128)S(1)}, f32[1536,128]{1,0:T(8,128)S(1)}, u32[]{:S(2)}, u32[]{:S(2)}) %collective-permute-start.24) | collective-permute-done | bytes 786464 | tf_op jit(solution)/shard_map/ppermute | solution.py:50
  180.5 7.6 %collective-permute-done.25.x_ref = f32[1536,128]{1,0:T(8,128)S(1)} collective-permute-done((f32[1536,128]{1,0:T(8,128)S(1)}, f32[1536,128]{1,0:T(8,128)S(1)}, u32[]{:S(2)}, u32[]{:S(2)}) %collective-permute-start.25) | collective-permute-done | bytes 786464 | tf_op jit(solution)/shard_map/ppermute | solution.py:50
  190.4 2.3 slot_flow.7
  192.7 7.5 %collective-permute-start.29 = (f32[64,256]{1,0:T(8,128)S(1)}, f32[64,256]{1,0:T(8,128)S(1)}, u32[]{:S(2)}, u32[]{:S(2)}) collective-permute-start(f32[64,256]{1,0:T(8,128)S(1)} %slot_flow.7), channel_id=1, source_target_pairs={{0,3},{1,2},{2,1},{3,0},{4,7},{5,6},{6,5},{7,4},{8,11},{9,10},{10,... | collective-permute-start | bytes 196616 | tf_op jit(solution)/shard_map/ppermute | solution.py:78
  200.7 2.4 collective-permute-done.29
  205.2 6.1 %slot_price.7 = (f32[1536,128]{1,0:T(8,128)S(1)}, f32[1536,128]{1,0:T(8,128)S(1)}, f32[1536,128]{1,0:T(8,128)S(1)}) custom-call(f32[64,256]{1,0:T(8,128)S(1)} %get-tuple-element.36.x_ref, f32[32,384,256]{2,1,0:T(8,128)} %pick.1.columns_ref.w_ref), custom_call_target="tpu_custom_call" | custom-call | bytes 18000000 | tf_op jit(solution)/shard_map/slot_price/pallas_call | solution.py:249
  214.1 3.0 %slot_price.6 = f32[1536,128]{1,0:T(8,128)S(1)} custom-call(f32[64,256]{1,0:T(8,128)S(1)} %get-tuple-element.36.x_ref, f32[32,384,256]{2,1,0:T(8,128)} %pick.1.columns_ref.w_ref), custom_call_target="tpu_custom_call" | custom-call | bytes 6000000 | tf_op jit(solution)/shard_map/slot_price/pallas_call | solution.py:249
  217.1 6.9 %collective-permute-done.30 = f32[1536,128]{1,0:T(8,128)S(1)} collective-permute-done((f32[1536,128]{1,0:T(8,128)S(1)}, f32[1536,128]{1,0:T(8,128)S(1)}, u32[]{:S(2)}, u32[]{:S(2)}) %collective-permute-start.30) | collective-permute-done | bytes 786464 | tf_op jit(solution)/shard_map/ppermute | solution.py:50
  224.0 8.2 %collective-permute-done.31 = f32[1536,128]{1,0:T(8,128)S(1)} collective-permute-done((f32[1536,128]{1,0:T(8,128)S(1)}, f32[1536,128]{1,0:T(8,128)S(1)}, u32[]{:S(2)}, u32[]{:S(2)}) %collective-permute-start.31) | collective-permute-done | bytes 786464 | tf_op jit(solution)/shard_map/ppermute | solution.py:50
  234.0 4.8 %collective-permute-done.33 = f32[384,128]{1,0:T(8,128)S(1)} collective-permute-done((f32[384,128]{1,0:T(8,128)S(1)}, f32[384,128]{1,0:T(8,128)S(1)}, u32[]{:S(2)}, u32[]{:S(2)}) %collective-permute-start.33) | collective-permute-done | bytes 196640 | tf_op jit(solution)/shard_map/ppermute | solution.py:50
  241.1 4.9 %collective-permute-done.36 = f32[192,128]{1,0:T(8,128)S(1)} collective-permute-done((f32[192,128]{1,0:T(8,128)S(1)}, f32[192,128]{1,0:T(8,128)S(1)}, u32[]{:S(2)}, u32[]{:S(2)}) %collective-permute-start.36) | collective-permute-done | bytes 98336 | tf_op jit(solution)/shard_map/ppermute | solution.py:50
  246.3 3.3 %collective-permute-start.37 = (f32[64,128]{0,1:T(8,128)S(1)}, f32[64,128]{0,1:T(8,128)S(1)}, u32[]{:S(2)}, u32[]{:S(2)}) collective-permute-start(f32[64,128]{0,1:T(8,128)S(1)} %get-tuple-element.49), channel_id=1, source_target_pairs={{0,1},{1,0},{2,3},{3,2},{4,5},{5,4},{6,7},{7,6},{8,9},{9,8},{10,11... | collective-permute-start | bytes 98312 | tf_op jit(solution)/shard_map/ppermute | solution.py:302
  (140 shorter events, 55.5 us)
Async XLA Ops:
  3.5 5.1 %collective-permute-start.2 = (f32[72,128]{1,0:T(8,128)S(1)}, f32[72,128]{1,0:T(8,128)S(1)}, u32[]{:S(2)}, u32[]{:S(2)}) collective-permute-start(f32[72,128]{1,0:T(8,128)S(1)} %get-tuple-element.55), channel_id=1, source_target_pairs={{0,3},{1,2},{2,1},{3,0},{4,7},{5,6},{6,5},{7,4},{8,11},{9,10},{10,... | collective-permute-start | bytes 110600 | tf_op jit(solution)/shard_map/ppermute | solution.py:302
  10.3 21.0 %collective-permute-start.3 = (f32[592,128]{1,0:T(8,128)S(1)}, f32[592,128]{1,0:T(8,128)S(1)}, u32[]{:S(2)}, u32[]{:S(2)}) collective-permute-start(f32[592,128]{1,0:T(8,128)S(1)} %pad_maximum_fusion.3), channel_id=1, source_target_pairs={{0,64},{1,65},{2,66},{3,67},{4,68},{5,69},{6,70},{7,71},{8,72},{9,... | collective-permute-start | bytes 909320 | tf_op jit(solution)/shard_map/ppermute | solution.py:50
  14.6 16.0 %all-to-all-start = ((f32[32,8,128]{2,1,0:T(8,128)}), f32[32,8,128]{2,1,0:T(8,128)S(1)}, u32[]{:S(2)}, u32[]{:S(2)}) async-start(f32[32,8,128]{2,1,0:T(8,128)} %broadcast_in_dim.36), calls=%async_computation | async-start | bytes 262144 | tf_op jit(solution)/shard_map/all_to_all | solution.py:367
  31.5 16.6 %collective-permute-start.6 = (f32[1152,128]{1,0:T(8,128)S(1)}, f32[1152,128]{1,0:T(8,128)S(1)}, u32[]{:S(2)}, u32[]{:S(2)}) collective-permute-start(f32[1152,128]{1,0:T(8,128)S(1)} %bitcast.78), channel_id=1, source_target_pairs={{0,16},{1,5},{2,18},{3,7},{4,20},{5,9},{6,22},{7,11},{8,24},{9,13}... | collective-permute-start | bytes 1769480 | tf_op jit(solution)/shard_map/ppermute | solution.py:50
  31.7 16.4 %collective-permute-start.5 = (f32[1152,128]{1,0:T(8,128)S(1)}, f32[1152,128]{1,0:T(8,128)S(1)}, u32[]{:S(2)}, u32[]{:S(2)}) collective-permute-start(f32[1152,128]{1,0:T(8,128)S(1)} %bitcast.79), channel_id=1, source_target_pairs={{0,32},{1,9},{2,34},{3,11},{4,36},{5,13},{6,38},{7,15},{8,40},{9,1... | collective-permute-start | bytes 1769480 | tf_op jit(solution)/shard_map/ppermute | solution.py:50
  33.8 14.9 %collective-permute-start.4 = (f32[1152,128]{1,0:T(8,128)S(1)}, f32[1152,128]{1,0:T(8,128)S(1)}, u32[]{:S(2)}, u32[]{:S(2)}) collective-permute-start(f32[1152,128]{1,0:T(8,128)S(1)} %bitcast.80), channel_id=1, source_target_pairs={{0,48},{1,13},{2,50},{3,15},{4,52},{5,1},{6,54},{7,3},{8,56},{9,5}... | collective-permute-start | bytes 1769480 | tf_op jit(solution)/shard_map/ppermute | solution.py:50
  48.9 29.3 %collective-permute-start.8 = (f32[4608,128]{1,0:T(8,128)S(1)}, f32[4608,128]{1,0:T(8,128)S(1)}, u32[]{:S(2)}, u32[]{:S(2)}) collective-permute-start(f32[4608,128]{1,0:T(8,128)S(1)} %pad_maximum_fusion.refs_4_), channel_id=1, source_target_pairs={{0,4},{1,17},{2,6},{3,19},{4,8},{5,21},{6,10},{7,23},{8,12},{9,25}... | collective-permute-start | bytes 7077896 | tf_op jit(solution)/shard_map/ppermute | solution.py:50
  49.3 28.9 %collective-permute-start.7 = (f32[4608,128]{1,0:T(8,128)S(1)}, f32[4608,128]{1,0:T(8,128)S(1)}, u32[]{:S(2)}, u32[]{:S(2)}) collective-permute-start(f32[4608,128]{1,0:T(8,128)S(1)} %pad_maximum_fusion.refs_4_), channel_id=1, source_target_pairs={{0,12},{1,49},{2,14},{3,51},{4,0},{5,53},{6,2},{7,55},{8,4},{9,57}... | collective-permute-start | bytes 7077896 | tf_op jit(solution)/shard_map/ppermute | solution.py:50
  79.6 16.0 %collective-permute-start.9 = (f32[2304,128]{1,0:T(8,128)S(1)}, f32[2304,128]{1,0:T(8,128)S(1)}, u32[]{:S(2)}, u32[]{:S(2)}) collective-permute-start(f32[2304,128]{1,0:T(8,128)S(1)} %slice.145), channel_id=1, source_target_pairs={{0,12},{1,49},{2,14},{3,51},{4,0},{5,53},{6,2},{7,55},{8,4},{9,57}... | collective-permute-start | bytes 3538952 | tf_op jit(solution)/shard_map/ppermute | solution.py:50
  81.1 16.6 %collective-permute-start.10 = (f32[2304,128]{1,0:T(8,128)S(1)}, f32[2304,128]{1,0:T(8,128)S(1)}, u32[]{:S(2)}, u32[]{:S(2)}) collective-permute-start(f32[2304,128]{1,0:T(8,128)S(1)} %slice.146), channel_id=1, source_target_pairs={{0,4},{1,17},{2,6},{3,19},{4,8},{5,21},{6,10},{7,23},{8,12},{9,25}... | collective-permute-start | bytes 3538952 | tf_op jit(solution)/shard_map/ppermute | solution.py:50
  103.4 7.9 %collective-permute-start.13 = (f32[64,256]{1,0:T(8,128)S(1)}, f32[64,256]{1,0:T(8,128)S(1)}, u32[]{:S(2)}, u32[]{:S(2)}) collective-permute-start(f32[64,256]{1,0:T(8,128)S(1)} %add.386), channel_id=1, source_target_pairs={{0,3},{1,2},{2,1},{3,0},{4,7},{5,6},{6,5},{7,4},{8,11},{9,10},{10,... | collective-permute-start | bytes 196616 | tf_op jit(solution)/shard_map/ppermute | solution.py:78
  120.0 12.8 %collective-permute-start.14 = (f32[1536,128]{1,0:T(8,128)S(1)}, f32[1536,128]{1,0:T(8,128)S(1)}, u32[]{:S(2)}, u32[]{:S(2)}) collective-permute-start(f32[1536,128]{1,0:T(8,128)S(1)} %get-tuple-element.30), channel_id=1, source_target_pairs={{0,8},{1,33},{2,10},{3,35},{4,12},{5,37},{6,14},{7,39},{8,0},{9,41... | collective-permute-start | bytes 2359304 | tf_op jit(solution)/shard_map/ppermute | solution.py:50
  121.3 19.9 %collective-permute-start.15 = (f32[1536,128]{1,0:T(8,128)S(1)}, f32[1536,128]{1,0:T(8,128)S(1)}, u32[]{:S(2)}, u32[]{:S(2)}) collective-permute-start(f32[1536,128]{1,0:T(8,128)S(1)} %get-tuple-element.31), channel_id=1, source_target_pairs={{0,4},{1,17},{2,6},{3,19},{4,8},{5,21},{6,10},{7,23},{8,12},{9,25}... | collective-permute-start | bytes 2359304 | tf_op jit(solution)/shard_map/ppermute | solution.py:50
  123.1 18.1 %collective-permute-start.16 = (f32[1536,128]{1,0:T(8,128)S(1)}, f32[1536,128]{1,0:T(8,128)S(1)}, u32[]{:S(2)}, u32[]{:S(2)}) collective-permute-start(f32[1536,128]{1,0:T(8,128)S(1)} %get-tuple-element.32), channel_id=1, source_target_pairs={{0,12},{1,49},{2,14},{3,51},{4,0},{5,53},{6,2},{7,55},{8,4},{9,57}... | collective-permute-start | bytes 2359304 | tf_op jit(solution)/shard_map/ppermute | solution.py:50
  141.4 6.4 %collective-permute-start.17 = (f32[384,128]{1,0:T(8,128)S(1)}, f32[384,128]{1,0:T(8,128)S(1)}, u32[]{:S(2)}, u32[]{:S(2)}) collective-permute-start(f32[384,128]{1,0:T(8,128)S(1)} %get-tuple-element.45), channel_id=1, source_target_pairs={{0,32},{1,9},{2,34},{3,11},{4,36},{5,13},{6,38},{7,15},{8,40},{9,1... | collective-permute-start | bytes 589832 | tf_op jit(solution)/shard_map/ppermute | solution.py:50
  141.5 6.3 %collective-permute-start.19 = (f32[384,128]{1,0:T(8,128)S(1)}, f32[384,128]{1,0:T(8,128)S(1)}, u32[]{:S(2)}, u32[]{:S(2)}) collective-permute-start(f32[384,128]{1,0:T(8,128)S(1)} %get-tuple-element.46), channel_id=1, source_target_pairs={{0,48},{1,13},{2,50},{3,15},{4,52},{5,1},{6,54},{7,3},{8,56},{9,5}... | collective-permute-start | bytes 589832 | tf_op jit(solution)/shard_map/ppermute | solution.py:50
  142.4 7.2 %collective-permute-start.18 = (f32[384,128]{1,0:T(8,128)S(1)}, f32[384,128]{1,0:T(8,128)S(1)}, u32[]{:S(2)}, u32[]{:S(2)}) collective-permute-start(f32[384,128]{1,0:T(8,128)S(1)} %get-tuple-element.47), channel_id=1, source_target_pairs={{0,16},{1,5},{2,18},{3,7},{4,20},{5,9},{6,22},{7,11},{8,24},{9,13}... | collective-permute-start | bytes 589832 | tf_op jit(solution)/shard_map/ppermute | solution.py:50
  149.6 6.1 %collective-permute-start.20 = (f32[384,128]{1,0:T(8,128)S(1)}, f32[384,128]{1,0:T(8,128)S(1)}, u32[]{:S(2)}, u32[]{:S(2)}) collective-permute-start(f32[384,128]{1,0:T(8,128)S(1)} %fusion.12), channel_id=1, source_target_pairs={{0,64},{1,65},{2,66},{3,67},{4,68},{5,69},{6,70},{7,71},{8,72},{9,... | collective-permute-start | bytes 589832 | tf_op jit(solution)/shard_map/ppermute | solution.py:50
  155.8 7.9 %collective-permute-start.23 = (f32[384,128]{1,0:T(8,128)S(1)}, f32[384,128]{1,0:T(8,128)S(1)}, u32[]{:S(2)}, u32[]{:S(2)}) collective-permute-start(f32[384,128]{1,0:T(8,128)S(1)} %get-tuple-element.38), channel_id=1, source_target_pairs={{0,16},{1,5},{2,18},{3,7},{4,20},{5,9},{6,22},{7,11},{8,24},{9,13}... | collective-permute-start | bytes 589832 | tf_op jit(solution)/shard_map/ppermute | solution.py:50
  155.9 7.8 %collective-permute-start.22 = (f32[384,128]{1,0:T(8,128)S(1)}, f32[384,128]{1,0:T(8,128)S(1)}, u32[]{:S(2)}, u32[]{:S(2)}) collective-permute-start(f32[384,128]{1,0:T(8,128)S(1)} %get-tuple-element.38), channel_id=1, source_target_pairs={{0,32},{1,9},{2,34},{3,11},{4,36},{5,13},{6,38},{7,15},{8,40},{9,1... | collective-permute-start | bytes 589832 | tf_op jit(solution)/shard_map/ppermute | solution.py:50
  157.7 6.7 %collective-permute-start.21 = (f32[384,128]{1,0:T(8,128)S(1)}, f32[384,128]{1,0:T(8,128)S(1)}, u32[]{:S(2)}, u32[]{:S(2)}) collective-permute-start(f32[384,128]{1,0:T(8,128)S(1)} %get-tuple-element.38), channel_id=1, source_target_pairs={{0,48},{1,13},{2,50},{3,15},{4,52},{5,1},{6,54},{7,3},{8,56},{9,5}... | collective-permute-start | bytes 589832 | tf_op jit(solution)/shard_map/ppermute | solution.py:50
  164.4 13.8 %collective-permute-start.24 = (f32[1536,128]{1,0:T(8,128)S(1)}, f32[1536,128]{1,0:T(8,128)S(1)}, u32[]{:S(2)}, u32[]{:S(2)}) collective-permute-start(f32[1536,128]{1,0:T(8,128)S(1)} %pad_maximum_fusion.1.x_ref), channel_id=1, source_target_pairs={{0,12},{1,49},{2,14},{3,51},{4,0},{5,53},{6,2},{7,55},{8,4},{9,57}... | collective-permute-start | bytes 2359304 | tf_op jit(solution)/shard_map/ppermute | solution.py:50
  167.3 20.8 %collective-permute-start.25 = (f32[1536,128]{1,0:T(8,128)S(1)}, f32[1536,128]{1,0:T(8,128)S(1)}, u32[]{:S(2)}, u32[]{:S(2)}) collective-permute-start(f32[1536,128]{1,0:T(8,128)S(1)} %pad_maximum_fusion.1.x_ref), channel_id=1, source_target_pairs={{0,4},{1,17},{2,6},{3,19},{4,8},{5,21},{6,10},{7,23},{8,12},{9,25}... | collective-permute-start | bytes 2359304 | tf_op jit(solution)/shard_map/ppermute | solution.py:50
  167.3 23.1 %collective-permute-start.26 = (f32[1536,128]{1,0:T(8,128)S(1)}, f32[1536,128]{1,0:T(8,128)S(1)}, u32[]{:S(2)}, u32[]{:S(2)}) collective-permute-start(f32[1536,128]{1,0:T(8,128)S(1)} %pad_maximum_fusion.1.x_ref), channel_id=1, source_target_pairs={{0,8},{1,33},{2,10},{3,35},{4,12},{5,37},{6,14},{7,39},{8,0},{9,41... | collective-permute-start | bytes 2359304 | tf_op jit(solution)/shard_map/ppermute | solution.py:50
  192.7 10.4 %collective-permute-start.29 = (f32[64,256]{1,0:T(8,128)S(1)}, f32[64,256]{1,0:T(8,128)S(1)}, u32[]{:S(2)}, u32[]{:S(2)}) collective-permute-start(f32[64,256]{1,0:T(8,128)S(1)} %slot_flow.7), channel_id=1, source_target_pairs={{0,3},{1,2},{2,1},{3,0},{4,7},{5,6},{6,5},{7,4},{8,11},{9,10},{10,... | collective-permute-start | bytes 196616 | tf_op jit(solution)/shard_map/ppermute | solution.py:78
  211.3 12.8 %collective-permute-start.30 = (f32[1536,128]{1,0:T(8,128)S(1)}, f32[1536,128]{1,0:T(8,128)S(1)}, u32[]{:S(2)}, u32[]{:S(2)}) collective-permute-start(f32[1536,128]{1,0:T(8,128)S(1)} %get-tuple-element.33), channel_id=1, source_target_pairs={{0,8},{1,33},{2,10},{3,35},{4,12},{5,37},{6,14},{7,39},{8,0},{9,41... | collective-permute-start | bytes 2359304 | tf_op jit(solution)/shard_map/ppermute | solution.py:50
  211.4 20.8 %collective-permute-start.31 = (f32[1536,128]{1,0:T(8,128)S(1)}, f32[1536,128]{1,0:T(8,128)S(1)}, u32[]{:S(2)}, u32[]{:S(2)}) collective-permute-start(f32[1536,128]{1,0:T(8,128)S(1)} %get-tuple-element.34), channel_id=1, source_target_pairs={{0,4},{1,17},{2,6},{3,19},{4,8},{5,21},{6,10},{7,23},{8,12},{9,25}... | collective-permute-start | bytes 2359304 | tf_op jit(solution)/shard_map/ppermute | solution.py:50
  212.6 19.6 %collective-permute-start.32 = (f32[1536,128]{1,0:T(8,128)S(1)}, f32[1536,128]{1,0:T(8,128)S(1)}, u32[]{:S(2)}, u32[]{:S(2)}) collective-permute-start(f32[1536,128]{1,0:T(8,128)S(1)} %get-tuple-element.35), channel_id=1, source_target_pairs={{0,12},{1,49},{2,14},{3,51},{4,0},{5,53},{6,2},{7,55},{8,4},{9,57}... | collective-permute-start | bytes 2359304 | tf_op jit(solution)/shard_map/ppermute | solution.py:50
  232.4 6.4 %collective-permute-start.33 = (f32[384,128]{1,0:T(8,128)S(1)}, f32[384,128]{1,0:T(8,128)S(1)}, u32[]{:S(2)}, u32[]{:S(2)}) collective-permute-start(f32[384,128]{1,0:T(8,128)S(1)} %get-tuple-element.42), channel_id=1, source_target_pairs={{0,32},{1,9},{2,34},{3,11},{4,36},{5,13},{6,38},{7,15},{8,40},{9,1... | collective-permute-start | bytes 589832 | tf_op jit(solution)/shard_map/ppermute | solution.py:50
  232.5 6.3 %collective-permute-start.35 = (f32[384,128]{1,0:T(8,128)S(1)}, f32[384,128]{1,0:T(8,128)S(1)}, u32[]{:S(2)}, u32[]{:S(2)}) collective-permute-start(f32[384,128]{1,0:T(8,128)S(1)} %get-tuple-element.43), channel_id=1, source_target_pairs={{0,48},{1,13},{2,50},{3,15},{4,52},{5,1},{6,54},{7,3},{8,56},{9,5}... | collective-permute-start | bytes 589832 | tf_op jit(solution)/shard_map/ppermute | solution.py:50
  232.6 8.3 %collective-permute-start.34 = (f32[384,128]{1,0:T(8,128)S(1)}, f32[384,128]{1,0:T(8,128)S(1)}, u32[]{:S(2)}, u32[]{:S(2)}) collective-permute-start(f32[384,128]{1,0:T(8,128)S(1)} %get-tuple-element.44), channel_id=1, source_target_pairs={{0,16},{1,5},{2,18},{3,7},{4,20},{5,9},{6,22},{7,11},{8,24},{9,13}... | collective-permute-start | bytes 589832 | tf_op jit(solution)/shard_map/ppermute | solution.py:50
  246.3 5.1 %collective-permute-start.37 = (f32[64,128]{0,1:T(8,128)S(1)}, f32[64,128]{0,1:T(8,128)S(1)}, u32[]{:S(2)}, u32[]{:S(2)}) collective-permute-start(f32[64,128]{0,1:T(8,128)S(1)} %get-tuple-element.49), channel_id=1, source_target_pairs={{0,1},{1,0},{2,3},{3,2},{4,5},{5,4},{6,7},{7,6},{8,9},{9,8},{10,11... | collective-permute-start | bytes 98312 | tf_op jit(solution)/shard_map/ppermute | solution.py:302
  (14 other events, 88.4 us)

commit v6 on v5

--- a/solution.py
+++ b/solution.py
@@ -373,15 +373,19 @@
     params = both[:, BLOCK_ROWS : BLOCK_ROWS + 3 * CAP].reshape(2, 3, CAP, 1, 128)
     lin, quad, top = (params[:, k] for k in range(3))
     now = both[:, LOAD_ROWS:BLOCK_ROWS].reshape(2, CAP, S, 128)
-    eight = gather_first(both[:, :BLOCK_ROWS].reshape(2 * BLOCK_ROWS, 128))
-    eight, codes = lax.optimization_barrier((eight, codes))
+    parts = ring_first(both[:, :BLOCK_ROWS].reshape(2 * BLOCK_ROWS, 128))
+    low, high = (jnp.concatenate(parts[k : k + 2], axis=0) for k in (0, 2))
+    low, high, codes = lax.optimization_barrier((low, high, codes))
     columns = pick(codes, ptdf)
-    one, three = moved(eight, "second", -1), moved(eight, "second", -3)
-    one, three, columns = lax.optimization_barrier((one, three, columns))
-    n = eight.shape[0] // 2
-    two_near, two_far = moved(one[:n], "second", -1), moved(three[n:], "second", -3)
+    one_low, three_high = moved(low, "second", -1), moved(high, "second", -3)
+    one_high, three_low = moved(high, "second", -1), moved(low, "second", -3)
+    one_low, three_high, columns = lax.optimization_barrier((one_low, three_high, columns))
+    two_low, two_high = moved(one_low, "second", -1), moved(three_high, "second", -3)
     load_part = slot_part = jnp.zeros((S, LINES_DEV), jnp.float32)
-    for xs, starts in (((eight, one, three), (0, 8, 24)), ((two_near, two_far), (16, 20))):
+    for xs, starts in (
+        ((low, high, one_low, three_high, one_high, three_low), (0, 4, 8, 28, 12, 24)),
+        ((two_low, two_high), (16, 20)),
+    ):
         load_part, slot_part = first_flow(
             load_part, slot_part, xs, columns, ptdf, block_of, starts
         )

time: 256 us -> 253 us (0.988)
    ppermute x28 -> x30, waiting for transfers between devices: 92.7 us -> 90 us  [moved(): return lax.ppermute(a, ('band', 'bus'), pairs)]
    ppermute x28 -> x30, starting transfers between devices: 28.4 us -> 27.6 us  [moved(): return lax.ppermute(a, ('band', 'bus'), pairs)]
  transfers between devices with their start and end apart: 41 -> 43, of which waited for: 26 -> 28; matrix products, arithmetic and copies ran while one was open for 1% -> 1% of each run, Pallas kernels for 20% -> 20%
where the time goes in v6:
time: 253 us
  waiting for transfers between devices  111 us (44%)
  Pallas kernels  70.8 us (28%)
  starting transfers between devices  59.7 us (24%)
  local copies, waits for them, and re-layouts  5.3 us (2%)
  other arithmetic  3.93 us (2%)
    ppermute x30, waiting for transfers between devices, moved(): return lax.ppermute(a, ('band', 'bus'), pairs)  90 us
    ppermute x30, starting transfers between devices, moved(): return lax.ppermute(a, ('band', 'bus'), pairs)  27.6 us
    pallas_call x1, Pallas kernels, pick(): pl.pallas_call(pick_kernel, grid=(N_BAND // PICK_STEP,), in_specs=[pl.Blo...  23.9 us
    pallas_call x2, Pallas kernels, first_flow(): pl.pallas_call(functools.partial(first_flow_kernel, steps), grid_spec=plt...  19.5 us
    pallas_call x4, Pallas kernels, slot_price(): pl.pallas_call(slot_price_kernel, grid=(n,), in_specs=[pl.BlockSpec((S, L...  18.2 us
    ppermute x6, starting transfers between devices, sum_bus(): lax.ppermute(a, 'bus', [(j, j ^ k) for j in range(N_BUS)])  14.7 us
    ppermute x6, starting transfers between devices, exchange_bus(): lax.ppermute(parts[k], 'bus', [(j, j ^ k) for j in range(N_BUS)])  10.2 us
    pallas_call x4, Pallas kernels, slot_flow(): pl.pallas_call(slot_flow_kernel, grid=(SLOT_STEPS,), in_specs=[pl.BlockSp...  9.17 us
  transfers between devices with their start and end apart: 43, of which 28 were waited for; matrix products, arithmetic and copies ran while one was open for 1% of the time, Pallas kernels for 20%

profile of v6, /device:TPU:1, one launch (start us, length us, event | category | flops | bytes accessed | tf_op | source)
XLA Modules:
  0.0 252.7 jit_solution(15317794671024425001)
XLA Ops:
  3.5 3.1 %collective-permute-start.2 = (f32[72,128]{1,0:T(8,128)S(1)}, f32[72,128]{1,0:T(8,128)S(1)}, u32[]{:S(2)}, u32[]{:S(2)}) collective-permute-start(f32[72,128]{1,0:T(8,128)S(1)} %get-tuple-element.57), channel_id=1, source_target_pairs={{0,3},{1,2},{2,1},{3,0},{4,7},{5,6},{6,5},{7,4},{8,11},{9,10},{10,... | collective-permute-start | bytes 110600 | tf_op jit(solution)/shard_map/ppermute | solution.py:302
  10.3 3.4 %collective-permute-start.3 = (f32[592,128]{1,0:T(8,128)S(1)}, f32[592,128]{1,0:T(8,128)S(1)}, u32[]{:S(2)}, u32[]{:S(2)}) collective-permute-start(f32[592,128]{1,0:T(8,128)S(1)} %pad_maximum_fusion.4), channel_id=1, source_target_pairs={{0,64},{1,65},{2,66},{3,67},{4,68},{5,69},{6,70},{7,71},{8,72},{9,... | collective-permute-start | bytes 909320 | tf_op jit(solution)/shard_map/ppermute | solution.py:50
  14.6 7.0 %all-to-all-start = ((f32[32,8,128]{2,1,0:T(8,128)}), f32[32,8,128]{2,1,0:T(8,128)S(1)}, u32[]{:S(2)}, u32[]{:S(2)}) async-start(f32[32,8,128]{2,1,0:T(8,128)} %broadcast_in_dim.36), calls=%async_computation | async-start | bytes 262144 | tf_op jit(solution)/shard_map/all_to_all | solution.py:367
  21.7 8.9 %all-to-all-done = f32[32,8,128]{2,1,0:T(8,128)S(1)} async-done(((f32[32,8,128]{2,1,0:T(8,128)}), f32[32,8,128]{2,1,0:T(8,128)S(1)}, u32[]{:S(2)}, u32[]{:S(2)}) %all-to-all-start) | async-done | bytes 131104 | tf_op jit(solution)/shard_map/all_to_all | solution.py:367
  34.0 6.6 %collective-permute-done.4 = f32[1152,128]{1,0:T(8,128)S(1)} collective-permute-done((f32[1152,128]{1,0:T(8,128)S(1)}, f32[1152,128]{1,0:T(8,128)S(1)}, u32[]{:S(2)}, u32[]{:S(2)}) %collective-permute-start.4) | collective-permute-done | bytes 589856 | tf_op jit(solution)/shard_map/ppermute | solution.py:50
  40.7 8.5 %collective-permute-done.6 = f32[1152,128]{1,0:T(8,128)S(1)} collective-permute-done((f32[1152,128]{1,0:T(8,128)S(1)}, f32[1152,128]{1,0:T(8,128)S(1)}, u32[]{:S(2)}, u32[]{:S(2)}) %collective-permute-start.6) | collective-permute-done | bytes 589856 | tf_op jit(solution)/shard_map/ppermute | solution.py:50
  51.0 2.5 collective-permute-start.9
  53.5 23.9 %pick.1.columns_ref.w_ref = f32[32,384,256]{2,1,0:T(8,128)} custom-call(f32[384,32]{1,0:T(8,128)S(1)} %reshape.356.code_ref, f32[256,24576]{1,0:T(8,128)} %refs_3_.3), custom_call_target="tpu_custom_call" | custom-call | bytes 90000000 | tf_op jit(solution)/shard_map/pick/pallas_call | solution.py:285
  80.6 13.8 %first_flow.2 = (f32[64,256]{1,0:T(8,128)S(1)}, f32[64,256]{1,0:T(8,128)S(1)}) custom-call(s32[24]{0:T(128)S(1)} %pad_add_fusion.idx_ref, s32[6]{0:T(128)S(1)} %copy-done.1, f32[64,256]{1,0:T(8,128)S(1)} %broadcast_in_dim.37.load_acc_ref.slot_acc_ref, f32[64,256]{1,0:T(8,128)S(1)} %broadcast_in_dim.37.load_acc_ref.slot_acc_ref, ...), custom_call_target="tpu_custom_call" | custom-call | bytes 54000000 | tf_op jit(solution)/shard_map/first_flow/pallas_call | solution.py:174
  95.0 5.7 %first_flow.3 = (f32[64,256]{1,0:T(8,128)S(1)}, f32[64,256]{1,0:T(8,128)S(1)}) custom-call(s32[8]{0:T(128)S(1)} %concatenate.34.idx_ref, s32[2]{0:T(128)S(1)} %copy-done, f32[64,256]{1,0:T(8,128)S(1)} %get-tuple-element.28.load_acc_ref, f32[64,256]{1,0:T(8,128)S(1)} %get-tuple-element.29.slot_acc_ref, f32[32,384,256]{2,1,0:T(8,128)} %pick.1.columns_ref.w_ref, ...), custom_call_target="tpu_custom_call" | custom-call | bytes 18000000 | tf_op jit(solution)/shard_map/first_flow/pallas_call | solution.py:174
  100.8 5.9 %collective-permute-start.15 = (f32[64,256]{1,0:T(8,128)S(1)}, f32[64,256]{1,0:T(8,128)S(1)}, u32[]{:S(2)}, u32[]{:S(2)}) collective-permute-start(f32[64,256]{1,0:T(8,128)S(1)} %add.386), channel_id=1, source_target_pairs={{0,3},{1,2},{2,1},{3,0},{4,7},{5,6},{6,5},{7,4},{8,11},{9,10},{10,... | collective-permute-start | bytes 196616 | tf_op jit(solution)/shard_map/ppermute | solution.py:78
  108.7 2.6 %collective-permute-done.14 = f32[64,256]{1,0:T(8,128)S(1)} collective-permute-done((f32[64,256]{1,0:T(8,128)S(1)}, f32[64,256]{1,0:T(8,128)S(1)}, u32[]{:S(2)}, u32[]{:S(2)}) %collective-permute-start.14) | collective-permute-done | bytes 65568 | tf_op jit(solution)/shard_map/ppermute | solution.py:78
  111.3 6.1 %slot_price.5 = (f32[1536,128]{1,0:T(8,128)S(1)}, f32[1536,128]{1,0:T(8,128)S(1)}, f32[1536,128]{1,0:T(8,128)S(1)}) custom-call(f32[64,256]{1,0:T(8,128)S(1)} %get-tuple-element.42.x_ref, f32[32,384,256]{2,1,0:T(8,128)} %pick.1.columns_ref.w_ref), custom_call_target="tpu_custom_call" | custom-call | bytes 18000000 | tf_op jit(solution)/shard_map/slot_price/pallas_call | solution.py:249
  118.2 2.7 %collective-permute-start.18 = (f32[1536,128]{1,0:T(8,128)S(1)}, f32[1536,128]{1,0:T(8,128)S(1)}, u32[]{:S(2)}, u32[]{:S(2)}) collective-permute-start(f32[1536,128]{1,0:T(8,128)S(1)} %get-tuple-element.34), channel_id=1, source_target_pairs={{0,12},{1,49},{2,14},{3,51},{4,0},{5,53},{6,2},{7,55},{8,4},{9,57}... | collective-permute-start | bytes 2359304 | tf_op jit(solution)/shard_map/ppermute | solution.py:50
  120.8 3.0 %slot_price.4 = f32[1536,128]{1,0:T(8,128)S(1)} custom-call(f32[64,256]{1,0:T(8,128)S(1)} %get-tuple-element.42.x_ref, f32[32,384,256]{2,1,0:T(8,128)} %pick.1.columns_ref.w_ref), custom_call_target="tpu_custom_call" | custom-call | bytes 6000000 | tf_op jit(solution)/shard_map/slot_price/pallas_call | solution.py:249
  123.8 6.3 %collective-permute-done.16 = f32[1536,128]{1,0:T(8,128)S(1)} collective-permute-done((f32[1536,128]{1,0:T(8,128)S(1)}, f32[1536,128]{1,0:T(8,128)S(1)}, u32[]{:S(2)}, u32[]{:S(2)}) %collective-permute-start.16) | collective-permute-done | bytes 786464 | tf_op jit(solution)/shard_map/ppermute | solution.py:50
  130.2 8.4 %collective-permute-done.17 = f32[1536,128]{1,0:T(8,128)S(1)} collective-permute-done((f32[1536,128]{1,0:T(8,128)S(1)}, f32[1536,128]{1,0:T(8,128)S(1)}, u32[]{:S(2)}, u32[]{:S(2)}) %collective-permute-start.17) | collective-permute-done | bytes 786464 | tf_op jit(solution)/shard_map/ppermute | solution.py:50
  140.4 4.7 %collective-permute-done.19 = f32[384,128]{1,0:T(8,128)S(1)} collective-permute-done((f32[384,128]{1,0:T(8,128)S(1)}, f32[384,128]{1,0:T(8,128)S(1)}, u32[]{:S(2)}, u32[]{:S(2)}) %collective-permute-start.19) | collective-permute-done | bytes 196640 | tf_op jit(solution)/shard_map/ppermute | solution.py:50
  147.8 5.6 %collective-permute-done.22 = f32[384,128]{1,0:T(8,128)S(1)} collective-permute-done((f32[384,128]{1,0:T(8,128)S(1)}, f32[384,128]{1,0:T(8,128)S(1)}, u32[]{:S(2)}, u32[]{:S(2)}) %collective-permute-start.22) | collective-permute-done | bytes 196640 | tf_op jit(solution)/shard_map/ppermute | solution.py:50
  156.2 5.5 %collective-permute-done.25 = f32[384,128]{1,0:T(8,128)S(1)} collective-permute-done((f32[384,128]{1,0:T(8,128)S(1)}, f32[384,128]{1,0:T(8,128)S(1)}, u32[]{:S(2)}, u32[]{:S(2)}) %collective-permute-start.25) | collective-permute-done | bytes 196640 | tf_op jit(solution)/shard_map/ppermute | solution.py:50
  166.4 8.1 %collective-permute-done.26.x_ref = f32[1536,128]{1,0:T(8,128)S(1)} collective-permute-done((f32[1536,128]{1,0:T(8,128)S(1)}, f32[1536,128]{1,0:T(8,128)S(1)}, u32[]{:S(2)}, u32[]{:S(2)}) %collective-permute-start.26) | collective-permute-done | bytes 786464 | tf_op jit(solution)/shard_map/ppermute | solution.py:50
  176.8 6.5 %collective-permute-done.27.x_ref = f32[1536,128]{1,0:T(8,128)S(1)} collective-permute-done((f32[1536,128]{1,0:T(8,128)S(1)}, f32[1536,128]{1,0:T(8,128)S(1)}, u32[]{:S(2)}, u32[]{:S(2)}) %collective-permute-start.27) | collective-permute-done | bytes 786464 | tf_op jit(solution)/shard_map/ppermute | solution.py:50
  185.6 2.3 slot_flow.7
  187.9 7.1 %collective-permute-start.31 = (f32[64,256]{1,0:T(8,128)S(1)}, f32[64,256]{1,0:T(8,128)S(1)}, u32[]{:S(2)}, u32[]{:S(2)}) collective-permute-start(f32[64,256]{1,0:T(8,128)S(1)} %slot_flow.7), channel_id=1, source_target_pairs={{0,3},{1,2},{2,1},{3,0},{4,7},{5,6},{6,5},{7,4},{8,11},{9,10},{10,... | collective-permute-start | bytes 196616 | tf_op jit(solution)/shard_map/ppermute | solution.py:78
  199.8 6.1 %slot_price.7 = (f32[1536,128]{1,0:T(8,128)S(1)}, f32[1536,128]{1,0:T(8,128)S(1)}, f32[1536,128]{1,0:T(8,128)S(1)}) custom-call(f32[64,256]{1,0:T(8,128)S(1)} %get-tuple-element.38.x_ref, f32[32,384,256]{2,1,0:T(8,128)} %pick.1.columns_ref.w_ref), custom_call_target="tpu_custom_call" | custom-call | bytes 18000000 | tf_op jit(solution)/shard_map/slot_price/pallas_call | solution.py:249
  207.1 2.7 %collective-permute-start.33 = (f32[1536,128]{1,0:T(8,128)S(1)}, f32[1536,128]{1,0:T(8,128)S(1)}, u32[]{:S(2)}, u32[]{:S(2)}) collective-permute-start(f32[1536,128]{1,0:T(8,128)S(1)} %get-tuple-element.36), channel_id=1, source_target_pairs={{0,4},{1,17},{2,6},{3,19},{4,8},{5,21},{6,10},{7,23},{8,12},{9,25}... | collective-permute-start | bytes 2359304 | tf_op jit(solution)/shard_map/ppermute | solution.py:50
  210.0 3.0 %slot_price.6 = f32[1536,128]{1,0:T(8,128)S(1)} custom-call(f32[64,256]{1,0:T(8,128)S(1)} %get-tuple-element.38.x_ref, f32[32,384,256]{2,1,0:T(8,128)} %pick.1.columns_ref.w_ref), custom_call_target="tpu_custom_call" | custom-call | bytes 6000000 | tf_op jit(solution)/shard_map/slot_price/pallas_call | solution.py:249
  213.0 5.7 %collective-permute-done.32 = f32[1536,128]{1,0:T(8,128)S(1)} collective-permute-done((f32[1536,128]{1,0:T(8,128)S(1)}, f32[1536,128]{1,0:T(8,128)S(1)}, u32[]{:S(2)}, u32[]{:S(2)}) %collective-permute-start.32) | collective-permute-done | bytes 786464 | tf_op jit(solution)/shard_map/ppermute | solution.py:50
  218.7 8.4 %collective-permute-done.33 = f32[1536,128]{1,0:T(8,128)S(1)} collective-permute-done((f32[1536,128]{1,0:T(8,128)S(1)}, f32[1536,128]{1,0:T(8,128)S(1)}, u32[]{:S(2)}, u32[]{:S(2)}) %collective-permute-start.33) | collective-permute-done | bytes 786464 | tf_op jit(solution)/shard_map/ppermute | solution.py:50
  229.5 4.8 %collective-permute-done.35 = f32[384,128]{1,0:T(8,128)S(1)} collective-permute-done((f32[384,128]{1,0:T(8,128)S(1)}, f32[384,128]{1,0:T(8,128)S(1)}, u32[]{:S(2)}, u32[]{:S(2)}) %collective-permute-start.35) | collective-permute-done | bytes 196640 | tf_op jit(solution)/shard_map/ppermute | solution.py:50
  236.5 4.7 %collective-permute-done.38 = f32[192,128]{1,0:T(8,128)S(1)} collective-permute-done((f32[192,128]{1,0:T(8,128)S(1)}, f32[192,128]{1,0:T(8,128)S(1)}, u32[]{:S(2)}, u32[]{:S(2)}) %collective-permute-start.38) | collective-permute-done | bytes 98336 | tf_op jit(solution)/shard_map/ppermute | solution.py:50
  241.5 4.9 %collective-permute-start.39 = (f32[64,128]{0,1:T(8,128)S(1)}, f32[64,128]{0,1:T(8,128)S(1)}, u32[]{:S(2)}, u32[]{:S(2)}) collective-permute-start(f32[64,128]{0,1:T(8,128)S(1)} %get-tuple-element.51), channel_id=1, source_target_pairs={{0,1},{1,0},{2,3},{3,2},{4,5},{5,4},{6,7},{7,6},{8,9},{9,8},{10,11... | collective-permute-start | bytes 98312 | tf_op jit(solution)/shard_map/ppermute | solution.py:302
  (144 shorter events, 53.2 us)
Async XLA Ops:
  10.3 21.0 %collective-permute-start.3 = (f32[592,128]{1,0:T(8,128)S(1)}, f32[592,128]{1,0:T(8,128)S(1)}, u32[]{:S(2)}, u32[]{:S(2)}) collective-permute-start(f32[592,128]{1,0:T(8,128)S(1)} %pad_maximum_fusion.4), channel_id=1, source_target_pairs={{0,64},{1,65},{2,66},{3,67},{4,68},{5,69},{6,70},{7,71},{8,72},{9,... | collective-permute-start | bytes 909320 | tf_op jit(solution)/shard_map/ppermute | solution.py:50
  14.6 16.0 %all-to-all-start = ((f32[32,8,128]{2,1,0:T(8,128)}), f32[32,8,128]{2,1,0:T(8,128)S(1)}, u32[]{:S(2)}, u32[]{:S(2)}) async-start(f32[32,8,128]{2,1,0:T(8,128)} %broadcast_in_dim.36), calls=%async_computation | async-start | bytes 262144 | tf_op jit(solution)/shard_map/all_to_all | solution.py:367
  31.5 9.1 %collective-permute-start.4 = (f32[1152,128]{1,0:T(8,128)S(1)}, f32[1152,128]{1,0:T(8,128)S(1)}, u32[]{:S(2)}, u32[]{:S(2)}) collective-permute-start(f32[1152,128]{1,0:T(8,128)S(1)} %bitcast.78), channel_id=1, source_target_pairs={{0,48},{1,13},{2,50},{3,15},{4,52},{5,1},{6,54},{7,3},{8,56},{9,5}... | collective-permute-start | bytes 1769480 | tf_op jit(solution)/shard_map/ppermute | solution.py:50
  32.6 16.6 %collective-permute-start.6 = (f32[1152,128]{1,0:T(8,128)S(1)}, f32[1152,128]{1,0:T(8,128)S(1)}, u32[]{:S(2)}, u32[]{:S(2)}) collective-permute-start(f32[1152,128]{1,0:T(8,128)S(1)} %bitcast.79), channel_id=1, source_target_pairs={{0,16},{1,5},{2,18},{3,7},{4,20},{5,9},{6,22},{7,11},{8,24},{9,13}... | collective-permute-start | bytes 1769480 | tf_op jit(solution)/shard_map/ppermute | solution.py:50
  33.0 16.2 %collective-permute-start.5 = (f32[1152,128]{1,0:T(8,128)S(1)}, f32[1152,128]{1,0:T(8,128)S(1)}, u32[]{:S(2)}, u32[]{:S(2)}) collective-permute-start(f32[1152,128]{1,0:T(8,128)S(1)} %bitcast.80), channel_id=1, source_target_pairs={{0,32},{1,9},{2,34},{3,11},{4,36},{5,13},{6,38},{7,15},{8,40},{9,1... | collective-permute-start | bytes 1769480 | tf_op jit(solution)/shard_map/ppermute | solution.py:50
  49.3 28.1 %collective-permute-start.7 = (f32[2304,128]{1,0:T(8,128)S(1)}, f32[2304,128]{1,0:T(8,128)S(1)}, u32[]{:S(2)}, u32[]{:S(2)}) collective-permute-start(f32[2304,128]{1,0:T(8,128)S(1)} %pad_maximum_fusion.refs_4_), channel_id=1, source_target_pairs={{0,12},{1,49},{2,14},{3,51},{4,0},{5,53},{6,2},{7,55},{8,4},{9,57}... | collective-permute-start | bytes 3538952 | tf_op jit(solution)/shard_map/ppermute | solution.py:50
  50.4 27.0 %collective-permute-start.8 = (f32[2304,128]{1,0:T(8,128)S(1)}, f32[2304,128]{1,0:T(8,128)S(1)}, u32[]{:S(2)}, u32[]{:S(2)}) collective-permute-start(f32[2304,128]{1,0:T(8,128)S(1)} %pad_maximum_fusion.1.refs_5_), channel_id=1, source_target_pairs={{0,4},{1,17},{2,6},{3,19},{4,8},{5,21},{6,10},{7,23},{8,12},{9,25}... | collective-permute-start | bytes 3538952 | tf_op jit(solution)/shard_map/ppermute | solution.py:50
  50.8 28.8 %collective-permute-start.10 = (f32[2304,128]{1,0:T(8,128)S(1)}, f32[2304,128]{1,0:T(8,128)S(1)}, u32[]{:S(2)}, u32[]{:S(2)}) collective-permute-start(f32[2304,128]{1,0:T(8,128)S(1)} %pad_maximum_fusion.refs_4_), channel_id=1, source_target_pairs={{0,4},{1,17},{2,6},{3,19},{4,8},{5,21},{6,10},{7,23},{8,12},{9,25}... | collective-permute-start | bytes 3538952 | tf_op jit(solution)/shard_map/ppermute | solution.py:50
  51.0 28.6 %collective-permute-start.9 = (f32[2304,128]{1,0:T(8,128)S(1)}, f32[2304,128]{1,0:T(8,128)S(1)}, u32[]{:S(2)}, u32[]{:S(2)}) collective-permute-start(f32[2304,128]{1,0:T(8,128)S(1)} %pad_maximum_fusion.1.refs_5_), channel_id=1, source_target_pairs={{0,12},{1,49},{2,14},{3,51},{4,0},{5,53},{6,2},{7,55},{8,4},{9,57}... | collective-permute-start | bytes 3538952 | tf_op jit(solution)/shard_map/ppermute | solution.py:50
  77.4 17.0 %collective-permute-start.11 = (f32[2304,128]{1,0:T(8,128)S(1)}, f32[2304,128]{1,0:T(8,128)S(1)}, u32[]{:S(2)}, u32[]{:S(2)}) collective-permute-start(f32[2304,128]{1,0:T(8,128)S(1)} %collective-permute-done.7.refs_6_), channel_id=1, source_target_pairs={{0,12},{1,49},{2,14},{3,51},{4,0},{5,53},{6,2},{7,55},{8,4},{9,57}... | collective-permute-start | bytes 3538952 | tf_op jit(solution)/shard_map/ppermute | solution.py:50
  78.5 16.6 %collective-permute-start.12 = (f32[2304,128]{1,0:T(8,128)S(1)}, f32[2304,128]{1,0:T(8,128)S(1)}, u32[]{:S(2)}, u32[]{:S(2)}) collective-permute-start(f32[2304,128]{1,0:T(8,128)S(1)} %collective-permute-done.8.refs_7_), channel_id=1, source_target_pairs={{0,4},{1,17},{2,6},{3,19},{4,8},{5,21},{6,10},{7,23},{8,12},{9,25}... | collective-permute-start | bytes 3538952 | tf_op jit(solution)/shard_map/ppermute | solution.py:50
  100.8 7.9 %collective-permute-start.15 = (f32[64,256]{1,0:T(8,128)S(1)}, f32[64,256]{1,0:T(8,128)S(1)}, u32[]{:S(2)}, u32[]{:S(2)}) collective-permute-start(f32[64,256]{1,0:T(8,128)S(1)} %add.386), channel_id=1, source_target_pairs={{0,3},{1,2},{2,1},{3,0},{4,7},{5,6},{6,5},{7,4},{8,11},{9,10},{10,... | collective-permute-start | bytes 196616 | tf_op jit(solution)/shard_map/ppermute | solution.py:78
  117.4 12.8 %collective-permute-start.16 = (f32[1536,128]{1,0:T(8,128)S(1)}, f32[1536,128]{1,0:T(8,128)S(1)}, u32[]{:S(2)}, u32[]{:S(2)}) collective-permute-start(f32[1536,128]{1,0:T(8,128)S(1)} %get-tuple-element.32), channel_id=1, source_target_pairs={{0,8},{1,33},{2,10},{3,35},{4,12},{5,37},{6,14},{7,39},{8,0},{9,41... | collective-permute-start | bytes 2359304 | tf_op jit(solution)/shard_map/ppermute | solution.py:50
  118.2 20.4 %collective-permute-start.17 = (f32[1536,128]{1,0:T(8,128)S(1)}, f32[1536,128]{1,0:T(8,128)S(1)}, u32[]{:S(2)}, u32[]{:S(2)}) collective-permute-start(f32[1536,128]{1,0:T(8,128)S(1)} %get-tuple-element.33), channel_id=1, source_target_pairs={{0,4},{1,17},{2,6},{3,19},{4,8},{5,21},{6,10},{7,23},{8,12},{9,25}... | collective-permute-start | bytes 2359304 | tf_op jit(solution)/shard_map/ppermute | solution.py:50
  118.2 20.4 %collective-permute-start.18 = (f32[1536,128]{1,0:T(8,128)S(1)}, f32[1536,128]{1,0:T(8,128)S(1)}, u32[]{:S(2)}, u32[]{:S(2)}) collective-permute-start(f32[1536,128]{1,0:T(8,128)S(1)} %get-tuple-element.34), channel_id=1, source_target_pairs={{0,12},{1,49},{2,14},{3,51},{4,0},{5,53},{6,2},{7,55},{8,4},{9,57}... | collective-permute-start | bytes 2359304 | tf_op jit(solution)/shard_map/ppermute | solution.py:50
  138.7 6.4 %collective-permute-start.19 = (f32[384,128]{1,0:T(8,128)S(1)}, f32[384,128]{1,0:T(8,128)S(1)}, u32[]{:S(2)}, u32[]{:S(2)}) collective-permute-start(f32[384,128]{1,0:T(8,128)S(1)} %get-tuple-element.47), channel_id=1, source_target_pairs={{0,32},{1,9},{2,34},{3,11},{4,36},{5,13},{6,38},{7,15},{8,40},{9,1... | collective-permute-start | bytes 589832 | tf_op jit(solution)/shard_map/ppermute | solution.py:50
  138.8 6.7 %collective-permute-start.21 = (f32[384,128]{1,0:T(8,128)S(1)}, f32[384,128]{1,0:T(8,128)S(1)}, u32[]{:S(2)}, u32[]{:S(2)}) collective-permute-start(f32[384,128]{1,0:T(8,128)S(1)} %get-tuple-element.48), channel_id=1, source_target_pairs={{0,48},{1,13},{2,50},{3,15},{4,52},{5,1},{6,54},{7,3},{8,56},{9,5}... | collective-permute-start | bytes 589832 | tf_op jit(solution)/shard_map/ppermute | solution.py:50
  140.1 7.2 %collective-permute-start.20 = (f32[384,128]{1,0:T(8,128)S(1)}, f32[384,128]{1,0:T(8,128)S(1)}, u32[]{:S(2)}, u32[]{:S(2)}) collective-permute-start(f32[384,128]{1,0:T(8,128)S(1)} %get-tuple-element.49), channel_id=1, source_target_pairs={{0,16},{1,5},{2,18},{3,7},{4,20},{5,9},{6,22},{7,11},{8,24},{9,13}... | collective-permute-start | bytes 589832 | tf_op jit(solution)/shard_map/ppermute | solution.py:50
  153.5 8.2 %collective-permute-start.25 = (f32[384,128]{1,0:T(8,128)S(1)}, f32[384,128]{1,0:T(8,128)S(1)}, u32[]{:S(2)}, u32[]{:S(2)}) collective-permute-start(f32[384,128]{1,0:T(8,128)S(1)} %get-tuple-element.40), channel_id=1, source_target_pairs={{0,16},{1,5},{2,18},{3,7},{4,20},{5,9},{6,22},{7,11},{8,24},{9,13}... | collective-permute-start | bytes 589832 | tf_op jit(solution)/shard_map/ppermute | solution.py:50
  153.6 8.1 %collective-permute-start.24 = (f32[384,128]{1,0:T(8,128)S(1)}, f32[384,128]{1,0:T(8,128)S(1)}, u32[]{:S(2)}, u32[]{:S(2)}) collective-permute-start(f32[384,128]{1,0:T(8,128)S(1)} %get-tuple-element.40), channel_id=1, source_target_pairs={{0,32},{1,9},{2,34},{3,11},{4,36},{5,13},{6,38},{7,15},{8,40},{9,1... | collective-permute-start | bytes 589832 | tf_op jit(solution)/shard_map/ppermute | solution.py:50
  155.4 6.9 %collective-permute-start.23 = (f32[384,128]{1,0:T(8,128)S(1)}, f32[384,128]{1,0:T(8,128)S(1)}, u32[]{:S(2)}, u32[]{:S(2)}) collective-permute-start(f32[384,128]{1,0:T(8,128)S(1)} %get-tuple-element.40), channel_id=1, source_target_pairs={{0,48},{1,13},{2,50},{3,15},{4,52},{5,1},{6,54},{7,3},{8,56},{9,5}... | collective-permute-start | bytes 589832 | tf_op jit(solution)/shard_map/ppermute | solution.py:50
  162.4 12.2 %collective-permute-start.26 = (f32[1536,128]{1,0:T(8,128)S(1)}, f32[1536,128]{1,0:T(8,128)S(1)}, u32[]{:S(2)}, u32[]{:S(2)}) collective-permute-start(f32[1536,128]{1,0:T(8,128)S(1)} %pad_maximum_fusion.2.x_ref), channel_id=1, source_target_pairs={{0,12},{1,49},{2,14},{3,51},{4,0},{5,53},{6,2},{7,55},{8,4},{9,57}... | collective-permute-start | bytes 2359304 | tf_op jit(solution)/shard_map/ppermute | solution.py:50
  162.5 20.8 %collective-permute-start.27 = (f32[1536,128]{1,0:T(8,128)S(1)}, f32[1536,128]{1,0:T(8,128)S(1)}, u32[]{:S(2)}, u32[]{:S(2)}) collective-permute-start(f32[1536,128]{1,0:T(8,128)S(1)} %pad_maximum_fusion.2.x_ref), channel_id=1, source_target_pairs={{0,4},{1,17},{2,6},{3,19},{4,8},{5,21},{6,10},{7,23},{8,12},{9,25}... | collective-permute-start | bytes 2359304 | tf_op jit(solution)/shard_map/ppermute | solution.py:50
  163.9 21.7 %collective-permute-start.28 = (f32[1536,128]{1,0:T(8,128)S(1)}, f32[1536,128]{1,0:T(8,128)S(1)}, u32[]{:S(2)}, u32[]{:S(2)}) collective-permute-start(f32[1536,128]{1,0:T(8,128)S(1)} %pad_maximum_fusion.2.x_ref), channel_id=1, source_target_pairs={{0,8},{1,33},{2,10},{3,35},{4,12},{5,37},{6,14},{7,39},{8,0},{9,41... | collective-permute-start | bytes 2359304 | tf_op jit(solution)/shard_map/ppermute | solution.py:50
  187.9 9.8 %collective-permute-start.31 = (f32[64,256]{1,0:T(8,128)S(1)}, f32[64,256]{1,0:T(8,128)S(1)}, u32[]{:S(2)}, u32[]{:S(2)}) collective-permute-start(f32[64,256]{1,0:T(8,128)S(1)} %slot_flow.7), channel_id=1, source_target_pairs={{0,3},{1,2},{2,1},{3,0},{4,7},{5,6},{6,5},{7,4},{8,11},{9,10},{10,... | collective-permute-start | bytes 196616 | tf_op jit(solution)/shard_map/ppermute | solution.py:78
  205.9 12.8 %collective-permute-start.32 = (f32[1536,128]{1,0:T(8,128)S(1)}, f32[1536,128]{1,0:T(8,128)S(1)}, u32[]{:S(2)}, u32[]{:S(2)}) collective-permute-start(f32[1536,128]{1,0:T(8,128)S(1)} %get-tuple-element.35), channel_id=1, source_target_pairs={{0,8},{1,33},{2,10},{3,35},{4,12},{5,37},{6,14},{7,39},{8,0},{9,41... | collective-permute-start | bytes 2359304 | tf_op jit(solution)/shard_map/ppermute | solution.py:50
  207.1 19.9 %collective-permute-start.33 = (f32[1536,128]{1,0:T(8,128)S(1)}, f32[1536,128]{1,0:T(8,128)S(1)}, u32[]{:S(2)}, u32[]{:S(2)}) collective-permute-start(f32[1536,128]{1,0:T(8,128)S(1)} %get-tuple-element.36), channel_id=1, source_target_pairs={{0,4},{1,17},{2,6},{3,19},{4,8},{5,21},{6,10},{7,23},{8,12},{9,25}... | collective-permute-start | bytes 2359304 | tf_op jit(solution)/shard_map/ppermute | solution.py:50
  209.8 17.8 %collective-permute-start.34 = (f32[1536,128]{1,0:T(8,128)S(1)}, f32[1536,128]{1,0:T(8,128)S(1)}, u32[]{:S(2)}, u32[]{:S(2)}) collective-permute-start(f32[1536,128]{1,0:T(8,128)S(1)} %get-tuple-element.37), channel_id=1, source_target_pairs={{0,12},{1,49},{2,14},{3,51},{4,0},{5,53},{6,2},{7,55},{8,4},{9,57}... | collective-permute-start | bytes 2359304 | tf_op jit(solution)/shard_map/ppermute | solution.py:50
  227.9 6.4 %collective-permute-start.35 = (f32[384,128]{1,0:T(8,128)S(1)}, f32[384,128]{1,0:T(8,128)S(1)}, u32[]{:S(2)}, u32[]{:S(2)}) collective-permute-start(f32[384,128]{1,0:T(8,128)S(1)} %get-tuple-element.44), channel_id=1, source_target_pairs={{0,32},{1,9},{2,34},{3,11},{4,36},{5,13},{6,38},{7,15},{8,40},{9,1... | collective-permute-start | bytes 589832 | tf_op jit(solution)/shard_map/ppermute | solution.py:50
  228.0 6.3 %collective-permute-start.37 = (f32[384,128]{1,0:T(8,128)S(1)}, f32[384,128]{1,0:T(8,128)S(1)}, u32[]{:S(2)}, u32[]{:S(2)}) collective-permute-start(f32[384,128]{1,0:T(8,128)S(1)} %get-tuple-element.45), channel_id=1, source_target_pairs={{0,48},{1,13},{2,50},{3,15},{4,52},{5,1},{6,54},{7,3},{8,56},{9,5}... | collective-permute-start | bytes 589832 | tf_op jit(solution)/shard_map/ppermute | solution.py:50
  228.1 8.0 %collective-permute-start.36 = (f32[384,128]{1,0:T(8,128)S(1)}, f32[384,128]{1,0:T(8,128)S(1)}, u32[]{:S(2)}, u32[]{:S(2)}) collective-permute-start(f32[384,128]{1,0:T(8,128)S(1)} %get-tuple-element.46), channel_id=1, source_target_pairs={{0,16},{1,5},{2,18},{3,7},{4,20},{5,9},{6,22},{7,11},{8,24},{9,13}... | collective-permute-start | bytes 589832 | tf_op jit(solution)/shard_map/ppermute | solution.py:50
  241.5 6.6 %collective-permute-start.39 = (f32[64,128]{0,1:T(8,128)S(1)}, f32[64,128]{0,1:T(8,128)S(1)}, u32[]{:S(2)}, u32[]{:S(2)}) collective-permute-start(f32[64,128]{0,1:T(8,128)S(1)} %get-tuple-element.51), channel_id=1, source_target_pairs={{0,1},{1,0},{2,3},{3,2},{4,5},{5,4},{6,7},{7,6},{8,9},{9,8},{10,11... | collective-permute-start | bytes 98312 | tf_op jit(solution)/shard_map/ppermute | solution.py:302
  (16 other events, 122.7 us)
